TPU v7x, 256 devices: a whole 4x4x8 slice. The times are simulated.
256 devices in a mesh: band: 8 (over y, core), space: 32 (over x, z).
Axes of the slice: x: 4, y: 4, z: 8, core: 2. Of those that a mesh axis runs over, the one named last changes fastest.
Arguments:
- left_factor: bfloat16 [8, 32768, 2048], P('band', 'space'), may hold values from -0.1875 to 0.1875
- right_factor: bfloat16 [8, 2048, 32768], P('band', None, 'space'), may hold values from -0.125 to 0.125
- data: bfloat16 [8, 256, 32768], P('band', None, 'space'), may hold values from -6 to 6
Outputs:
- solution: float32 [256, 32768], P('band', 'space')
- residual: float32 [256, 32768], P('band', 'space')
All inputs are finite; a program needn't handle non-finite values.
Results may differ from a plain program's by a relative error of at most 0.03.
Values may be sent and summed in bfloat16 or wider, within the bound.
No kernel may reach another device: no remote copies, remote signals or barrier semaphores. Data moves between devices by JAX's collectives and lax.ppermute only.
A program may use at most 64 MiB of HBM per device.

v0:
```python
import jax
import jax.numpy as jnp
from jax import lax
from jax.sharding import PartitionSpec as P

ITERS = 2


damping = 1.0


def squares(vector):
    return lax.psum(jnp.sum(vector * vector, axis=1), "space")


def per_device(left_factor, right_factor, data):
    left = left_factor[0]
    right = right_factor[0]
    images = data.shape[1]
    bands = lax.axis_size("band")
    share = images // bands
    offset = lax.axis_index("band") * share
    contract = (((1,), (1,)), ((), ()))

    def adjoint(seen):
        back = lax.dot_general(seen, right, contract, preferred_element_type=jnp.float32).astype(
            jnp.bfloat16
        )
        return lax.dot_general(
            lax.all_to_all(back, "space", split_axis=1, concat_axis=1, tiled=True),
            left,
            contract,
            preferred_element_type=jnp.float32,
        )

    def combine(partial_value):
        return lax.psum(partial_value, "band")

    residual = combine(adjoint(data[0]))
    solution = jnp.zeros_like(residual)
    direction = residual
    norm_now = squares(residual)
    for step in range(ITERS):
        rounded = direction.astype(jnp.bfloat16)
        coeff = jnp.dot(rounded, left, preferred_element_type=jnp.float32).astype(jnp.bfloat16)
        seen = jnp.dot(
            lax.all_to_all(coeff, "space", split_axis=1, concat_axis=1, tiled=True),
            right,
            preferred_element_type=jnp.float32,
        )
        image = combine(adjoint(seen.astype(jnp.bfloat16))) + damping * direction
        curv = lax.psum(jnp.sum(direction * image, axis=1), "space")
        alpha = norm_now / curv
        solution = solution + alpha[:, None] * direction
        residual = residual - alpha[:, None] * image
        norm_next = squares(residual)
        direction = residual + (norm_next / norm_now)[:, None] * direction
        norm_now = norm_next
    return (
        lax.dynamic_slice_in_dim(solution, offset, share, 0),
        lax.dynamic_slice_in_dim(residual, offset, share, 0),
    )


def solution(mesh):
    return jax.shard_map(
        per_device,
        mesh=mesh,
        in_specs=(P("band", "space", None), P("band", None, "space"), P("band", None, "space")),
        out_specs=(P("band", "space"), P("band", "space")),
        check_vma=False,
    )
```

profile of v0, /device:TPU:32, one launch (start us, length us, event | category | flops | bytes accessed | tf_op | source)
XLA Modules:
  0.0 645.7 jit_solution(18139205870715117056)
XLA Ops:
  8.2 3.5 fusion.20
  12.2 39.5 %all_to_all.60 = bf16[256,32,64]{0,2,1:T(8,128)(2,1)S(1)} all-to-all(bf16[256,32,64]{0,2,1:T(8,128)(2,1)S(1)} %bitcast.58), channel_id=1, replica_groups=mesh['band'=8,'space'=32] {'space'}, dimensions={1} | all-to-all | bytes 2097152 | tf_op jit(solution)/shard_map/all_to_all | solution.py:30
  51.7 4.6 fusion.8
  56.4 64.3 %all-reduce.5.cloned.1.call-done = f32[256,1024]{1,0:T(8,128)} async-done(((f32[256,1024]{1,0:T(8,128)}), f32[256,1024]{1,0:T(8,128)}) %all-reduce.5.cloned.1.call-update) | async-done | bytes 1048592 | tf_op jit(solution)/shard_map/psum | solution.py:37
  120.7 3.8 fusion.29
  125.0 36.5 %all_to_all.61 = bf16[256,32,64]{0,2,1:T(8,128)(2,1)S(1)} all-to-all(bf16[256,32,64]{0,2,1:T(8,128)(2,1)S(1)} %bitcast.59), channel_id=1, replica_groups=mesh['band'=8,'space'=32] {'space'}, dimensions={1} | all-to-all | bytes 2097152 | tf_op jit(solution)/shard_map/all_to_all | solution.py:47
  161.5 6.9 %fusion.23 = bf16[256,2048]{1,0:T(8,128)(2,1)} fusion(bf16[1,2048,1024]{2,1,0:T(8,128)(2,1)} %param.4, bf16[256,2048]{0,1:T(8,128)(2,1)S(1)} %bitcast.64), kind=kOutput, calls=%fused_computation.21 | convolution fusion | flops 2148270080 | bytes 6291456 | tf_op jit(solution)/shard_map/dot_general | solution.py:26
  169.9 30.6 %all_to_all.62 = bf16[256,32,64]{0,2,1:T(8,128)(2,1)S(1)} all-to-all(bf16[256,32,64]{0,2,1:T(8,128)(2,1)S(1)} %bitcast.60), channel_id=1, replica_groups=mesh['band'=8,'space'=32] {'space'}, dimensions={1} | all-to-all | bytes 2097152 | tf_op jit(solution)/shard_map/all_to_all | solution.py:30
  200.5 4.6 fusion.4
  205.1 67.7 %all-reduce.7.cloned.1.call-done = f32[256,1024]{1,0:T(8,128)} async-done(((f32[256,1024]{1,0:T(8,128)}), f32[256,1024]{1,0:T(8,128)}) %all-reduce.7.cloned.1.call-update) | async-done | bytes 1048592 | tf_op jit(solution)/shard_map/psum | solution.py:37
  272.8 1.5 multiply_reduce_fusion.2
  274.3 71.6 %all-reduce = (f32[256]{0:T(256)S(1)}, f32[256]{0:T(256)S(1)}) all-reduce(f32[256]{0:T(256)S(1)} %get-tuple-element.3, f32[256]{0:T(256)S(1)} %get-tuple-element.2), channel_id=1, replica_groups=mesh['band'=8,'space'=32] {'space'}, use_global_device_ids=true, to_apply=%region_2.0 | all-reduce | flops 512 | bytes 4096 | tf_op jit(solution)/shard_map/psum | solution.py:13
  347.1 74.5 %psum.53 = f32[256]{0:T(256)S(1)} all-reduce(f32[256]{0:T(256)S(1)} %get-tuple-element.8), channel_id=1, replica_groups=mesh['band'=8,'space'=32] {'space'}, use_global_device_ids=true, to_apply=%region_7.0 | all-reduce | flops 256 | bytes 2048 | tf_op jit(solution)/shard_map/psum | solution.py:13
  423.0 4.4 fusion.32
  427.4 2.3 copy.8
  429.7 33.6 %all_to_all.63 = bf16[256,32,64]{0,2,1:T(8,128)(2,1)} all-to-all(bf16[256,32,64]{0,2,1:T(8,128)(2,1)} %bitcast.61), channel_id=1, replica_groups=mesh['band'=8,'space'=32] {'space'}, dimensions={1} | all-to-all | bytes 2097152 | tf_op jit(solution)/shard_map/all_to_all | solution.py:47
  463.4 7.2 %fusion.26 = bf16[256,2048]{1,0:T(8,128)(2,1)} fusion(bf16[1,2048,1024]{2,1,0:T(8,128)(2,1)} %param.4, bf16[256,2048]{0,1:T(8,128)(2,1)} %bitcast.66), kind=kOutput, calls=%fused_computation.22 | convolution fusion | flops 2148270080 | bytes 6291456 | tf_op jit(solution)/shard_map/dot_general | solution.py:26
  470.5 2.3 copy.9
  472.8 24.4 %all_to_all.64 = bf16[256,32,64]{0,2,1:T(8,128)(2,1)S(1)} all-to-all(bf16[256,32,64]{0,2,1:T(8,128)(2,1)} %bitcast.62), channel_id=1, replica_groups=mesh['band'=8,'space'=32] {'space'}, dimensions={1} | all-to-all | bytes 2097152 | tf_op jit(solution)/shard_map/all_to_all | solution.py:30
  497.2 4.5 fusion
  501.8 61.7 %all-reduce.9.cloned.1.call-done = f32[256,1024]{1,0:T(8,128)} async-done(((f32[256,1024]{1,0:T(8,128)}), f32[256,1024]{1,0:T(8,128)}) %all-reduce.9.cloned.1.call-update) | async-done | bytes 1048592 | tf_op jit(solution)/shard_map/psum | solution.py:37
  563.5 2.3 multiply_reduce_fusion
  565.8 71.5 %psum.55 = f32[256]{0:T(256)S(1)} all-reduce(f32[256]{0:T(256)S(1)} %get-tuple-element.6), channel_id=1, replica_groups=mesh['band'=8,'space'=32] {'space'}, use_global_device_ids=true, to_apply=%region_10.0 | all-reduce | flops 256 | bytes 2048 | tf_op jit(solution)/shard_map/psum | solution.py:52
  637.4 1.8 dynamic-slice_subtract_fusion
  (20 shorter events, 6.5 us)
Async XLA Ops:
  7.2 1.0 copy-start
  7.2 113.5 %all-reduce.5.cloned.1.call-start = ((), (), s32[]{:S(2)}) async-start(), calls=%async_computation.5 | async-start | bytes 2097152 | tf_op jit(solution)/shard_map/psum | solution.py:37
  56.3 216.5 %all-reduce.7.cloned.1.call-start = ((), (), s32[]{:S(2)}) async-start(), calls=%async_computation.6 | async-start | bytes 2097152 | tf_op jit(solution)/shard_map/psum | solution.py:37
  200.5 72.4 %copy-start.1 = (f32[256,1024]{1,0:T(8,128)S(1)}, f32[256,1024]{1,0:T(8,128)}, u32[]{:S(2)}) copy-start(f32[256,1024]{1,0:T(8,128)} %all-reduce.5.cloned.1.call-done) | copy-start | bytes 3145732
  205.1 358.4 %all-reduce.9.cloned.1.call-start = ((), (), s32[]{:S(2)}) async-start(), calls=%async_computation.7 | async-start | bytes 2097152 | tf_op jit(solution)/shard_map/psum | solution.py:37
Sparse Core Ops, SparseCore 0:
  56.4 64.2 all-reduce.4
  205.2 67.5 all-reduce.6
  501.9 61.5 all-reduce.8
where the time goes:
time: 649 us; the launch traced here: 646 us
  blocking collectives  382 us (59%)
  waiting for transfers between devices  194 us (30%)
  matrix products  39.3 us (6%)
  between operations  13.8 us (2%)
  local copies, waits for them, and re-layouts  8.23 us (1%)
  other arithmetic  8.19 us (1%)
    psum x3, waiting for transfers between devices, combine(): return lax.psum(partial_value, 'band')  194 us
    psum x2, blocking collectives, squares(): return lax.psum(jnp.sum(vector * vector, axis=1), 'space')  146 us
    all_to_all x3, blocking collectives, adjoint(): lax.all_to_all(back, 'space', split_axis=1, concat_axis=1, tiled=True)  94.5 us
    psum x1, blocking collectives, per_device(): curv = lax.psum(jnp.sum(direction * image, axis=1), 'space')  71.5 us
    all_to_all x2, blocking collectives, per_device(): lax.all_to_all(coeff, 'space', split_axis=1, concat_axis=1, tiled=True)  70.2 us
    dot_general x3, matrix products, adjoint(): lax.dot_general(seen, right, contract, preferred_element_type=jnp.float32)  17.5 us
    dot_general x3, matrix products, adjoint(): lax.dot_general(lax.all_to_all(back, 'space', split_axis=1, concat_axis=1...  13.7 us
  transfers between devices with their start and end apart: 3, of which 3 were waited for; matrix products, arithmetic and copies ran while one was open for 0% of the time, Pallas kernels for 0%

commit v1 on v0

v1 whole, which is shorter than its diff:
```python
import jax
import jax.numpy as jnp
from jax import lax
from jax.sharding import Mesh, PartitionSpec as P

NCH = 1
damping = 1.0
BAND = "band"
SPACE = "space"
f32, bf16 = jnp.float32, jnp.bfloat16


def split(value):
    high = value.astype(bf16)
    return high, (value - high.astype(f32)).astype(bf16)


def per_device(left_factor, right_factor, data):
    left, right = left_factor[0], right_factor[0]
    images = data.shape[1]
    cells, width = left.shape
    bands, blocks = lax.axis_size(BAND), lax.axis_size(SPACE)
    rank = width // blocks
    extra = 8
    m = images // NCH
    share = m // bands
    leftT, rightT = left.T, right.T
    leftT, rightT = lax.optimization_barrier((leftT, rightT))

    def exchange(v):
        return lax.all_to_all(v, SPACE, 0, 0, tiled=True)

    def send(back, scalars=None):
        back = back.reshape(blocks, rank, m)
        if scalars is None:
            return exchange(back), None
        rows = []
        for s in scalars:
            rows += list(split(s))
        rows = jnp.stack(rows + [jnp.zeros_like(rows[0])] * (extra - len(rows)))
        got = exchange(jnp.concatenate([back, jnp.broadcast_to(rows[None], (blocks, extra, m))], axis=1))
        sums = got[:, rank:, :].astype(f32).sum(0)
        return got[:, :rank, :], [sums[2 * i] + sums[2 * i + 1] for i in range(len(scalars))]

    def reduce_band(recv, scalars=None):
        part = lax.dot_general(left, recv.reshape(width, m), (((1,), (0,)), ((), ())), preferred_element_type=f32)
        part = part.T.astype(bf16)
        if scalars is not None:
            cols = []
            for s in scalars:
                cols += list(split(s))
            cols = jnp.stack(cols, axis=1)
            cols = jnp.pad(cols, ((0, 0), (0, 128 - cols.shape[1])))
            part = jnp.concatenate([part, cols], axis=1)
        got = lax.all_to_all(part.reshape(bands, share, part.shape[1]), BAND, 0, 0, tiled=True)
        got = got.astype(f32).sum(0)
        if scalars is None:
            return got, None
        tail = got[:, cells:]
        return got[:, :cells], [(tail[:, 2 * i] + tail[:, 2 * i + 1])[:, None] for i in range(len(scalars))]

    def gather(v):
        v = jnp.broadcast_to(v.astype(bf16)[None], (bands,) + v.shape)
        return lax.all_to_all(v, BAND, 0, 0, tiled=True).reshape(m, cells)

    def back_of(w, dims):
        return lax.dot_general(right, w, (((1,), (dims,)), ((), ())), preferred_element_type=f32).astype(bf16)

    def forward(p):
        coeff = lax.dot_general(leftT, p, (((1,), (1,)), ((), ())), preferred_element_type=f32).astype(bf16)
        recv = exchange(coeff.reshape(blocks, rank, m)).reshape(width, m)
        return lax.dot_general(rightT, recv, (((1,), (0,)), ((), ())), preferred_element_type=f32)

    def sumsq(a, b, axis):
        return jnp.sum(a.astype(f32) * b.astype(f32), axis=axis)

    sols, ress = [], []
    st = [dict() for _ in range(NCH)]
    for c in range(NCH):
        d = data[0, c * m:(c + 1) * m]
        recv, _ = send(back_of(d, 1))
        r0, _ = reduce_band(recv)
        p0 = gather(r0)
        s0 = forward(p0)
        pp = sumsq(p0, p0, 1) / bands
        cc = sumsq(s0, s0, 0) + damping * pp
        recv, sc = send(back_of(s0.astype(bf16), 0), [pp, cc])
        q0, (rr0, c0) = reduce_band(recv, sc)
        q0 = q0 + damping * r0
        a0 = rr0 / c0
        r1 = r0 - a0 * q0
        p1 = gather(r1)
        s1 = forward(p1)
        rp = sumsq(p1, p1, 1) / bands
        rx = sumsq(p1, p0, 1) / bands
        ss = sumsq(s1, s1, 0) + damping * rp
        sx = sumsq(s1, s0, 0) + damping * rx
        recv, sc = send(back_of(s1.astype(bf16), 0), [rp, ss, sx])
        q1, (rr1, n11, n01) = reduce_band(recv, sc)
        q1 = q1 + damping * r1
        b0 = rr1 / rr0
        c1 = n11 + 2 * b0 * n01 + b0 * b0 * c0
        a1 = rr1 / c1
        sols.append(a0 * r0 + a1 * (r1 + b0 * r0))
        ress.append(r1 - a1 * (q1 + b0 * q0))
    if NCH == 1:
        return sols[0], ress[0]
    return jnp.concatenate(sols), jnp.concatenate(ress)


def solution(mesh):
    return jax.shard_map(
        per_device,
        mesh=mesh,
        in_specs=(P("band", "space", None), P("band", None, "space"), P("band", None, "space")),
        out_specs=(P("band", "space"), P("band", "space")),
        check_vma=False,
    )
```

time: 649 us -> 283 us (0.44)
  blocking collectives: 382 us -> 168 us
  waiting for transfers between devices: 194 us -> 66.4 us
  matrix products: 39.3 us -> 24.8 us
  starting transfers between devices: 0.12 us -> 13.2 us
  between operations: 13.8 us -> 0.99 us
    psum x3 -> x0, blocking collectives: 218 us -> none  [the longest x2 146 us: squares(): return lax.psum(jnp.sum(vector * vector, axis=1), 'space')]
    psum x3 -> x0, waiting for transfers between devices: 194 us -> none  [combine(): return lax.psum(partial_value, 'band')]
    all_to_all x0 -> x3, waiting for transfers between devices: none -> 66.4 us  [the longest x2 56.2 us: exchange(): return lax.all_to_all(v, SPACE, 0, 0, tiled=True)]
    dot_general x8 -> x10, matrix products: 39.3 us -> 24.8 us  [the longest x2 7.63 us: forward(): lax.dot_general(rightT, recv, (((1,), (0,)), ((), ())), preferred_element...]
    all_to_all x0 -> x3, starting transfers between devices: none -> 13.2 us  [the longest x2 9.73 us: exchange(): return lax.all_to_all(v, SPACE, 0, 0, tiled=True)]
    all_to_all x5 -> x7, blocking collectives: 165 us -> 168 us  [the longest x3 113 us: exchange(): return lax.all_to_all(v, SPACE, 0, 0, tiled=True)]
where the time goes in v1:
time: 283 us; the launch traced here: 281 us
  blocking collectives  168 us (59%)
  waiting for transfers between devices  66.4 us (23%)
  matrix products  24.8 us (9%)
  starting transfers between devices  13.2 us (5%)
  local copies, waits for them, and re-layouts  4.88 us (2%)
    all_to_all x3, blocking collectives, exchange(): return lax.all_to_all(v, SPACE, 0, 0, tiled=True)  113 us
    all_to_all x2, waiting for transfers between devices, exchange(): return lax.all_to_all(v, SPACE, 0, 0, tiled=True)  56.2 us
    all_to_all x3, blocking collectives, reduce_band(): lax.all_to_all(part.reshape(bands, share, part.shape[1]), BAND, 0, 0, til...  41.9 us
    all_to_all x1, blocking collectives, gather(): return lax.all_to_all(v, BAND, 0, 0, tiled=True).reshape(m, cells)  12.8 us
    all_to_all x1, waiting for transfers between devices, gather(): return lax.all_to_all(v, BAND, 0, 0, tiled=True).reshape(m, cells)  10.3 us
    all_to_all x2, starting transfers between devices, exchange(): return lax.all_to_all(v, SPACE, 0, 0, tiled=True)  9.73 us
    dot_general x2, matrix products, forward(): lax.dot_general(rightT, recv, (((1,), (0,)), ((), ())), preferred_element...  7.63 us
    dot_general x2, matrix products, forward(): lax.dot_general(leftT, p, (((1,), (1,)), ((), ())), preferred_element_typ...  6.97 us
  transfers between devices with their start and end apart: 3, of which 3 were waited for; matrix products, arithmetic and copies ran while one was open for 0% of the time, Pallas kernels for 0%

profile of v1, /device:TPU:32, one launch (start us, length us, event | category | flops | bytes accessed | tf_op | source)
XLA Modules:
  0.0 280.6 jit_solution(15877260193665194760)
XLA Ops:
  0.6 1.0 copy-done
  1.7 3.6 %fusion.15 = bf16[2048,256]{1,0:T(8,128)(2,1)S(1)} fusion(bf16[1,2048,1024]{2,1,0:T(8,128)(2,1)} %param.4, bf16[1,256,1024]{2,1,0:T(8,128)(2,1)S(1)} %copy-done), kind=kOutput, calls=%fused_computation.13 | convolution fusion | flops 1074266112 | bytes 5767168 | tf_op jit(solution)/shard_map/dot_general | solution.py:67
  5.3 39.5 %all_to_all.50 = bf16[32,64,256]{2,1,0:T(8,128)(2,1)S(1)} all-to-all(bf16[32,64,256]{2,1,0:T(8,128)(2,1)S(1)} %bitcast.113), channel_id=1, replica_groups=mesh['band'=8,'space'=32] {'space'}, dimensions={0} | all-to-all | bytes 2097152 | tf_op jit(solution)/shard_map/all_to_all | solution.py:31
  44.8 1.3 fusion.30
  46.1 14.7 %all_to_all.51 = bf16[8,32,1024]{2,1,0:T(8,128)(2,1)S(1)} all-to-all(bf16[8,32,1024]{2,1,0:T(8,128)(2,1)S(1)} %bitcast.114), channel_id=1, replica_groups=mesh['band'=8,'space'=32] {'band'}, dimensions={0} | all-to-all | bytes 1048576 | tf_op jit(solution)/shard_map/all_to_all | solution.py:55
  61.8 3.5 %all-to-all-start.2 = ((bf16[8,32,1024]{2,1,0:T(8,128)(2,1)}), bf16[8,32,1024]{2,1,0:T(8,128)(2,1)S(1)}, u32[]{:S(2)}, u32[]{:S(2)}) async-start(bf16[8,32,1024]{2,1,0:T(8,128)(2,1)} %broadcast_in_dim.8), calls=%async_computation.2 | async-start | bytes 1048576 | tf_op jit(solution)/shard_map/all_to_all | solution.py:64
  65.3 10.3 %all-to-all-done.2 = bf16[8,32,1024]{2,1,0:T(8,128)(2,1)S(1)} async-done(((bf16[8,32,1024]{2,1,0:T(8,128)(2,1)}), bf16[8,32,1024]{2,1,0:T(8,128)(2,1)S(1)}, u32[]{:S(2)}, u32[]{:S(2)}) %all-to-all-start.2) | async-done | bytes 524320 | tf_op jit(solution)/shard_map/all_to_all | solution.py:64
  75.5 4.5 %convolution_convert_fusion.1 = bf16[2048,256]{1,0:T(8,128)(2,1)} fusion(bf16[2048,1024]{0,1:T(8,128)(2,1)} %bitcast.120, bf16[256,1024]{1,0:T(8,128)(2,1)S(1)} %bitcast.101), kind=kOutput, calls=%fused_computation.16 | convolution fusion | flops 1074266112 | bytes 5767168 | tf_op jit(solution)/shard_map/dot_general | solution.py:70
  80.0 5.2 %all-to-all-start.3 = ((bf16[32,64,256]{2,1,0:T(8,128)(2,1)}), bf16[32,64,256]{2,1,0:T(8,128)(2,1)S(1)}, u32[]{:S(2)}, u32[]{:S(2)}) async-start(bf16[32,64,256]{2,1,0:T(8,128)(2,1)} %bitcast.9), calls=%async_computation.3 | async-start | bytes 2097152 | tf_op jit(solution)/shard_map/all_to_all | solution.py:31
  85.5 28.1 %all-to-all-done.3 = bf16[32,64,256]{2,1,0:T(8,128)(2,1)S(1)} async-done(((bf16[32,64,256]{2,1,0:T(8,128)(2,1)}), bf16[32,64,256]{2,1,0:T(8,128)(2,1)S(1)}, u32[]{:S(2)}, u32[]{:S(2)}) %all-to-all-start.3) | async-done | bytes 1048608 | tf_op jit(solution)/shard_map/all_to_all | solution.py:31
  113.6 3.6 %multiply_reduce_fusion.2 = (f32[256]{0:T(256)S(1)}, f32[1024,256]{1,0:T(8,128)S(1)}) fusion(bf16[1024,2048]{0,1:T(8,128)(2,1)} %bitcast.118, bf16[2048,256]{1,0:T(8,128)(2,1)S(1)} %bitcast.109), kind=kOutput, calls=%fused_computation.37 | convolution fusion | flops 1074265856 | bytes 6292480 | tf_op jit(solution)/shard_map/dot_general | solution.py:72
  118.2 1.3 fusion.21
  120.3 36.9 %all_to_all.52 = bf16[32,72,256]{2,1,0:T(8,128)(2,1)S(1)} all-to-all(bf16[32,72,256]{2,1,0:T(8,128)(2,1)S(1)} %pad_maximum_fusion), channel_id=1, replica_groups=mesh['band'=8,'space'=32] {'space'}, dimensions={0} | all-to-all | bytes 2359296 | tf_op jit(solution)/shard_map/all_to_all | solution.py:31
  157.3 1.3 fusion.33
  158.9 13.7 %all_to_all.53 = bf16[8,32,1152]{2,1,0:T(8,128)(2,1)S(1)} all-to-all(bf16[8,32,1152]{2,1,0:T(8,128)(2,1)S(1)} %bitcast.104), channel_id=1, replica_groups=mesh['band'=8,'space'=32] {'band'}, dimensions={0} | all-to-all | bytes 1179648 | tf_op jit(solution)/shard_map/all_to_all | solution.py:55
  173.0 12.8 %all_to_all.54 = bf16[8,32,1024]{2,1,0:T(8,128)(2,1)S(1)} all-to-all(bf16[8,32,1024]{2,1,0:T(8,128)(2,1)S(1)} %broadcast_in_dim.10), channel_id=1, replica_groups=mesh['band'=8,'space'=32] {'band'}, dimensions={0} | all-to-all | bytes 1048576 | tf_op jit(solution)/shard_map/all_to_all | solution.py:64
  185.9 2.4 convolution_convert_fusion
  188.3 4.5 %all-to-all-start.7 = ((bf16[32,64,256]{2,1,0:T(8,128)(2,1)}), bf16[32,64,256]{2,1,0:T(8,128)(2,1)S(1)}, u32[]{:S(2)}, u32[]{:S(2)}) async-start(bf16[32,64,256]{2,1,0:T(8,128)(2,1)} %bitcast.108), calls=%async_computation.7 | async-start | bytes 2097152 | tf_op jit(solution)/shard_map/all_to_all | solution.py:31
  193.3 28.1 %all-to-all-done.7 = bf16[32,64,256]{2,1,0:T(8,128)(2,1)S(1)} async-done(((bf16[32,64,256]{2,1,0:T(8,128)(2,1)}), bf16[32,64,256]{2,1,0:T(8,128)(2,1)S(1)}, u32[]{:S(2)}, u32[]{:S(2)}) %all-to-all-start.7) | async-done | bytes 1048608 | tf_op jit(solution)/shard_map/all_to_all | solution.py:31
  221.4 4.0 %multiply_reduce_fusion = (f32[256]{0:T(256)S(1)}, f32[256]{0:T(256)S(1)}, bf16[1024,256]{1,0:T(8,128)(2,1)S(1)}) fusion(f32[1024,256]{1,0:T(8,128)} %copy-done.7, bf16[1024,2048]{0,1:T(8,128)(2,1)} %bitcast.119, bf16[2048,256]{1,0:T(8,128)(2,1)S(1)} %bitcast.107), kind=kOutput, calls=%fused_computation.35 | convolution fusion | flops 1075052032 | bytes 6817792 | tf_op jit(solution)/shard_map/dot_general | solution.py:72
  225.4 1.3 fusion.24
  227.4 36.9 %all_to_all.55 = bf16[32,72,256]{2,1,0:T(8,128)(2,1)S(1)} all-to-all(bf16[32,72,256]{2,1,0:T(8,128)(2,1)S(1)} %pad_maximum_fusion.1), channel_id=1, replica_groups=mesh['band'=8,'space'=32] {'space'}, dimensions={0} | all-to-all | bytes 2359296 | tf_op jit(solution)/shard_map/all_to_all | solution.py:31
  264.5 1.3 fusion.27
  266.0 13.5 %all_to_all.56 = bf16[8,32,1152]{2,1,0:T(8,128)(2,1)S(1)} all-to-all(bf16[8,32,1152]{2,1,0:T(8,128)(2,1)S(1)} %bitcast.105), channel_id=1, replica_groups=mesh['band'=8,'space'=32] {'band'}, dimensions={0} | all-to-all | bytes 1179648 | tf_op jit(solution)/shard_map/all_to_all | solution.py:55
  (59 shorter events, 6.3 us)
Async XLA Ops:
  0.6 1.0 copy-start
  1.7 43.2 %copy-start.3 = (bf16[1,1024,2048]{2,1,0:T(8,128)(2,1)S(1)}, bf16[1,1024,2048]{2,1,0:T(8,128)(2,1)}, u32[]{:S(2)}) copy-start(bf16[1,1024,2048]{2,1,0:T(8,128)(2,1)} %param.3) | copy-start | bytes 12582916
  61.8 13.8 %all-to-all-start.2 = ((bf16[8,32,1024]{2,1,0:T(8,128)(2,1)}), bf16[8,32,1024]{2,1,0:T(8,128)(2,1)S(1)}, u32[]{:S(2)}, u32[]{:S(2)}) async-start(bf16[8,32,1024]{2,1,0:T(8,128)(2,1)} %broadcast_in_dim.8), calls=%async_computation.2 | async-start | bytes 1048576 | tf_op jit(solution)/shard_map/all_to_all | solution.py:64
  80.0 33.5 %all-to-all-start.3 = ((bf16[32,64,256]{2,1,0:T(8,128)(2,1)}), bf16[32,64,256]{2,1,0:T(8,128)(2,1)S(1)}, u32[]{:S(2)}, u32[]{:S(2)}) async-start(bf16[32,64,256]{2,1,0:T(8,128)(2,1)} %bitcast.9), calls=%async_computation.3 | async-start | bytes 2097152 | tf_op jit(solution)/shard_map/all_to_all | solution.py:31
  113.6 4.6 %copy-start.1 = (bf16[1,2048,1024]{2,1,0:T(8,128)(2,1)S(1)}, bf16[1,2048,1024]{2,1,0:T(8,128)(2,1)}, u32[]{:S(2)}) copy-start(bf16[1,2048,1024]{2,1,0:T(8,128)(2,1)} %param.4) | copy-start | bytes 12582916
  117.2 1.0 copy-start.7
  120.2 37.1 %copy-start.4 = (bf16[1,1024,2048]{2,1,0:T(8,128)(2,1)S(1)}, bf16[1,1024,2048]{2,1,0:T(8,128)(2,1)}, u32[]{:S(2)}) copy-start(bf16[1,1024,2048]{2,1,0:T(8,128)(2,1)} %param.3) | copy-start | bytes 12582916
  158.8 27.0 %copy-start.5 = (bf16[1,1024,2048]{2,1,0:T(8,128)(2,1)S(1)}, bf16[1,1024,2048]{2,1,0:T(8,128)(2,1)}, u32[]{:S(2)}) copy-start(bf16[1,1024,2048]{2,1,0:T(8,128)(2,1)} %param.3) | copy-start | bytes 12582916
  188.3 33.1 %all-to-all-start.7 = ((bf16[32,64,256]{2,1,0:T(8,128)(2,1)}), bf16[32,64,256]{2,1,0:T(8,128)(2,1)S(1)}, u32[]{:S(2)}, u32[]{:S(2)}) async-start(bf16[32,64,256]{2,1,0:T(8,128)(2,1)} %bitcast.108), calls=%async_computation.7 | async-start | bytes 2097152 | tf_op jit(solution)/shard_map/all_to_all | solution.py:31
  221.4 4.0 %copy-start.2 = (bf16[1,2048,1024]{2,1,0:T(8,128)(2,1)S(1)}, bf16[1,2048,1024]{2,1,0:T(8,128)(2,1)}, u32[]{:S(2)}) copy-start(bf16[1,2048,1024]{2,1,0:T(8,128)(2,1)} %param.4) | copy-start | bytes 12582916
  227.4 37.1 %copy-start.6 = (bf16[1,1024,2048]{2,1,0:T(8,128)(2,1)S(1)}, bf16[1,1024,2048]{2,1,0:T(8,128)(2,1)}, u32[]{:S(2)}) copy-start(bf16[1,1024,2048]{2,1,0:T(8,128)(2,1)} %param.3) | copy-start | bytes 12582916

commit v2 on v0

v2 whole, which is shorter than its diff:
```python
import functools
import jax
import jax.numpy as jnp
from jax import lax
from jax.experimental import pallas as pl
from jax.experimental.pallas import tpu as pltpu
from jax.sharding import PartitionSpec as P

damping = 1.0
BAND = "band"
SPACE = "space"
f32, bf16 = jnp.float32, jnp.bfloat16
EXTRA = 8
TAIL = 128
STEP = 256

VMEM = pl.BlockSpec(memory_space=pltpu.VMEM)
SMEM = pl.BlockSpec(memory_space=pltpu.SMEM)


def order_of(blocks):
    if blocks != 32:
        return list(range(blocks))
    return [x * 8 + high * 4 + low for low in range(4) for x in range(4) for high in range(2)]


def dot(a, b, dims=((1,), (0,))):
    return lax.dot_general(a, b, (dims, ((), ())), preferred_element_type=f32)


def call(body, outs, scratch, flops, args, specs=None):
    moved = sum(a.size * a.dtype.itemsize for a in args) + sum(o.size * o.dtype.itemsize for o in outs)
    return pl.pallas_call(
        body,
        out_shape=outs,
        in_specs=specs or [VMEM] * len(args),
        out_specs=[VMEM] * len(outs),
        scratch_shapes=scratch,
        cost_estimate=pl.CostEstimate(flops=flops, bytes_accessed=moved, transcendentals=0),
        compiler_params=pltpu.CompilerParams(vmem_limit_bytes=40 * 1024 * 1024),
    )(*args)


def shape(dims, kind):
    return jax.ShapeDtypeStruct(dims, kind)


def put_blocks(out, rows, first, place, rank):
    for i in range(rows.shape[0] // rank):
        out[place[first + i], :rank, :] = rows[i * rank:(i + 1) * rank]


def take_blocks(got, natural, order, rank):
    for q, s in enumerate(order):
        natural[s * rank:(s + 1) * rank, :] = got[q, :rank, :]


def first_body(place, rank, share, perm, d, r, out, dp):
    for k in range(d.shape[0] // share):
        dp[k * share:(k + 1) * share, :] = d[pl.ds(pl.multiple_of(perm[k] * share, share), share), :]
    step = min(STEP, r.shape[0])
    for j in range(0, r.shape[0], step):
        put_blocks(out, dot(r[j:j + step, :], dp[...], ((1,), (1,))).astype(bf16), j // rank, place, rank)


def adjoint_body(order, rank, tail, got, l, own, oth, natural):
    take_blocks(got, natural, order, rank)
    cells, half = l.shape[0], own.shape[0]
    step = min(STEP, cells)
    for j in range(0, cells, step):
        t = dot(l[j:j + step, :], natural[...]).T
        own[:, j:j + step] = t[:half]
        oth[:, j:j + step] = t[half:].astype(bf16)
    if tail:
        rows = got[0, rank:, :].astype(f32)
        for q in range(1, len(order)):
            rows = rows + got[q, rank:, :].astype(f32)
        rows = rows[:4] + rows[4:]
        high = rows.astype(bf16).astype(f32)
        t = jnp.concatenate([high, rows - high, jnp.zeros((TAIL - 8, rows.shape[1]), f32)], axis=0).T
        own[:, cells:] = t[:half]
        oth[:, cells:] = t[half:].astype(bf16)


def pair_body(cells, tail, own, got, mine, *rest):
    share = mine.shape[0]
    total = own[:, :cells] + got[:, :cells].astype(f32)
    mine[:, :cells] = total[:share]
    for k, out in enumerate(rest):
        out[:, :cells] = total[(k + 1) * share:(k + 2) * share].astype(bf16)
    if tail:
        part = own[:, cells:] + got[:, cells:].astype(f32)
        lane = lax.broadcasted_iota(jnp.int32, part.shape, 1)
        both = part + pltpu.roll(part, TAIL - 4, 1)
        high = both.astype(bf16).astype(f32)
        low = pltpu.roll(both - high, 4, 1)
        part = jnp.where(lane < 4, high, jnp.where(lane < 8, low, 0.0))
        mine[:, cells:] = part[:share]
        for k, out in enumerate(rest):
            out[:, cells:] = part[(k + 1) * share:(k + 2) * share].astype(bf16)


def coeff_body(place, rank, bands, cross, pa, pb, *rest):
    if cross:
        qa, qb, l, out, norms, p = rest
    else:
        l, out, norms, p = rest
    half = pa.shape[0]
    p[:half, :] = pa[...]
    p[half:, :] = pb[...]
    width = l.shape[1]
    step = min(STEP, width)
    for j in range(0, width, step):
        put_blocks(out, dot(p[...], l[:, j:j + step]).astype(bf16).T, j // rank, place, rank)
    lane = lax.broadcasted_iota(jnp.int32, (half, TAIL), 1)
    for h, (now, old) in enumerate(((pa, qa), (pb, qb)) if cross else ((pa, None), (pb, None))):
        v = now[...].astype(f32)
        col = jnp.where(lane == 0, jnp.sum(v * v, axis=1, keepdims=True) * (1.0 / bands), 0.0)
        if cross:
            col = jnp.where(lane == 1, jnp.sum(v * old[...].astype(f32), axis=1, keepdims=True) * (1.0 / bands), col)
        norms[h * half:(h + 1) * half, :] = col


def middle_body(order, place, rank, cross, got, norms, r, *rest):
    if cross:
        old, out, seen, natural, turned = rest
    else:
        out, seen, natural, turned = rest
    take_blocks(got, natural, order, rank)
    width, cells = r.shape
    step = min(STEP, width)
    for j in range(0, width, step):
        turned[:, j:j + step] = natural[j:j + step, :].T
    step = min(STEP, cells)
    square = product = None
    for j in range(0, cells, step):
        s = dot(turned[...], r[:, j:j + step])
        seen[:, j:j + step] = s.astype(bf16)
        a = jnp.sum(s * s, axis=1, keepdims=True)
        square = a if square is None else square + a
        if cross:
            a = jnp.sum(s * old[:, j:j + step].astype(f32), axis=1, keepdims=True)
            product = a if product is None else product + a
    step = min(STEP, width)
    for j in range(0, width, step):
        back = dot(r[j:j + step, :], seen[...], ((1,), (1,))).astype(bf16)
        put_blocks(out, back, j // rank, place, rank)
    tile = norms[...]
    lane = lax.broadcasted_iota(jnp.int32, tile.shape, 1)
    pp, px = tile[:, 0:1], tile[:, 1:2]
    cols = jnp.where(lane == 0, pp, jnp.where(lane == 1, square + damping * pp, 0.0))
    if cross:
        cols = jnp.where(lane == 2, product + damping * px, cols)
    rows = cols.T[:4]
    high = rows.astype(bf16).astype(f32)
    rows = jnp.concatenate([high, rows - high], axis=0).astype(bf16)
    for q in range(len(order)):
        out[q, rank:, :] = rows


def per_device(left_factor, right_factor, data):
    left, right, d = left_factor[0], right_factor[0], data[0]
    m, cells = d.shape
    width = left.shape[1]
    bands, blocks = lax.axis_size(BAND), lax.axis_size(SPACE)
    rank = width // blocks
    share, half, pairs = m // bands, m // 2, bands // 2
    order = order_of(blocks)
    place = [order.index(s) for s in range(blocks)]
    me = lax.axis_index(BAND)
    work = 2 * m * cells * width

    def exchange(v):
        return lax.all_to_all(v, SPACE, 0, 0, tiled=True, axis_index_groups=[order])

    def swap(v, flip):
        return lax.ppermute(v, BAND, [(i, i ^ flip) for i in range(bands)])

    def reduce_band(got, tail):
        columns = cells + (TAIL if tail else 0)
        own, oth = call(
            functools.partial(adjoint_body, order, rank, tail),
            [shape((half, columns), f32), shape((half, columns), bf16)],
            [pltpu.VMEM((width, m), bf16)], work, (got, left),
        )
        mine, *rest = call(
            functools.partial(pair_body, cells, tail),
            [shape((share, columns), f32)] + [shape((share, columns), bf16)] * (pairs - 1),
            [], half * columns, (own, swap(oth, 1)),
        )
        total = mine
        for k in range(1, pairs):
            total = total + swap(rest[k - 1], 2 * k).astype(f32)
        if not tail:
            return total, None
        return total[:, :cells], total[:, cells:cells + 4] + total[:, cells + 4:cells + 8]

    def gather(v):
        v = v.astype(bf16)
        v = jnp.concatenate([v] + [swap(v, 2 * k) for k in range(1, pairs)], axis=0)
        return v, swap(v, 1)

    def forward(now, old=()):
        coeff, norms = call(
            functools.partial(coeff_body, place, rank, bands, bool(old)),
            [shape((blocks, rank, m), bf16), shape((m, TAIL), f32)],
            [pltpu.VMEM((m, cells), bf16)], work, (*now, *old, left),
        )
        return exchange(coeff), norms

    def middle(got, norms, old=()):
        out, seen = call(
            functools.partial(middle_body, order, place, rank, bool(old)),
            [shape((blocks, rank + EXTRA, m), bf16), shape((m, cells), bf16)],
            [pltpu.VMEM((width, m), bf16), pltpu.VMEM((m, width), bf16)], 2 * work, (got, norms, right, *old),
        )
        return exchange(out), seen

    perm = jnp.stack([me ^ (2 * y + c) for c in range(2) for y in range(pairs)]).astype(jnp.int32)
    back = call(
        functools.partial(first_body, place, rank, share),
        [shape((blocks, rank, m), bf16)], [pltpu.VMEM((m, cells), bf16)], work, (perm, d, right),
        [SMEM, VMEM, VMEM],
    )[0]
    got = exchange(back)
    r0, _ = reduce_band(got, False)
    p0 = gather(r0)
    got, norms = forward(p0)
    got, s0 = middle(got, norms)
    q0, sums = reduce_band(got, True)
    rr0, c0 = sums[:, 0:1], sums[:, 1:2]
    q0 = q0 + damping * r0
    a0 = rr0 / c0
    r1 = r0 - a0 * q0
    p1 = gather(r1)
    got, norms = forward(p1, p0)
    got, _ = middle(got, norms, (s0,))
    q1, sums = reduce_band(got, True)
    rr1, n11, n01 = sums[:, 0:1], sums[:, 1:2], sums[:, 2:3]
    q1 = q1 + damping * r1
    b0 = rr1 / rr0
    c1 = n11 + 2 * b0 * n01 + b0 * b0 * c0
    a1 = rr1 / c1
    return a0 * r0 + a1 * (r1 + b0 * r0), r1 - a1 * (q1 + b0 * q0)


def solution(mesh):
    return jax.shard_map(
        per_device,
        mesh=mesh,
        in_specs=(P("band", "space", None), P("band", None, "space"), P("band", None, "space")),
        out_specs=(P("band", "space"), P("band", "space")),
        check_vma=False,
    )
```

time: 649 us -> 251 us (0.39)
  blocking collectives: 382 us -> 180 us
  waiting for transfers between devices: 194 us -> 27.4 us
  matrix products: 39.3 us -> 0 us
  starting transfers between devices: 0.12 us -> 23.2 us
  Pallas kernels: 0 us -> 14 us
  between operations: 13.8 us -> 0.79 us
  other arithmetic: 8.19 us -> 1.6 us
    psum x3 -> x0, blocking collectives: 218 us -> none  [the longest x2 146 us: squares(): return lax.psum(jnp.sum(vector * vector, axis=1), 'space')]
    psum x3 -> x0, waiting for transfers between devices: 194 us -> none  [combine(): return lax.psum(partial_value, 'band')]
    dot_general x8 -> x0, matrix products: 39.3 us -> none  [the longest x3 17.5 us: adjoint(): lax.dot_general(seen, right, contract, preferred_element_type=jnp.float32)]
    ppermute x0 -> x20, waiting for transfers between devices: none -> 27.4 us  [swap(): return lax.ppermute(v, BAND, [(i, i ^ flip) for i in range(bands)])]
    ppermute x0 -> x20, starting transfers between devices: none -> 23.2 us  [swap(): return lax.ppermute(v, BAND, [(i, i ^ flip) for i in range(bands)])]
    all_to_all x5, blocking collectives: 165 us -> 180 us  [exchange(): return lax.all_to_all(v, SPACE, 0, 0, tiled=True, axis_index_groups=[order])]
    pallas_call x0 -> x11, Pallas kernels: none -> 14 us  [call(): pl.pallas_call(body, out_shape=outs, in_specs=specs or [VMEM] * len(args)...]
    convert_element_type x5 -> x0, local copies, waits for them, and re-layouts: 7.08 us -> none  [the longest x3 4.28 us: adjoint(): lax.dot_general(seen, right, contract, preferred_element_type=jnp.float32)]
  transfers between devices with their start and end apart: 3 -> 20, of which waited for: 3 -> 18; matrix products, arithmetic and copies ran while one was open for 0% -> 0% of each run, Pallas kernels for 0% -> 0%
where the time goes in v2:
time: 251 us; the launch traced here: 250 us
  blocking collectives  180 us (72%)
  waiting for transfers between devices  27.4 us (11%)
  starting transfers between devices  23.2 us (9%)
  Pallas kernels  14 us (6%)
  local copies, waits for them, and re-layouts  3.32 us (1%)
    all_to_all x5, blocking collectives, exchange(): return lax.all_to_all(v, SPACE, 0, 0, tiled=True, axis_index_groups=[order])  180 us
    ppermute x20, waiting for transfers between devices, swap(): return lax.ppermute(v, BAND, [(i, i ^ flip) for i in range(bands)])  27.4 us
    ppermute x20, starting transfers between devices, swap(): return lax.ppermute(v, BAND, [(i, i ^ flip) for i in range(bands)])  23.2 us
    pallas_call x11, Pallas kernels, call(): pl.pallas_call(body, out_shape=outs, in_specs=specs or [VMEM] * len(args)...  14 us
  transfers between devices with their start and end apart: 20, of which 18 were waited for; matrix products, arithmetic and copies ran while one was open for 0% of the time, Pallas kernels for 0%

profile of v2, /device:TPU:32, one launch (start us, length us, event | category | flops | bytes accessed | tf_op | source)
XLA Modules:
  0.0 250.0 jit_solution(13530314496561109233)
XLA Ops:
  0.7 2.2 copy-done.1
  4.0 1.8 shard_map.50
  5.8 40.2 %all_to_all.25.got = bf16[32,64,256]{2,1,0:T(8,128)(2,1)S(1)} all-to-all(bf16[32,64,256]{2,1,0:T(8,128)(2,1)S(1)} %shard_map.50), channel_id=1, replica_groups={{0,4,8,12,16,20,24,28,1,5,9,13,17,21,25,29,2,6,10,14,18,22,26,30,3,7,11..., dimensions={0} | all-to-all | bytes 2097152 | tf_op jit(solution)/shard_map/all_to_all | solution.py:174
  49.0 1.7 collective-permute-start.1
  50.7 2.9 %collective-permute-start.2 = (bf16[32,1024]{1,0:T(8,128)(2,1)S(1)}, bf16[32,1024]{1,0:T(8,128)(2,1)S(1)}, u32[]{:S(2)}, u32[]{:S(2)}) collective-permute-start(bf16[32,1024]{1,0:T(8,128)(2,1)S(1)} %get-tuple-element.31), channel_id=1, source_target_pairs={{0,128},{32,160},{64,192},{96,224},{128,0},{160,32},{192,64},{224,... | collective-permute-start | bytes 196616 | tf_op jit(solution)/shard_map/ppermute | solution.py:177
  53.8 3.3 %collective-permute-done.2 = bf16[32,1024]{1,0:T(8,128)(2,1)S(1)} collective-permute-done((bf16[32,1024]{1,0:T(8,128)(2,1)S(1)}, bf16[32,1024]{1,0:T(8,128)(2,1)S(1)}, u32[]{:S(2)}, u32[]{:S(2)}) %collective-permute-start.2) | collective-permute-done | bytes 65568 | tf_op jit(solution)/shard_map/ppermute | solution.py:177
  57.1 2.0 collective-permute-done.3
  60.5 2.8 %collective-permute-start.4 = (bf16[32,1024]{1,0:T(8,128)(2,1)S(1)}, bf16[32,1024]{1,0:T(8,128)(2,1)S(1)}, u32[]{:S(2)}, u32[]{:S(2)}) collective-permute-start(bf16[32,1024]{1,0:T(8,128)(2,1)S(1)} %get-tuple-element.54), channel_id=1, source_target_pairs={{0,64},{32,96},{64,0},{96,32},{128,192},{160,224},{192,128},{224,1... | collective-permute-start | bytes 196616 | tf_op jit(solution)/shard_map/ppermute | solution.py:177
  69.2 33.8 %all_to_all.26.got = bf16[32,64,256]{2,1,0:T(8,128)(2,1)S(1)} all-to-all(bf16[32,64,256]{2,1,0:T(8,128)(2,1)S(1)} %get-tuple-element.33), channel_id=1, replica_groups={{0,4,8,12,16,20,24,28,1,5,9,13,17,21,25,29,2,6,10,14,18,22,26,30,3,7,11..., dimensions={0} | all-to-all | bytes 2097152 | tf_op jit(solution)/shard_map/all_to_all | solution.py:174
  103.0 2.4 shard_map.54
  105.4 36.1 %all_to_all.27.got = bf16[32,72,256]{2,1,0:T(8,128)(2,1)S(1)} all-to-all(bf16[32,72,256]{2,1,0:T(8,128)(2,1)S(1)} %get-tuple-element.35), channel_id=1, replica_groups={{0,4,8,12,16,20,24,28,1,5,9,13,17,21,25,29,2,6,10,14,18,22,26,30,3,7,11..., dimensions={0} | all-to-all | bytes 2359296 | tf_op jit(solution)/shard_map/all_to_all | solution.py:174
  143.0 1.6 collective-permute-done.8.got
  146.1 2.1 collective-permute-start.10
  149.9 2.3 collective-permute-done.10
  152.2 1.6 collective-permute-done.11
  155.9 2.5 collective-permute-start.12
  159.8 1.6 collective-permute-done.13
  164.5 33.5 %all_to_all.28.got = bf16[32,64,256]{2,1,0:T(8,128)(2,1)S(1)} all-to-all(bf16[32,64,256]{2,1,0:T(8,128)(2,1)S(1)} %get-tuple-element.42), channel_id=1, replica_groups={{0,4,8,12,16,20,24,28,1,5,9,13,17,21,25,29,2,6,10,14,18,22,26,30,3,7,11..., dimensions={0} | all-to-all | bytes 2097152 | tf_op jit(solution)/shard_map/all_to_all | solution.py:174
  197.9 2.5 shard_map.58
  200.4 36.1 %all_to_all.29.got = bf16[32,72,256]{2,1,0:T(8,128)(2,1)S(1)} all-to-all(bf16[32,72,256]{2,1,0:T(8,128)(2,1)S(1)} %get-tuple-element.45), channel_id=1, replica_groups={{0,4,8,12,16,20,24,28,1,5,9,13,17,21,25,29,2,6,10,14,18,22,26,30,3,7,11..., dimensions={0} | all-to-all | bytes 2359296 | tf_op jit(solution)/shard_map/all_to_all | solution.py:174
  238.0 1.6 collective-permute-done.16.got
  241.1 2.1 collective-permute-start.18
  244.7 2.6 %collective-permute-done.18 = bf16[32,1152]{1,0:T(8,128)(2,1)S(1)} collective-permute-done((bf16[32,1152]{1,0:T(8,128)(2,1)S(1)}, bf16[32,1152]{1,0:T(8,128)(2,1)S(1)}, u32[]{:S(2)}, u32[]{:S(2)}) %collective-permute-start.18) | collective-permute-done | bytes 73760 | tf_op jit(solution)/shard_map/ppermute | solution.py:177
  247.2 1.6 collective-permute-done.19
  (52 shorter events, 28.5 us)
Async XLA Ops:
  0.7 2.2 copy-start.1
  2.9 1.0 copy-start.3
  4.0 42.0 %copy-start = (bf16[1,1024,2048]{2,1,0:T(8,128)(2,1)S(1)}, bf16[1,1024,2048]{2,1,0:T(8,128)(2,1)}, u32[]{:S(2)}) copy-start(bf16[1,1024,2048]{2,1,0:T(8,128)(2,1)} %param.3) | copy-start | bytes 12582916
  47.4 1.6 collective-permute-start
  49.0 4.8 %collective-permute-start.1 = (bf16[32,1024]{1,0:T(8,128)(2,1)S(1)}, bf16[32,1024]{1,0:T(8,128)(2,1)S(1)}, u32[]{:S(2)}, u32[]{:S(2)}) collective-permute-start(bf16[32,1024]{1,0:T(8,128)(2,1)S(1)} %get-tuple-element.30), channel_id=1, source_target_pairs={{0,64},{32,96},{64,0},{96,32},{128,192},{160,224},{192,128},{224,1... | collective-permute-start | bytes 196616 | tf_op jit(solution)/shard_map/ppermute | solution.py:177
  50.7 6.4 %collective-permute-start.2 = (bf16[32,1024]{1,0:T(8,128)(2,1)S(1)}, bf16[32,1024]{1,0:T(8,128)(2,1)S(1)}, u32[]{:S(2)}, u32[]{:S(2)}) collective-permute-start(bf16[32,1024]{1,0:T(8,128)(2,1)S(1)} %get-tuple-element.31), channel_id=1, source_target_pairs={{0,128},{32,160},{64,192},{96,224},{128,0},{160,32},{192,64},{224,... | collective-permute-start | bytes 196616 | tf_op jit(solution)/shard_map/ppermute | solution.py:177
  53.6 5.5 %collective-permute-start.3 = (bf16[32,1024]{1,0:T(8,128)(2,1)S(1)}, bf16[32,1024]{1,0:T(8,128)(2,1)S(1)}, u32[]{:S(2)}, u32[]{:S(2)}) collective-permute-start(bf16[32,1024]{1,0:T(8,128)(2,1)S(1)} %get-tuple-element.32), channel_id=1, source_target_pairs={{0,192},{32,224},{64,128},{96,160},{128,64},{160,96},{192,0},{224,... | collective-permute-start | bytes 196616 | tf_op jit(solution)/shard_map/ppermute | solution.py:177
  59.1 5.6 %collective-permute-start.6 = (bf16[32,1024]{1,0:T(8,128)(2,1)S(1)}, bf16[32,1024]{1,0:T(8,128)(2,1)S(1)}, u32[]{:S(2)}, u32[]{:S(2)}) collective-permute-start(bf16[32,1024]{1,0:T(8,128)(2,1)S(1)} %get-tuple-element.54), channel_id=1, source_target_pairs={{0,192},{32,224},{64,128},{96,160},{128,64},{160,96},{192,0},{224,... | collective-permute-start | bytes 196616 | tf_op jit(solution)/shard_map/ppermute | solution.py:177
  59.8 5.8 %collective-permute-start.5 = (bf16[32,1024]{1,0:T(8,128)(2,1)S(1)}, bf16[32,1024]{1,0:T(8,128)(2,1)S(1)}, u32[]{:S(2)}, u32[]{:S(2)}) collective-permute-start(bf16[32,1024]{1,0:T(8,128)(2,1)S(1)} %get-tuple-element.54), channel_id=1, source_target_pairs={{0,128},{32,160},{64,192},{96,224},{128,0},{160,32},{192,64},{224,... | collective-permute-start | bytes 196616 | tf_op jit(solution)/shard_map/ppermute | solution.py:177
  60.5 5.8 %collective-permute-start.4 = (bf16[32,1024]{1,0:T(8,128)(2,1)S(1)}, bf16[32,1024]{1,0:T(8,128)(2,1)S(1)}, u32[]{:S(2)}, u32[]{:S(2)}) collective-permute-start(bf16[32,1024]{1,0:T(8,128)(2,1)S(1)} %get-tuple-element.54), channel_id=1, source_target_pairs={{0,64},{32,96},{64,0},{96,32},{128,192},{160,224},{192,128},{224,1... | collective-permute-start | bytes 196616 | tf_op jit(solution)/shard_map/ppermute | solution.py:177
  66.3 1.6 collective-permute-start.7
  67.9 35.1 %copy-start.2 = (bf16[1,2048,1024]{2,1,0:T(8,128)(2,1)S(1)}, bf16[1,2048,1024]{2,1,0:T(8,128)(2,1)}, u32[]{:S(2)}) copy-start(bf16[1,2048,1024]{2,1,0:T(8,128)(2,1)} %param.4) | copy-start | bytes 12582916
  142.9 1.7 collective-permute-start.8
  144.7 5.2 %collective-permute-start.9 = (bf16[32,1152]{1,0:T(8,128)(2,1)S(1)}, bf16[32,1152]{1,0:T(8,128)(2,1)S(1)}, u32[]{:S(2)}, u32[]{:S(2)}) collective-permute-start(bf16[32,1152]{1,0:T(8,128)(2,1)S(1)} %get-tuple-element.39), channel_id=1, source_target_pairs={{0,64},{32,96},{64,0},{96,32},{128,192},{160,224},{192,128},{224,1... | collective-permute-start | bytes 221192 | tf_op jit(solution)/shard_map/ppermute | solution.py:177
  146.1 6.1 %collective-permute-start.10 = (bf16[32,1152]{1,0:T(8,128)(2,1)S(1)}, bf16[32,1152]{1,0:T(8,128)(2,1)S(1)}, u32[]{:S(2)}, u32[]{:S(2)}) collective-permute-start(bf16[32,1152]{1,0:T(8,128)(2,1)S(1)} %get-tuple-element.40), channel_id=1, source_target_pairs={{0,128},{32,160},{64,192},{96,224},{128,0},{160,32},{192,64},{224,... | collective-permute-start | bytes 221192 | tf_op jit(solution)/shard_map/ppermute | solution.py:177
  148.3 5.6 %collective-permute-start.11 = (bf16[32,1152]{1,0:T(8,128)(2,1)S(1)}, bf16[32,1152]{1,0:T(8,128)(2,1)S(1)}, u32[]{:S(2)}, u32[]{:S(2)}) collective-permute-start(bf16[32,1152]{1,0:T(8,128)(2,1)S(1)} %get-tuple-element.41), channel_id=1, source_target_pairs={{0,192},{32,224},{64,128},{96,160},{128,64},{160,96},{192,0},{224,... | collective-permute-start | bytes 221192 | tf_op jit(solution)/shard_map/ppermute | solution.py:177
  154.2 5.6 %collective-permute-start.14 = (bf16[32,1024]{1,0:T(8,128)(2,1)S(1)}, bf16[32,1024]{1,0:T(8,128)(2,1)S(1)}, u32[]{:S(2)}, u32[]{:S(2)}) collective-permute-start(bf16[32,1024]{1,0:T(8,128)(2,1)S(1)} %fusion.3), channel_id=1, source_target_pairs={{0,192},{32,224},{64,128},{96,160},{128,64},{160,96},{192,0},{224,... | collective-permute-start | bytes 196616 | tf_op jit(solution)/shard_map/ppermute | solution.py:177
  155.6 5.8 %collective-permute-start.13 = (bf16[32,1024]{1,0:T(8,128)(2,1)S(1)}, bf16[32,1024]{1,0:T(8,128)(2,1)S(1)}, u32[]{:S(2)}, u32[]{:S(2)}) collective-permute-start(bf16[32,1024]{1,0:T(8,128)(2,1)S(1)} %fusion.3), channel_id=1, source_target_pairs={{0,128},{32,160},{64,192},{96,224},{128,0},{160,32},{192,64},{224,... | collective-permute-start | bytes 196616 | tf_op jit(solution)/shard_map/ppermute | solution.py:177
  155.9 5.4 %collective-permute-start.12 = (bf16[32,1024]{1,0:T(8,128)(2,1)S(1)}, bf16[32,1024]{1,0:T(8,128)(2,1)S(1)}, u32[]{:S(2)}, u32[]{:S(2)}) collective-permute-start(bf16[32,1024]{1,0:T(8,128)(2,1)S(1)} %fusion.3), channel_id=1, source_target_pairs={{0,64},{32,96},{64,0},{96,32},{128,192},{160,224},{192,128},{224,1... | collective-permute-start | bytes 196616 | tf_op jit(solution)/shard_map/ppermute | solution.py:177
  161.4 1.6 collective-permute-start.15
  237.9 1.7 collective-permute-start.16
  239.7 4.9 %collective-permute-start.17 = (bf16[32,1152]{1,0:T(8,128)(2,1)S(1)}, bf16[32,1152]{1,0:T(8,128)(2,1)S(1)}, u32[]{:S(2)}, u32[]{:S(2)}) collective-permute-start(bf16[32,1152]{1,0:T(8,128)(2,1)S(1)} %get-tuple-element.49), channel_id=1, source_target_pairs={{0,64},{32,96},{64,0},{96,32},{128,192},{160,224},{192,128},{224,1... | collective-permute-start | bytes 221192 | tf_op jit(solution)/shard_map/ppermute | solution.py:177
  241.1 6.1 %collective-permute-start.18 = (bf16[32,1152]{1,0:T(8,128)(2,1)S(1)}, bf16[32,1152]{1,0:T(8,128)(2,1)S(1)}, u32[]{:S(2)}, u32[]{:S(2)}) collective-permute-start(bf16[32,1152]{1,0:T(8,128)(2,1)S(1)} %get-tuple-element.50), channel_id=1, source_target_pairs={{0,128},{32,160},{64,192},{96,224},{128,0},{160,32},{192,64},{224,... | collective-permute-start | bytes 221192 | tf_op jit(solution)/shard_map/ppermute | solution.py:177
  243.3 5.6 %collective-permute-start.19 = (bf16[32,1152]{1,0:T(8,128)(2,1)S(1)}, bf16[32,1152]{1,0:T(8,128)(2,1)S(1)}, u32[]{:S(2)}, u32[]{:S(2)}) collective-permute-start(bf16[32,1152]{1,0:T(8,128)(2,1)S(1)} %get-tuple-element.51), channel_id=1, source_target_pairs={{0,192},{32,224},{64,128},{96,160},{128,64},{160,96},{192,0},{224,... | collective-permute-start | bytes 221192 | tf_op jit(solution)/shard_map/ppermute | solution.py:177

commit v3 on v2

--- a/solution.py
+++ b/solution.py
@@ -46,13 +46,18 @@
 
 
 def put_blocks(out, rows, first, place, rank):
+    half = rows.shape[1] // 2
     for i in range(rows.shape[0] // rank):
-        out[place[first + i], :rank, :] = rows[i * rank:(i + 1) * rank]
+        block = rows[i * rank:(i + 1) * rank]
+        out[place[first + i], :rank, :] = block[:, :half]
+        out[place[first + i], rank:2 * rank, :] = block[:, half:]
 
 
 def take_blocks(got, natural, order, rank):
+    half = got.shape[2]
     for q, s in enumerate(order):
-        natural[s * rank:(s + 1) * rank, :] = got[q, :rank, :]
+        natural[s * rank:(s + 1) * rank, :half] = got[q, :rank, :]
+        natural[s * rank:(s + 1) * rank, half:] = got[q, rank:2 * rank, :]
 
 
 def first_body(place, rank, share, perm, d, r, out, dp):
@@ -63,7 +68,7 @@
         put_blocks(out, dot(r[j:j + step, :], dp[...], ((1,), (1,))).astype(bf16), j // rank, place, rank)
 
 
-def adjoint_body(order, rank, tail, got, l, own, oth, natural):
+def adjoint_body(order, rank, scalars, got, l, own, oth, natural):
     take_blocks(got, natural, order, rank)
     cells, half = l.shape[0], own.shape[0]
     step = min(STEP, cells)
@@ -71,33 +76,91 @@
         t = dot(l[j:j + step, :], natural[...]).T
         own[:, j:j + step] = t[:half]
         oth[:, j:j + step] = t[half:].astype(bf16)
-    if tail:
-        rows = got[0, rank:, :].astype(f32)
+    if scalars:
+        rows = got[0, 2 * rank:, :].astype(f32)
         for q in range(1, len(order)):
-            rows = rows + got[q, rank:, :].astype(f32)
-        rows = rows[:4] + rows[4:]
+            rows = rows + got[q, 2 * rank:, :].astype(f32)
+        rows = jnp.concatenate([rows[:4], rows[4:]], axis=1)
+        first = rows[0:1] + rows[1:2]
+        zero = jnp.zeros_like(first)
+        if scalars == 2:
+            rows = [first, rows[2:3] + rows[3:4], zero, zero]
+        else:
+            rows = [first, rows[2:3], rows[3:4], zero]
+        rows = jnp.concatenate(rows, axis=0)
         high = rows.astype(bf16).astype(f32)
         t = jnp.concatenate([high, rows - high, jnp.zeros((TAIL - 8, rows.shape[1]), f32)], axis=0).T
         own[:, cells:] = t[:half]
         oth[:, cells:] = t[half:].astype(bf16)
 
 
-def pair_body(cells, tail, own, got, mine, *rest):
+def resplit(part):
+    lane = lax.broadcasted_iota(jnp.int32, part.shape, 1)
+    both = part + pltpu.roll(part, TAIL - 4, 1)
+    high = both.astype(bf16).astype(f32)
+    return jnp.where(lane < 4, high, jnp.where(lane < 8, pltpu.roll(both - high, 4, 1), 0.0))
+
+
+def pair_body(cells, tail, own, got, low, high):
+    mid = cells // 2
+    low[...] = (own[:, :mid] + got[:, :mid].astype(f32)).astype(bf16)
+    high[:, :mid] = (own[:, mid:cells] + got[:, mid:cells].astype(f32)).astype(bf16)
+    if tail:
+        high[:, mid:] = resplit(own[:, cells:] + got[:, cells:].astype(f32)).astype(bf16)
+
+
+def summed(v, got, k, b, share, columns):
+    rows, far = slice(b * share, (b + 1) * share), slice((b ^ k) * share, ((b ^ k) + 1) * share)
+    return v[rows, columns].astype(f32) + got[far, columns].astype(f32)
+
+
+def step_body(k, pairs, cells, v, got, out):
+    share = v.shape[0] // pairs
+    for b in range(pairs):
+        rows = slice(b * share, (b + 1) * share)
+        out[rows, :cells] = summed(v, got, k, b, share, slice(0, cells)).astype(bf16)
+        if v.shape[1] > cells:
+            out[rows, cells:] = resplit(summed(v, got, k, b, share, slice(cells, None))).astype(bf16)
+
+
+def spread_body(cells, own, got, mine, *rest):
     share = mine.shape[0]
     total = own[:, :cells] + got[:, :cells].astype(f32)
+    part = resplit(own[:, cells:] + got[:, cells:].astype(f32))
     mine[:, :cells] = total[:share]
+    mine[:, cells:] = part[:share]
     for k, out in enumerate(rest):
-        out[:, :cells] = total[(k + 1) * share:(k + 2) * share].astype(bf16)
-    if tail:
-        part = own[:, cells:] + got[:, cells:].astype(f32)
-        lane = lax.broadcasted_iota(jnp.int32, part.shape, 1)
-        both = part + pltpu.roll(part, TAIL - 4, 1)
-        high = both.astype(bf16).astype(f32)
-        low = pltpu.roll(both - high, 4, 1)
-        part = jnp.where(lane < 4, high, jnp.where(lane < 8, low, 0.0))
-        mine[:, cells:] = part[:share]
-        for k, out in enumerate(rest):
-            out[:, cells:] = part[(k + 1) * share:(k + 2) * share].astype(bf16)
+        rows = slice((k + 1) * share, (k + 2) * share)
+        out[:, :cells] = total[rows].astype(bf16)
+        out[:, cells:] = part[rows].astype(bf16)
+
+
+def start_body(pairs, low, got_low, high, got_high, r, p):
+    share, mid = r.shape[0] // pairs, low.shape[1]
+    for b in range(pairs):
+        rows = slice(b * share, (b + 1) * share)
+        for v, got, k, columns in ((low, got_low, 3, slice(0, mid)), (high, got_high, 1, slice(mid, 2 * mid))):
+            total = summed(v, got, k, b, share, slice(0, mid))
+            r[rows, columns] = total
+            p[rows, columns] = total.astype(bf16)
+
+
+def update_body(pairs, low, got_low, high, got_high, old, q, r, p, sums):
+    share, mid = r.shape[0] // pairs, low.shape[1]
+    for b in range(pairs):
+        rows = slice(b * share, (b + 1) * share)
+        tail = summed(high, got_high, 1, b, share, slice(mid, None))
+        tail = tail + pltpu.roll(tail, TAIL - 4, 1)
+        if b == 0:
+            sums[...] = tail
+        alpha = tail[:, 0:1] / tail[:, 1:2]
+        for v, got, k, columns in ((low, got_low, 3, slice(0, mid)), (high, got_high, 1, slice(mid, 2 * mid))):
+            was = old[rows, columns]
+            image = summed(v, got, k, b, share, slice(0, mid)) + damping * was
+            new = was - alpha * image
+            q[rows, columns] = image
+            r[rows, columns] = new
+            p[rows, columns] = new.astype(bf16)
 
 
 def coeff_body(place, rank, bands, cross, pa, pb, *rest):
@@ -151,11 +214,13 @@
     cols = jnp.where(lane == 0, pp, jnp.where(lane == 1, square + damping * pp, 0.0))
     if cross:
         cols = jnp.where(lane == 2, product + damping * px, cols)
-    rows = cols.T[:4]
-    high = rows.astype(bf16).astype(f32)
-    rows = jnp.concatenate([high, rows - high], axis=0).astype(bf16)
+    rows = cols.T[:8]
+    low = rows - rows.astype(bf16).astype(f32)
+    rows = jnp.concatenate([rows[0:1], low[0:1], rows[1:2], rows[2:3] if cross else low[1:2]], axis=0)
+    half = rows.shape[1] // 2
+    rows = jnp.concatenate([rows[:, :half], rows[:, half:]], axis=0).astype(bf16)
     for q in range(len(order)):
-        out[q, rank:, :] = rows
+        out[q, 2 * rank:, :] = rows
 
 
 def per_device(left_factor, right_factor, data):
@@ -176,34 +241,34 @@
     def swap(v, flip):
         return lax.ppermute(v, BAND, [(i, i ^ flip) for i in range(bands)])
 
-    def reduce_band(got, tail):
-        columns = cells + (TAIL if tail else 0)
+    def adjoint(got, scalars):
+        columns = cells + (TAIL if scalars else 0)
         own, oth = call(
-            functools.partial(adjoint_body, order, rank, tail),
+            functools.partial(adjoint_body, order, rank, scalars),
             [shape((half, columns), f32), shape((half, columns), bf16)],
             [pltpu.VMEM((width, m), bf16)], work, (got, left),
         )
-        mine, *rest = call(
+        return own, swap(oth, 1)
+
+    def along_y(own, got, tail):
+        mid = cells // 2
+        wide = mid + (TAIL if tail else 0)
+        low, high = call(
             functools.partial(pair_body, cells, tail),
-            [shape((share, columns), f32)] + [shape((share, columns), bf16)] * (pairs - 1),
-            [], half * columns, (own, swap(oth, 1)),
+            [shape((half, mid), bf16), shape((half, wide), bf16)], [], own.size, (own, got),
         )
-        total = mine
-        for k in range(1, pairs):
-            total = total + swap(rest[k - 1], 2 * k).astype(f32)
-        if not tail:
-            return total, None
-        return total[:, :cells], total[:, cells:cells + 4] + total[:, cells + 4:cells + 8]
-
-    def gather(v):
-        v = v.astype(bf16)
-        v = jnp.concatenate([v] + [swap(v, 2 * k) for k in range(1, pairs)], axis=0)
-        return v, swap(v, 1)
+        got_low, got_high = swap(low, 2), swap(high, 6)
+
+        def step(k, v, got):
+            return call(functools.partial(step_body, k, pairs, mid), [shape(v.shape, bf16)], [], v.size, (v, got))[0]
+
+        low, high = step(1, low, got_low), step(3, high, got_high)
+        return low, swap(low, 6), high, swap(high, 2)
 
     def forward(now, old=()):
         coeff, norms = call(
             functools.partial(coeff_body, place, rank, bands, bool(old)),
-            [shape((blocks, rank, m), bf16), shape((m, TAIL), f32)],
+            [shape((blocks, 2 * rank, half), bf16), shape((m, TAIL), f32)],
             [pltpu.VMEM((m, cells), bf16)], work, (*now, *old, left),
         )
         return exchange(coeff), norms
@@ -211,7 +276,7 @@
     def middle(got, norms, old=()):
         out, seen = call(
             functools.partial(middle_body, order, place, rank, bool(old)),
-            [shape((blocks, rank + EXTRA, m), bf16), shape((m, cells), bf16)],
+            [shape((blocks, 2 * rank + EXTRA, half), bf16), shape((m, cells), bf16)],
             [pltpu.VMEM((width, m), bf16), pltpu.VMEM((m, width), bf16)], 2 * work, (got, norms, right, *old),
         )
         return exchange(out), seen
@@ -219,28 +284,42 @@
     perm = jnp.stack([me ^ (2 * y + c) for c in range(2) for y in range(pairs)]).astype(jnp.int32)
     back = call(
         functools.partial(first_body, place, rank, share),
-        [shape((blocks, rank, m), bf16)], [pltpu.VMEM((m, cells), bf16)], work, (perm, d, right),
+        [shape((blocks, 2 * rank, half), bf16)], [pltpu.VMEM((m, cells), bf16)], work, (perm, d, right),
         [SMEM, VMEM, VMEM],
     )[0]
-    got = exchange(back)
-    r0, _ = reduce_band(got, False)
-    p0 = gather(r0)
+    state = shape((half, cells), f32)
+    parts = along_y(*adjoint(exchange(back), 0), False)
+    r0, p0 = call(
+        functools.partial(start_body, pairs), [state, shape((half, cells), bf16)], [], state.size, parts
+    )
+    p0 = (p0, swap(p0, 1))
     got, norms = forward(p0)
     got, s0 = middle(got, norms)
-    q0, sums = reduce_band(got, True)
-    rr0, c0 = sums[:, 0:1], sums[:, 1:2]
-    q0 = q0 + damping * r0
-    a0 = rr0 / c0
-    r1 = r0 - a0 * q0
-    p1 = gather(r1)
+    parts = along_y(*adjoint(got, 2), True)
+    q0, r1, p1, sums0 = call(
+        functools.partial(update_body, pairs),
+        [state, state, shape((half, cells), bf16), shape((share, TAIL), f32)], [], state.size, (*parts, r0),
+    )
+    p1 = (p1, swap(p1, 1))
     got, norms = forward(p1, p0)
     got, _ = middle(got, norms, (s0,))
-    q1, sums = reduce_band(got, True)
-    rr1, n11, n01 = sums[:, 0:1], sums[:, 1:2], sums[:, 2:3]
-    q1 = q1 + damping * r1
-    b0 = rr1 / rr0
-    c1 = n11 + 2 * b0 * n01 + b0 * b0 * c0
-    a1 = rr1 / c1
+    own, got = adjoint(got, 3)
+    columns = cells + TAIL
+    mine, *rest = call(
+        functools.partial(spread_body, cells),
+        [shape((share, columns), f32)] + [shape((share, columns), bf16)] * (pairs - 1),
+        [], half * columns, (own, got),
+    )
+    total = mine
+    for k in range(1, pairs):
+        total = total + swap(rest[k - 1], 2 * k).astype(f32)
+    sums1 = total[:, cells:cells + 4] + total[:, cells + 4:cells + 8]
+    r0, q0, r1 = r0[:share], q0[:share], r1[:share]
+    q1 = total[:, :cells] + damping * r1
+    rr0, c0 = sums0[:, 0:1], sums0[:, 1:2]
+    rr1, n11, n01 = sums1[:, 0:1], sums1[:, 1:2], sums1[:, 2:3]
+    a0, b0 = rr0 / c0, rr1 / rr0
+    a1 = rr1 / (n11 + 2 * b0 * n01 + b0 * b0 * c0)
     return a0 * r0 + a1 * (r1 + b0 * r0), r1 - a1 * (q1 + b0 * q0)
 
 

time: 251 us -> 243 us (0.968)
  starting transfers between devices: 23.2 us -> 16 us
  blocking collectives: 180 us -> 177 us
    ppermute x20 -> x16, starting transfers between devices: 23.2 us -> 16 us  [swap(): return lax.ppermute(v, BAND, [(i, i ^ flip) for i in range(bands)])]
    all_to_all x5, blocking collectives: 180 us -> 177 us  [exchange(): return lax.all_to_all(v, SPACE, 0, 0, tiled=True, axis_index_groups=[order])]
    ppermute x20 -> x16, waiting for transfers between devices: 27.4 us -> 28.7 us  [swap(): return lax.ppermute(v, BAND, [(i, i ^ flip) for i in range(bands)])]
    pallas_call x11 -> x17, Pallas kernels: 14 us -> 14.7 us  [call(): pl.pallas_call(body, out_shape=outs, in_specs=specs or [VMEM] * len(args)...]
  transfers between devices with their start and end apart: 20 -> 16, of which waited for: 18 -> 13; matrix products, arithmetic and copies ran while one was open for 0% -> 0% of each run, Pallas kernels for 0% -> 0%
where the time goes in v3:
time: 243 us; the launch traced here: 242 us
  blocking collectives  177 us (73%)
  waiting for transfers between devices  28.7 us (12%)
  starting transfers between devices  16 us (7%)
  Pallas kernels  14.7 us (6%)
  local copies, waits for them, and re-layouts  3.32 us (1%)
    all_to_all x5, blocking collectives, exchange(): return lax.all_to_all(v, SPACE, 0, 0, tiled=True, axis_index_groups=[order])  177 us
    ppermute x16, waiting for transfers between devices, swap(): return lax.ppermute(v, BAND, [(i, i ^ flip) for i in range(bands)])  28.7 us
    ppermute x16, starting transfers between devices, swap(): return lax.ppermute(v, BAND, [(i, i ^ flip) for i in range(bands)])  16 us
    pallas_call x17, Pallas kernels, call(): pl.pallas_call(body, out_shape=outs, in_specs=specs or [VMEM] * len(args)...  14.7 us
  transfers between devices with their start and end apart: 16, of which 13 were waited for; matrix products, arithmetic and copies ran while one was open for 0% of the time, Pallas kernels for 0%

profile of v3, /device:TPU:32, one launch (start us, length us, event | category | flops | bytes accessed | tf_op | source)
XLA Modules:
  0.0 241.6 jit_solution(5718972430777413428)
XLA Ops:
  0.7 2.2 copy-done.1
  4.0 1.8 shard_map.50
  5.8 40.2 %all_to_all.25.got = bf16[32,128,128]{2,1,0:T(8,128)(2,1)S(1)} all-to-all(bf16[32,128,128]{2,1,0:T(8,128)(2,1)S(1)} %shard_map.50), channel_id=1, replica_groups={{0,4,8,12,16,20,24,28,1,5,9,13,17,21,25,29,2,6,10,14,18,22,26,30,3,7,11..., dimensions={0} | all-to-all | bytes 2097152 | tf_op jit(solution)/shard_map/all_to_all | solution.py:239
  49.1 1.7 collective-permute-start.1
  50.7 2.2 collective-permute-start.3
  52.9 1.8 collective-permute-done.1.got
  54.7 3.1 %collective-permute-start.2 = (bf16[128,512]{1,0:T(8,128)(2,1)S(1)}, bf16[128,512]{1,0:T(8,128)(2,1)S(1)}, u32[]{:S(2)}, u32[]{:S(2)}) collective-permute-start(bf16[128,512]{1,0:T(8,128)(2,1)S(1)} %shard_map.53.low), channel_id=1, source_target_pairs={{0,192},{32,224},{64,128},{96,160},{128,64},{160,96},{192,0},{224,... | collective-permute-start | bytes 393224 | tf_op jit(solution)/shard_map/ppermute | solution.py:242
  58.1 2.9 %collective-permute-done.2.got_low = bf16[128,512]{1,0:T(8,128)(2,1)S(1)} collective-permute-done((bf16[128,512]{1,0:T(8,128)(2,1)S(1)}, bf16[128,512]{1,0:T(8,128)(2,1)S(1)}, u32[]{:S(2)}, u32[]{:S(2)}) %collective-permute-start.2) | collective-permute-done | bytes 131104 | tf_op jit(solution)/shard_map/ppermute | solution.py:242
  61.0 1.9 collective-permute-done.4.got_high
  66.0 33.8 %all_to_all.26.got = bf16[32,128,128]{2,1,0:T(8,128)(2,1)S(1)} all-to-all(bf16[32,128,128]{2,1,0:T(8,128)(2,1)S(1)} %get-tuple-element.34), channel_id=1, replica_groups={{0,4,8,12,16,20,24,28,1,5,9,13,17,21,25,29,2,6,10,14,18,22,26,30,3,7,11..., dimensions={0} | all-to-all | bytes 2097152 | tf_op jit(solution)/shard_map/all_to_all | solution.py:239
  99.7 2.4 shard_map.57
  102.2 34.7 %all_to_all.27.got = bf16[32,136,128]{2,1,0:T(8,128)(2,1)S(1)} all-to-all(bf16[32,136,128]{2,1,0:T(8,128)(2,1)S(1)} %get-tuple-element.36), channel_id=1, replica_groups={{0,4,8,12,16,20,24,28,1,5,9,13,17,21,25,29,2,6,10,14,18,22,26,30,3,7,11..., dimensions={0} | all-to-all | bytes 2228224 | tf_op jit(solution)/shard_map/all_to_all | solution.py:239
  138.6 1.6 collective-permute-done.6.got
  140.3 1.6 collective-permute-start.9
  142.0 5.9 %collective-permute-done.9.got = bf16[128,640]{1,0:T(8,128)(2,1)S(1)} collective-permute-done((bf16[128,640]{1,0:T(8,128)(2,1)S(1)}, bf16[128,640]{1,0:T(8,128)(2,1)S(1)}, u32[]{:S(2)}, u32[]{:S(2)}) %collective-permute-start.9) | collective-permute-done | bytes 163872 | tf_op jit(solution)/shard_map/ppermute | solution.py:242
  148.2 1.6 collective-permute-start.8
  149.8 4.6 %collective-permute-done.8.got_low = bf16[128,512]{1,0:T(8,128)(2,1)S(1)} collective-permute-done((bf16[128,512]{1,0:T(8,128)(2,1)S(1)}, bf16[128,512]{1,0:T(8,128)(2,1)S(1)}, u32[]{:S(2)}, u32[]{:S(2)}) %collective-permute-start.8) | collective-permute-done | bytes 131104 | tf_op jit(solution)/shard_map/ppermute | solution.py:242
  157.8 33.4 %all_to_all.28.got = bf16[32,128,128]{2,1,0:T(8,128)(2,1)S(1)} all-to-all(bf16[32,128,128]{2,1,0:T(8,128)(2,1)S(1)} %get-tuple-element.44), channel_id=1, replica_groups={{0,4,8,12,16,20,24,28,1,5,9,13,17,21,25,29,2,6,10,14,18,22,26,30,3,7,11..., dimensions={0} | all-to-all | bytes 2097152 | tf_op jit(solution)/shard_map/all_to_all | solution.py:239
  191.3 2.5 %shard_map.64 = (bf16[32,136,128]{2,1,0:T(8,128)(2,1)S(1)}, bf16[256,1024]{1,0:T(8,128)(2,1)}) custom-call(bf16[32,128,128]{2,1,0:T(8,128)(2,1)S(1)} %all_to_all.28.got, f32[256,128]{1,0:T(8,128)S(1)} %get-tuple-element.45.norms, bf16[2048,1024]{1,0:T(8,128)(2,1)S(1)} %bitcast.18, bf16[256,1024]{1,0:T(8,128)(2,1)S(1)} %get-tuple-element.46.rest_0_), custom_call_target="tpu_custom_call" | custom-call | flops 2147483648 | bytes 7536640 | tf_op jit(solution)/shard_map/pallas_call | solution.py:33
  193.8 34.7 %all_to_all.29.got = bf16[32,136,128]{2,1,0:T(8,128)(2,1)S(1)} all-to-all(bf16[32,136,128]{2,1,0:T(8,128)(2,1)S(1)} %get-tuple-element.47), channel_id=1, replica_groups={{0,4,8,12,16,20,24,28,1,5,9,13,17,21,25,29,2,6,10,14,18,22,26,30,3,7,11..., dimensions={0} | all-to-all | bytes 2228224 | tf_op jit(solution)/shard_map/all_to_all | solution.py:239
  232.6 2.2 collective-permute-start.14
  234.8 1.7 collective-permute-start.15
  236.9 1.9 collective-permute-done.14
  238.8 1.6 collective-permute-done.15
  (43 shorter events, 18.6 us)
Async XLA Ops:
  0.7 2.2 copy-start.1
  2.9 1.0 copy-start.3
  4.0 42.0 %copy-start = (bf16[1,1024,2048]{2,1,0:T(8,128)(2,1)S(1)}, bf16[1,1024,2048]{2,1,0:T(8,128)(2,1)}, u32[]{:S(2)}) copy-start(bf16[1,1024,2048]{2,1,0:T(8,128)(2,1)} %param.3) | copy-start | bytes 12582916
  47.4 1.6 collective-permute-start
  49.1 5.6 %collective-permute-start.1 = (bf16[128,512]{1,0:T(8,128)(2,1)S(1)}, bf16[128,512]{1,0:T(8,128)(2,1)S(1)}, u32[]{:S(2)}, u32[]{:S(2)}) collective-permute-start(bf16[128,512]{1,0:T(8,128)(2,1)S(1)} %get-tuple-element.31.v), channel_id=1, source_target_pairs={{0,64},{32,96},{64,0},{96,32},{128,192},{160,224},{192,128},{224,1... | collective-permute-start | bytes 393224 | tf_op jit(solution)/shard_map/ppermute | solution.py:242
  50.7 7.1 %collective-permute-start.3 = (bf16[128,512]{1,0:T(8,128)(2,1)S(1)}, bf16[128,512]{1,0:T(8,128)(2,1)S(1)}, u32[]{:S(2)}, u32[]{:S(2)}) collective-permute-start(bf16[128,512]{1,0:T(8,128)(2,1)S(1)} %get-tuple-element.32.v), channel_id=1, source_target_pairs={{0,192},{32,224},{64,128},{96,160},{128,64},{160,96},{192,0},{224,... | collective-permute-start | bytes 393224 | tf_op jit(solution)/shard_map/ppermute | solution.py:242
  54.7 6.3 %collective-permute-start.2 = (bf16[128,512]{1,0:T(8,128)(2,1)S(1)}, bf16[128,512]{1,0:T(8,128)(2,1)S(1)}, u32[]{:S(2)}, u32[]{:S(2)}) collective-permute-start(bf16[128,512]{1,0:T(8,128)(2,1)S(1)} %shard_map.53.low), channel_id=1, source_target_pairs={{0,192},{32,224},{64,128},{96,160},{128,64},{160,96},{192,0},{224,... | collective-permute-start | bytes 393224 | tf_op jit(solution)/shard_map/ppermute | solution.py:242
  57.9 5.1 %collective-permute-start.4 = (bf16[128,512]{1,0:T(8,128)(2,1)S(1)}, bf16[128,512]{1,0:T(8,128)(2,1)S(1)}, u32[]{:S(2)}, u32[]{:S(2)}) collective-permute-start(bf16[128,512]{1,0:T(8,128)(2,1)S(1)} %shard_map.54.high), channel_id=1, source_target_pairs={{0,64},{32,96},{64,0},{96,32},{128,192},{160,224},{192,128},{224,1... | collective-permute-start | bytes 393224 | tf_op jit(solution)/shard_map/ppermute | solution.py:242
  63.0 1.6 collective-permute-start.5
  64.6 35.1 %copy-start.2 = (bf16[1,2048,1024]{2,1,0:T(8,128)(2,1)S(1)}, bf16[1,2048,1024]{2,1,0:T(8,128)(2,1)}, u32[]{:S(2)}) copy-start(bf16[1,2048,1024]{2,1,0:T(8,128)(2,1)} %param.4) | copy-start | bytes 12582916
  138.3 1.9 collective-permute-start.6
  140.3 7.5 %collective-permute-start.9 = (bf16[128,640]{1,0:T(8,128)(2,1)S(1)}, bf16[128,640]{1,0:T(8,128)(2,1)S(1)}, u32[]{:S(2)}, u32[]{:S(2)}) collective-permute-start(bf16[128,640]{1,0:T(8,128)(2,1)S(1)} %get-tuple-element.40.v), channel_id=1, source_target_pairs={{0,192},{32,224},{64,128},{96,160},{128,64},{160,96},{192,0},{224,... | collective-permute-start | bytes 491528 | tf_op jit(solution)/shard_map/ppermute | solution.py:242
  142.0 6.2 %collective-permute-start.7 = (bf16[128,512]{1,0:T(8,128)(2,1)S(1)}, bf16[128,512]{1,0:T(8,128)(2,1)S(1)}, u32[]{:S(2)}, u32[]{:S(2)}) collective-permute-start(bf16[128,512]{1,0:T(8,128)(2,1)S(1)} %get-tuple-element.39.v), channel_id=1, source_target_pairs={{0,64},{32,96},{64,0},{96,32},{128,192},{160,224},{192,128},{224,1... | collective-permute-start | bytes 393224 | tf_op jit(solution)/shard_map/ppermute | solution.py:242
  148.1 6.4 %collective-permute-start.10 = (bf16[128,640]{1,0:T(8,128)(2,1)S(1)}, bf16[128,640]{1,0:T(8,128)(2,1)S(1)}, u32[]{:S(2)}, u32[]{:S(2)}) collective-permute-start(bf16[128,640]{1,0:T(8,128)(2,1)S(1)} %shard_map.61.high), channel_id=1, source_target_pairs={{0,64},{32,96},{64,0},{96,32},{128,192},{160,224},{192,128},{224,1... | collective-permute-start | bytes 491528 | tf_op jit(solution)/shard_map/ppermute | solution.py:242
  148.2 6.3 %collective-permute-start.8 = (bf16[128,512]{1,0:T(8,128)(2,1)S(1)}, bf16[128,512]{1,0:T(8,128)(2,1)S(1)}, u32[]{:S(2)}, u32[]{:S(2)}) collective-permute-start(bf16[128,512]{1,0:T(8,128)(2,1)S(1)} %shard_map.60.low), channel_id=1, source_target_pairs={{0,192},{32,224},{64,128},{96,160},{128,64},{160,96},{192,0},{224,... | collective-permute-start | bytes 393224 | tf_op jit(solution)/shard_map/ppermute | solution.py:242
  154.8 1.6 collective-permute-start.11
  229.9 1.7 collective-permute-start.12
  231.7 5.2 %collective-permute-start.13 = (bf16[32,1152]{1,0:T(8,128)(2,1)S(1)}, bf16[32,1152]{1,0:T(8,128)(2,1)S(1)}, u32[]{:S(2)}, u32[]{:S(2)}) collective-permute-start(bf16[32,1152]{1,0:T(8,128)(2,1)S(1)} %get-tuple-element.51), channel_id=1, source_target_pairs={{0,64},{32,96},{64,0},{96,32},{128,192},{160,224},{192,128},{224,1... | collective-permute-start | bytes 221192 | tf_op jit(solution)/shard_map/ppermute | solution.py:242
  232.6 6.2 %collective-permute-start.14 = (bf16[32,1152]{1,0:T(8,128)(2,1)S(1)}, bf16[32,1152]{1,0:T(8,128)(2,1)S(1)}, u32[]{:S(2)}, u32[]{:S(2)}) collective-permute-start(bf16[32,1152]{1,0:T(8,128)(2,1)S(1)} %get-tuple-element.52), channel_id=1, source_target_pairs={{0,128},{32,160},{64,192},{96,224},{128,0},{160,32},{192,64},{224,... | collective-permute-start | bytes 221192 | tf_op jit(solution)/shard_map/ppermute | solution.py:242
  234.8 5.6 %collective-permute-start.15 = (bf16[32,1152]{1,0:T(8,128)(2,1)S(1)}, bf16[32,1152]{1,0:T(8,128)(2,1)S(1)}, u32[]{:S(2)}, u32[]{:S(2)}) collective-permute-start(bf16[32,1152]{1,0:T(8,128)(2,1)S(1)} %get-tuple-element.53), channel_id=1, source_target_pairs={{0,192},{32,224},{64,128},{96,160},{128,64},{160,96},{192,0},{224,... | collective-permute-start | bytes 221192 | tf_op jit(solution)/shard_map/ppermute | solution.py:242

commit v4 on v3

--- a/solution.py
+++ b/solution.py
@@ -21,7 +21,7 @@
 def order_of(blocks):
     if blocks != 32:
         return list(range(blocks))
-    return [x * 8 + high * 4 + low for low in range(4) for x in range(4) for high in range(2)]
+    return [(x if z % 2 == 0 else 3 - x) * 8 + z for z in range(8) for x in range(4)]
 
 
 def dot(a, b, dims=((1,), (0,))):
@@ -70,12 +70,7 @@
 
 def adjoint_body(order, rank, scalars, got, l, own, oth, natural):
     take_blocks(got, natural, order, rank)
-    cells, half = l.shape[0], own.shape[0]
-    step = min(STEP, cells)
-    for j in range(0, cells, step):
-        t = dot(l[j:j + step, :], natural[...]).T
-        own[:, j:j + step] = t[:half]
-        oth[:, j:j + step] = t[half:].astype(bf16)
+    adjoint_rows(natural, l, 0, l.shape[0] // 2, own, oth)
     if scalars:
         rows = got[0, 2 * rank:, :].astype(f32)
         for q in range(1, len(order)):
@@ -90,8 +85,23 @@
         rows = jnp.concatenate(rows, axis=0)
         high = rows.astype(bf16).astype(f32)
         t = jnp.concatenate([high, rows - high, jnp.zeros((TAIL - 8, rows.shape[1]), f32)], axis=0).T
-        own[:, cells:] = t[:half]
-        oth[:, cells:] = t[half:].astype(bf16)
+        mid, half = l.shape[0] // 2, own.shape[0]
+        own[:, mid:] = t[:half]
+        oth[:, mid:] = t[half:].astype(bf16)
+
+
+def adjoint_rows(natural, l, begin, end, own, oth):
+    half = own.shape[0]
+    step = min(STEP, end - begin)
+    for j in range(begin, end, step):
+        t = dot(l[j:j + step, :], natural[...]).T
+        columns = slice(j - begin, j - begin + step)
+        own[:, columns] = t[:half]
+        oth[:, columns] = t[half:].astype(bf16)
+
+
+def adjoint_second_body(natural, l, own, oth):
+    adjoint_rows(natural, l, l.shape[0] // 2, l.shape[0], own, oth)
 
 
 def resplit(part):
@@ -101,12 +111,10 @@
     return jnp.where(lane < 4, high, jnp.where(lane < 8, pltpu.roll(both - high, 4, 1), 0.0))
 
 
-def pair_body(cells, tail, own, got, low, high):
-    mid = cells // 2
-    low[...] = (own[:, :mid] + got[:, :mid].astype(f32)).astype(bf16)
-    high[:, :mid] = (own[:, mid:cells] + got[:, mid:cells].astype(f32)).astype(bf16)
-    if tail:
-        high[:, mid:] = resplit(own[:, cells:] + got[:, cells:].astype(f32)).astype(bf16)
+def pair_body(mid, own, got, out):
+    out[:, :mid] = (own[:, :mid] + got[:, :mid].astype(f32)).astype(bf16)
+    if own.shape[1] > mid:
+        out[:, mid:] = resplit(own[:, mid:] + got[:, mid:].astype(f32)).astype(bf16)
 
 
 def summed(v, got, k, b, share, columns):
@@ -123,65 +131,74 @@
             out[rows, cells:] = resplit(summed(v, got, k, b, share, slice(cells, None))).astype(bf16)
 
 
-def spread_body(cells, own, got, mine, *rest):
-    share = mine.shape[0]
-    total = own[:, :cells] + got[:, :cells].astype(f32)
-    part = resplit(own[:, cells:] + got[:, cells:].astype(f32))
-    mine[:, :cells] = total[:share]
+def spread_body(low, got_low, high, got_high, mine, *rest):
+    share, mid = mine.shape[0], high.shape[1]
+    cells = 2 * mid
+    total = low[:, :mid] + got_low[:, :mid].astype(f32)
+    second = high[...] + got_high[...].astype(f32)
+    part = resplit(low[:, mid:] + got_low[:, mid:].astype(f32))
+    mine[:, :mid] = total[:share]
+    mine[:, mid:cells] = second[:share]
     mine[:, cells:] = part[:share]
     for k, out in enumerate(rest):
         rows = slice((k + 1) * share, (k + 2) * share)
-        out[:, :cells] = total[rows].astype(bf16)
+        out[:, :mid] = total[rows].astype(bf16)
+        out[:, mid:cells] = second[rows].astype(bf16)
         out[:, cells:] = part[rows].astype(bf16)
 
 
-def start_body(pairs, low, got_low, high, got_high, r, p):
-    share, mid = r.shape[0] // pairs, low.shape[1]
+def start_body(k, pairs, v, got, r, p):
+    share = r.shape[0] // pairs
     for b in range(pairs):
         rows = slice(b * share, (b + 1) * share)
-        for v, got, k, columns in ((low, got_low, 3, slice(0, mid)), (high, got_high, 1, slice(mid, 2 * mid))):
-            total = summed(v, got, k, b, share, slice(0, mid))
-            r[rows, columns] = total
-            p[rows, columns] = total.astype(bf16)
-
-
-def update_body(pairs, low, got_low, high, got_high, old, q, r, p, sums):
-    share, mid = r.shape[0] // pairs, low.shape[1]
+        total = summed(v, got, k, b, share, slice(None))
+        r[rows, :] = total
+        p[rows, :] = total.astype(bf16)
+
+
+def update_body(k, pairs, first, v, got, old, *rest):
+    if first:
+        q, r, p, scalars = rest
+    else:
+        scalars, q, r, p = rest
+    share, mid = r.shape[0] // pairs, r.shape[1]
     for b in range(pairs):
         rows = slice(b * share, (b + 1) * share)
-        tail = summed(high, got_high, 1, b, share, slice(mid, None))
-        tail = tail + pltpu.roll(tail, TAIL - 4, 1)
-        if b == 0:
-            sums[...] = tail
+        if first:
+            tail = summed(v, got, k, b, share, slice(mid, None))
+            scalars[rows, :] = tail + pltpu.roll(tail, TAIL - 4, 1)
+        tail = scalars[rows, :]
         alpha = tail[:, 0:1] / tail[:, 1:2]
-        for v, got, k, columns in ((low, got_low, 3, slice(0, mid)), (high, got_high, 1, slice(mid, 2 * mid))):
-            was = old[rows, columns]
-            image = summed(v, got, k, b, share, slice(0, mid)) + damping * was
-            new = was - alpha * image
-            q[rows, columns] = image
-            r[rows, columns] = new
-            p[rows, columns] = new.astype(bf16)
-
-
-def coeff_body(place, rank, bands, cross, pa, pb, *rest):
-    if cross:
-        qa, qb, l, out, norms, p = rest
-    else:
-        l, out, norms, p = rest
-    half = pa.shape[0]
-    p[:half, :] = pa[...]
-    p[half:, :] = pb[...]
+        was = old[rows, :]
+        image = summed(v, got, k, b, share, slice(0, mid)) + damping * was
+        new = was - alpha * image
+        q[rows, :] = image
+        r[rows, :] = new
+        p[rows, :] = new.astype(bf16)
+
+
+def coeff_body(place, rank, bands, cross, *refs):
+    now, old, (l, out, norms, p) = refs[:4], refs[4:-4], refs[-4:]
+    half, mid = now[0].shape
+    lane = lax.broadcasted_iota(jnp.int32, (half, TAIL), 1)
+    for h in range(2):
+        rows = slice(h * half, (h + 1) * half)
+        square = product = 0.0
+        for c in range(2):
+            v = now[2 * h + c][...]
+            p[rows, c * mid:(c + 1) * mid] = v
+            v = v.astype(f32)
+            square = square + jnp.sum(v * v, axis=1, keepdims=True)
+            if cross:
+                product = product + jnp.sum(v * old[2 * h + c][...].astype(f32), axis=1, keepdims=True)
+        col = jnp.where(lane == 0, square * (1.0 / bands), 0.0)
+        if cross:
+            col = jnp.where(lane == 1, product * (1.0 / bands), col)
+        norms[rows, :] = col
     width = l.shape[1]
     step = min(STEP, width)
     for j in range(0, width, step):
         put_blocks(out, dot(p[...], l[:, j:j + step]).astype(bf16).T, j // rank, place, rank)
-    lane = lax.broadcasted_iota(jnp.int32, (half, TAIL), 1)
-    for h, (now, old) in enumerate(((pa, qa), (pb, qb)) if cross else ((pa, None), (pb, None))):
-        v = now[...].astype(f32)
-        col = jnp.where(lane == 0, jnp.sum(v * v, axis=1, keepdims=True) * (1.0 / bands), 0.0)
-        if cross:
-            col = jnp.where(lane == 1, jnp.sum(v * old[...].astype(f32), axis=1, keepdims=True) * (1.0 / bands), col)
-        norms[h * half:(h + 1) * half, :] = col
 
 
 def middle_body(order, place, rank, cross, got, norms, r, *rest):
@@ -230,6 +247,7 @@
     bands, blocks = lax.axis_size(BAND), lax.axis_size(SPACE)
     rank = width // blocks
     share, half, pairs = m // bands, m // 2, bands // 2
+    mid = cells // 2
     order = order_of(blocks)
     place = [order.index(s) for s in range(blocks)]
     me = lax.axis_index(BAND)
@@ -242,28 +260,22 @@
         return lax.ppermute(v, BAND, [(i, i ^ flip) for i in range(bands)])
 
     def adjoint(got, scalars):
-        columns = cells + (TAIL if scalars else 0)
+        wide = mid + (TAIL if scalars else 0)
+        own, oth, natural = call(
+            functools.partial(adjoint_body, order, rank, scalars),
+            [shape((half, wide), f32), shape((half, wide), bf16), shape((width, m), bf16)], [], work // 2, (got, left),
+        )
+        low = own, swap(oth, 1)
         own, oth = call(
-            functools.partial(adjoint_body, order, rank, scalars),
-            [shape((half, columns), f32), shape((half, columns), bf16)],
-            [pltpu.VMEM((width, m), bf16)], work, (got, left),
+            adjoint_second_body, [shape((half, mid), f32), shape((half, mid), bf16)], [], work // 2, (natural, left)
         )
-        return own, swap(oth, 1)
-
-    def along_y(own, got, tail):
-        mid = cells // 2
-        wide = mid + (TAIL if tail else 0)
-        low, high = call(
-            functools.partial(pair_body, cells, tail),
-            [shape((half, mid), bf16), shape((half, wide), bf16)], [], own.size, (own, got),
-        )
-        got_low, got_high = swap(low, 2), swap(high, 6)
-
-        def step(k, v, got):
-            return call(functools.partial(step_body, k, pairs, mid), [shape(v.shape, bf16)], [], v.size, (v, got))[0]
-
-        low, high = step(1, low, got_low), step(3, high, got_high)
-        return low, swap(low, 6), high, swap(high, 2)
+        return low, (own, swap(oth, 1))
+
+    def along_y(k, own, got):
+        v = call(functools.partial(pair_body, mid), [shape(got.shape, bf16)], [], own.size, (own, got))[0]
+        got = swap(v, 2 * k)
+        v = call(functools.partial(step_body, k, pairs, mid), [shape(v.shape, bf16)], [], v.size, (v, got))[0]
+        return v, swap(v, 2 * (4 - k))
 
     def forward(now, old=()):
         coeff, norms = call(
@@ -287,34 +299,43 @@
         [shape((blocks, 2 * rank, half), bf16)], [pltpu.VMEM((m, cells), bf16)], work, (perm, d, right),
         [SMEM, VMEM, VMEM],
     )[0]
-    state = shape((half, cells), f32)
-    parts = along_y(*adjoint(exchange(back), 0), False)
-    r0, p0 = call(
-        functools.partial(start_body, pairs), [state, shape((half, cells), bf16)], [], state.size, parts
-    )
-    p0 = (p0, swap(p0, 1))
+    state, sent = shape((half, mid), f32), shape((half, mid), bf16)
+    ways = (1, 3)
+    r0, p0 = [], []
+    for k, piece in zip(ways, adjoint(exchange(back), 0)):
+        r, p = call(functools.partial(start_body, 4 - k, pairs), [state, sent], [], state.size, along_y(k, *piece))
+        r0.append(r)
+        p0.append(p)
+    p0 += [swap(p, 1) for p in p0]
     got, norms = forward(p0)
     got, s0 = middle(got, norms)
-    parts = along_y(*adjoint(got, 2), True)
-    q0, r1, p1, sums0 = call(
-        functools.partial(update_body, pairs),
-        [state, state, shape((half, cells), bf16), shape((share, TAIL), f32)], [], state.size, (*parts, r0),
+    low, high = adjoint(got, 2)
+    q, r, p, sums0 = call(
+        functools.partial(update_body, 3, pairs, True),
+        [state, state, sent, shape((half, TAIL), f32)], [], state.size, (*along_y(1, *low), r0[0]),
     )
-    p1 = (p1, swap(p1, 1))
+    q0, r1, p1 = [q], [r], [p]
+    q, r, p = call(
+        functools.partial(update_body, 1, pairs, False),
+        [state, state, sent], [], state.size, (*along_y(3, *high), r0[1], sums0),
+    )
+    q0, r1, p1 = q0 + [q], r1 + [r], p1 + [p]
+    p1 += [swap(p, 1) for p in p1]
     got, norms = forward(p1, p0)
     got, _ = middle(got, norms, (s0,))
-    own, got = adjoint(got, 3)
+    low, high = adjoint(got, 3)
     columns = cells + TAIL
     mine, *rest = call(
-        functools.partial(spread_body, cells),
+        spread_body,
         [shape((share, columns), f32)] + [shape((share, columns), bf16)] * (pairs - 1),
-        [], half * columns, (own, got),
+        [], half * columns, (*low, *high),
     )
     total = mine
     for k in range(1, pairs):
         total = total + swap(rest[k - 1], 2 * k).astype(f32)
     sums1 = total[:, cells:cells + 4] + total[:, cells + 4:cells + 8]
-    r0, q0, r1 = r0[:share], q0[:share], r1[:share]
+    r0, q0, r1 = (jnp.concatenate([v[:share] for v in pair], axis=1) for pair in (r0, q0, r1))
+    sums0 = sums0[:share]
     q1 = total[:, :cells] + damping * r1
     rr0, c0 = sums0[:, 0:1], sums0[:, 1:2]
     rr1, n11, n01 = sums1[:, 0:1], sums1[:, 1:2], sums1[:, 2:3]

time: 243 us -> 241 us (level)
  waiting for transfers between devices: 28.7 us -> 22.9 us
  starting transfers between devices: 16 us -> 20 us
    ppermute x16 -> x21, waiting for transfers between devices: 28.7 us -> 22.9 us  [swap(): return lax.ppermute(v, BAND, [(i, i ^ flip) for i in range(bands)])]
    ppermute x16 -> x21, starting transfers between devices: 16 us -> 20 us  [swap(): return lax.ppermute(v, BAND, [(i, i ^ flip) for i in range(bands)])]
    pallas_call x17 -> x24, Pallas kernels: 14.7 us -> 15.5 us  [call(): pl.pallas_call(body, out_shape=outs, in_specs=specs or [VMEM] * len(args)...]
  transfers between devices with their start and end apart: 16 -> 21, of which waited for: 13 -> 13; matrix products, arithmetic and copies ran while one was open for 0% -> 0% of each run, Pallas kernels for 0% -> 1%
where the time goes in v4:
time: 241 us; the launch traced here: 239 us
  blocking collectives  175 us (73%)
  waiting for transfers between devices  22.9 us (10%)
  starting transfers between devices  20 us (8%)
  Pallas kernels  15.5 us (6%)
  local copies, waits for them, and re-layouts  3.36 us (1%)
    all_to_all x5, blocking collectives, exchange(): return lax.all_to_all(v, SPACE, 0, 0, tiled=True, axis_index_groups=[order])  175 us
    ppermute x21, waiting for transfers between devices, swap(): return lax.ppermute(v, BAND, [(i, i ^ flip) for i in range(bands)])  22.9 us
    ppermute x21, starting transfers between devices, swap(): return lax.ppermute(v, BAND, [(i, i ^ flip) for i in range(bands)])  20 us
    pallas_call x24, Pallas kernels, call(): pl.pallas_call(body, out_shape=outs, in_specs=specs or [VMEM] * len(args)...  15.5 us
  transfers between devices with their start and end apart: 21, of which 13 were waited for; matrix products, arithmetic and copies ran while one was open for 0% of the time, Pallas kernels for 1%

profile of v4, /device:TPU:32, one launch (start us, length us, event | category | flops | bytes accessed | tf_op | source)
XLA Modules:
  0.0 239.0 jit_solution(12597680811997122698)
XLA Ops:
  0.7 2.2 copy-done.1
  4.0 1.8 shard_map.50
  5.8 39.5 %all_to_all.25.got = bf16[32,128,128]{2,1,0:T(8,128)(2,1)S(1)} all-to-all(bf16[32,128,128]{2,1,0:T(8,128)(2,1)S(1)} %shard_map.50), channel_id=1, replica_groups={{0,8,16,24,25,17,9,1,2,10,18,26,27,19,11,3,4,12,20,28,29,21,13,5,6,14,2..., dimensions={0} | all-to-all | bytes 2097152 | tf_op jit(solution)/shard_map/all_to_all | solution.py:257
  47.7 1.7 collective-permute-start.1
  49.4 2.4 %collective-permute-start.4 = (bf16[128,512]{1,0:T(8,128)(2,1)S(1)}, bf16[128,512]{1,0:T(8,128)(2,1)S(1)}, u32[]{:S(2)}, u32[]{:S(2)}) collective-permute-start(bf16[128,512]{1,0:T(8,128)(2,1)S(1)} %shard_map.56.v), channel_id=1, source_target_pairs={{0,192},{32,224},{64,128},{96,160},{128,64},{160,96},{192,0},{224,... | collective-permute-start | bytes 393224 | tf_op jit(solution)/shard_map/ppermute | solution.py:260
  51.8 1.5 collective-permute-done.1.got
  53.3 3.1 %collective-permute-start.2 = (bf16[128,512]{1,0:T(8,128)(2,1)S(1)}, bf16[128,512]{1,0:T(8,128)(2,1)S(1)}, u32[]{:S(2)}, u32[]{:S(2)}) collective-permute-start(bf16[128,512]{1,0:T(8,128)(2,1)S(1)} %shard_map.53.v), channel_id=1, source_target_pairs={{0,192},{32,224},{64,128},{96,160},{128,64},{160,96},{192,0},{224,... | collective-permute-start | bytes 393224 | tf_op jit(solution)/shard_map/ppermute | solution.py:260
  56.7 2.9 %collective-permute-done.2.got = bf16[128,512]{1,0:T(8,128)(2,1)S(1)} collective-permute-done((bf16[128,512]{1,0:T(8,128)(2,1)S(1)}, bf16[128,512]{1,0:T(8,128)(2,1)S(1)}, u32[]{:S(2)}, u32[]{:S(2)}) %collective-permute-start.2) | collective-permute-done | bytes 131104 | tf_op jit(solution)/shard_map/ppermute | solution.py:260
  59.7 1.8 collective-permute-done.5.got
  61.7 1.3 collective-permute-done.7.refs_3_.refs_7_
  64.3 33.2 %all_to_all.26.got = bf16[32,128,128]{2,1,0:T(8,128)(2,1)S(1)} all-to-all(bf16[32,128,128]{2,1,0:T(8,128)(2,1)S(1)} %get-tuple-element.46), channel_id=1, replica_groups={{0,8,16,24,25,17,9,1,2,10,18,26,27,19,11,3,4,12,20,28,29,21,13,5,6,14,2..., dimensions={0} | all-to-all | bytes 2097152 | tf_op jit(solution)/shard_map/all_to_all | solution.py:257
  97.5 2.4 %shard_map.60 = (bf16[32,136,128]{2,1,0:T(8,128)(2,1)S(1)}, bf16[256,1024]{1,0:T(8,128)(2,1)S(1)}) custom-call(bf16[32,128,128]{2,1,0:T(8,128)(2,1)S(1)} %all_to_all.26.got, f32[256,128]{1,0:T(8,128)S(1)} %get-tuple-element.47.norms, bf16[2048,1024]{1,0:T(8,128)(2,1)S(1)} %bitcast.20), custom_call_target="tpu_custom_call" | custom-call | flops 2147483648 | bytes 7012352 | tf_op jit(solution)/shard_map/pallas_call | solution.py:33
  99.9 34.8 %all_to_all.27.got = bf16[32,136,128]{2,1,0:T(8,128)(2,1)S(1)} all-to-all(bf16[32,136,128]{2,1,0:T(8,128)(2,1)S(1)} %get-tuple-element.48), channel_id=1, replica_groups={{0,8,16,24,25,17,9,1,2,10,18,26,27,19,11,3,4,12,20,28,29,21,13,5,6,14,2..., dimensions={0} | all-to-all | bytes 2228224 | tf_op jit(solution)/shard_map/all_to_all | solution.py:257
  138.3 2.4 %collective-permute-start.12 = (bf16[128,512]{1,0:T(8,128)(2,1)S(1)}, bf16[128,512]{1,0:T(8,128)(2,1)S(1)}, u32[]{:S(2)}, u32[]{:S(2)}) collective-permute-start(bf16[128,512]{1,0:T(8,128)(2,1)S(1)} %shard_map.66.v), channel_id=1, source_target_pairs={{0,192},{32,224},{64,128},{96,160},{128,64},{160,96},{192,0},{224,... | collective-permute-start | bytes 393224 | tf_op jit(solution)/shard_map/ppermute | solution.py:260
  140.7 3.0 %collective-permute-done.9.got = bf16[128,640]{1,0:T(8,128)(2,1)S(1)} collective-permute-done((bf16[128,640]{1,0:T(8,128)(2,1)S(1)}, bf16[128,640]{1,0:T(8,128)(2,1)S(1)}, u32[]{:S(2)}, u32[]{:S(2)}) %collective-permute-start.9) | collective-permute-done | bytes 163872 | tf_op jit(solution)/shard_map/ppermute | solution.py:260
  143.9 2.4 %collective-permute-start.10 = (bf16[128,640]{1,0:T(8,128)(2,1)S(1)}, bf16[128,640]{1,0:T(8,128)(2,1)S(1)}, u32[]{:S(2)}, u32[]{:S(2)}) collective-permute-start(bf16[128,640]{1,0:T(8,128)(2,1)S(1)} %shard_map.63.v), channel_id=1, source_target_pairs={{0,192},{32,224},{64,128},{96,160},{128,64},{160,96},{192,0},{224,... | collective-permute-start | bytes 491528 | tf_op jit(solution)/shard_map/ppermute | solution.py:260
  146.5 4.1 %collective-permute-done.10.got = bf16[128,640]{1,0:T(8,128)(2,1)S(1)} collective-permute-done((bf16[128,640]{1,0:T(8,128)(2,1)S(1)}, bf16[128,640]{1,0:T(8,128)(2,1)S(1)}, u32[]{:S(2)}, u32[]{:S(2)}) %collective-permute-start.10) | collective-permute-done | bytes 163872 | tf_op jit(solution)/shard_map/ppermute | solution.py:260
  153.1 1.3 shard_map.69
  154.4 33.0 %all_to_all.28.got = bf16[32,128,128]{2,1,0:T(8,128)(2,1)S(1)} all-to-all(bf16[32,128,128]{2,1,0:T(8,128)(2,1)S(1)} %get-tuple-element.59), channel_id=1, replica_groups={{0,8,16,24,25,17,9,1,2,10,18,26,27,19,11,3,4,12,20,28,29,21,13,5,6,14,2..., dimensions={0} | all-to-all | bytes 2097152 | tf_op jit(solution)/shard_map/all_to_all | solution.py:257
  187.4 2.5 %shard_map.70 = (bf16[32,136,128]{2,1,0:T(8,128)(2,1)S(1)}, bf16[256,1024]{1,0:T(8,128)(2,1)}) custom-call(bf16[32,128,128]{2,1,0:T(8,128)(2,1)S(1)} %all_to_all.28.got, f32[256,128]{1,0:T(8,128)S(1)} %get-tuple-element.60.norms, bf16[2048,1024]{1,0:T(8,128)(2,1)S(1)} %bitcast.21, bf16[256,1024]{1,0:T(8,128)(2,1)S(1)} %get-tuple-element.61.rest_0_), custom_call_target="tpu_custom_call" | custom-call | flops 2147483648 | bytes 7536640 | tf_op jit(solution)/shard_map/pallas_call | solution.py:33
  189.9 34.7 %all_to_all.29.got = bf16[32,136,128]{2,1,0:T(8,128)(2,1)S(1)} all-to-all(bf16[32,136,128]{2,1,0:T(8,128)(2,1)S(1)} %get-tuple-element.62), channel_id=1, replica_groups={{0,8,16,24,25,17,9,1,2,10,18,26,27,19,11,3,4,12,20,28,29,21,13,5,6,14,2..., dimensions={0} | all-to-all | bytes 2228224 | tf_op jit(solution)/shard_map/all_to_all | solution.py:257
  228.2 4.0 %collective-permute-start.19 = (bf16[32,1152]{1,0:T(8,128)(2,1)S(1)}, bf16[32,1152]{1,0:T(8,128)(2,1)S(1)}, u32[]{:S(2)}, u32[]{:S(2)}) collective-permute-start(bf16[32,1152]{1,0:T(8,128)(2,1)S(1)} %get-tuple-element.70), channel_id=1, source_target_pairs={{0,128},{32,160},{64,192},{96,224},{128,0},{160,32},{192,64},{224,... | collective-permute-start | bytes 221192 | tf_op jit(solution)/shard_map/ppermute | solution.py:260
  233.0 3.3 %collective-permute-done.19 = bf16[32,1152]{1,0:T(8,128)(2,1)S(1)} collective-permute-done((bf16[32,1152]{1,0:T(8,128)(2,1)S(1)}, bf16[32,1152]{1,0:T(8,128)(2,1)S(1)}, u32[]{:S(2)}, u32[]{:S(2)}) %collective-permute-start.19) | collective-permute-done | bytes 73760 | tf_op jit(solution)/shard_map/ppermute | solution.py:260
  236.3 1.5 collective-permute-done.20
  (66 shorter events, 17.2 us)
Async XLA Ops:
  0.7 2.2 copy-start.1
  4.0 41.4 %copy-start = (bf16[1,1024,2048]{2,1,0:T(8,128)(2,1)S(1)}, bf16[1,1024,2048]{2,1,0:T(8,128)(2,1)}, u32[]{:S(2)}) copy-start(bf16[1,1024,2048]{2,1,0:T(8,128)(2,1)} %param.3) | copy-start | bytes 12582916
  46.2 1.5 collective-permute-start
  47.1 2.3 collective-permute-start.3
  47.7 5.6 %collective-permute-start.1 = (bf16[128,512]{1,0:T(8,128)(2,1)S(1)}, bf16[128,512]{1,0:T(8,128)(2,1)S(1)}, u32[]{:S(2)}, u32[]{:S(2)}) collective-permute-start(bf16[128,512]{1,0:T(8,128)(2,1)S(1)} %shard_map.52.v), channel_id=1, source_target_pairs={{0,64},{32,96},{64,0},{96,32},{128,192},{160,224},{192,128},{224,1... | collective-permute-start | bytes 393224 | tf_op jit(solution)/shard_map/ppermute | solution.py:260
  49.4 7.0 %collective-permute-start.4 = (bf16[128,512]{1,0:T(8,128)(2,1)S(1)}, bf16[128,512]{1,0:T(8,128)(2,1)S(1)}, u32[]{:S(2)}, u32[]{:S(2)}) collective-permute-start(bf16[128,512]{1,0:T(8,128)(2,1)S(1)} %shard_map.56.v), channel_id=1, source_target_pairs={{0,192},{32,224},{64,128},{96,160},{128,64},{160,96},{192,0},{224,... | collective-permute-start | bytes 393224 | tf_op jit(solution)/shard_map/ppermute | solution.py:260
  53.3 6.3 %collective-permute-start.2 = (bf16[128,512]{1,0:T(8,128)(2,1)S(1)}, bf16[128,512]{1,0:T(8,128)(2,1)S(1)}, u32[]{:S(2)}, u32[]{:S(2)}) collective-permute-start(bf16[128,512]{1,0:T(8,128)(2,1)S(1)} %shard_map.53.v), channel_id=1, source_target_pairs={{0,192},{32,224},{64,128},{96,160},{128,64},{160,96},{192,0},{224,... | collective-permute-start | bytes 393224 | tf_op jit(solution)/shard_map/ppermute | solution.py:260
  56.5 5.1 %collective-permute-start.5 = (bf16[128,512]{1,0:T(8,128)(2,1)S(1)}, bf16[128,512]{1,0:T(8,128)(2,1)S(1)}, u32[]{:S(2)}, u32[]{:S(2)}) collective-permute-start(bf16[128,512]{1,0:T(8,128)(2,1)S(1)} %shard_map.57.v), channel_id=1, source_target_pairs={{0,64},{32,96},{64,0},{96,32},{128,192},{160,224},{192,128},{224,1... | collective-permute-start | bytes 393224 | tf_op jit(solution)/shard_map/ppermute | solution.py:260
  59.6 2.0 collective-permute-start.6
  61.6 1.4 collective-permute-start.7
  63.0 34.5 %copy-start.2 = (bf16[1,2048,1024]{2,1,0:T(8,128)(2,1)S(1)}, bf16[1,2048,1024]{2,1,0:T(8,128)(2,1)}, u32[]{:S(2)}) copy-start(bf16[1,2048,1024]{2,1,0:T(8,128)(2,1)} %param.4) | copy-start | bytes 12582916
  135.6 1.7 collective-permute-start.8
  136.7 1.6 collective-permute-start.11
  137.4 6.3 %collective-permute-start.9 = (bf16[128,640]{1,0:T(8,128)(2,1)S(1)}, bf16[128,640]{1,0:T(8,128)(2,1)S(1)}, u32[]{:S(2)}, u32[]{:S(2)}) collective-permute-start(bf16[128,640]{1,0:T(8,128)(2,1)S(1)} %shard_map.62.v), channel_id=1, source_target_pairs={{0,64},{32,96},{64,0},{96,32},{128,192},{160,224},{192,128},{224,1... | collective-permute-start | bytes 491528 | tf_op jit(solution)/shard_map/ppermute | solution.py:260
  138.3 8.1 %collective-permute-start.12 = (bf16[128,512]{1,0:T(8,128)(2,1)S(1)}, bf16[128,512]{1,0:T(8,128)(2,1)S(1)}, u32[]{:S(2)}, u32[]{:S(2)}) collective-permute-start(bf16[128,512]{1,0:T(8,128)(2,1)S(1)} %shard_map.66.v), channel_id=1, source_target_pairs={{0,192},{32,224},{64,128},{96,160},{128,64},{160,96},{192,0},{224,... | collective-permute-start | bytes 393224 | tf_op jit(solution)/shard_map/ppermute | solution.py:260
  143.9 6.7 %collective-permute-start.10 = (bf16[128,640]{1,0:T(8,128)(2,1)S(1)}, bf16[128,640]{1,0:T(8,128)(2,1)S(1)}, u32[]{:S(2)}, u32[]{:S(2)}) collective-permute-start(bf16[128,640]{1,0:T(8,128)(2,1)S(1)} %shard_map.63.v), channel_id=1, source_target_pairs={{0,192},{32,224},{64,128},{96,160},{128,64},{160,96},{192,0},{224,... | collective-permute-start | bytes 491528 | tf_op jit(solution)/shard_map/ppermute | solution.py:260
  146.4 5.1 %collective-permute-start.13 = (bf16[128,512]{1,0:T(8,128)(2,1)S(1)}, bf16[128,512]{1,0:T(8,128)(2,1)S(1)}, u32[]{:S(2)}, u32[]{:S(2)}) collective-permute-start(bf16[128,512]{1,0:T(8,128)(2,1)S(1)} %shard_map.67.v), channel_id=1, source_target_pairs={{0,64},{32,96},{64,0},{96,32},{128,192},{160,224},{192,128},{224,1... | collective-permute-start | bytes 393224 | tf_op jit(solution)/shard_map/ppermute | solution.py:260
  150.9 1.4 collective-permute-start.14
  151.6 1.4 collective-permute-start.15
  225.4 2.5 %collective-permute-start.16 = (bf16[128,640]{1,0:T(8,128)(2,1)S(1)}, bf16[128,640]{1,0:T(8,128)(2,1)S(1)}, u32[]{:S(2)}, u32[]{:S(2)}) collective-permute-start(bf16[128,640]{1,0:T(8,128)(2,1)S(1)} %get-tuple-element.64), channel_id=1, source_target_pairs={{0,32},{32,0},{64,96},{96,64},{128,160},{160,128},{192,224},{224,1... | collective-permute-start | bytes 491528 | tf_op jit(solution)/shard_map/ppermute | solution.py:260
  226.4 1.6 collective-permute-start.17
  228.1 4.9 %collective-permute-start.18 = (bf16[32,1152]{1,0:T(8,128)(2,1)S(1)}, bf16[32,1152]{1,0:T(8,128)(2,1)S(1)}, u32[]{:S(2)}, u32[]{:S(2)}) collective-permute-start(bf16[32,1152]{1,0:T(8,128)(2,1)S(1)} %get-tuple-element.69), channel_id=1, source_target_pairs={{0,64},{32,96},{64,0},{96,32},{128,192},{160,224},{192,128},{224,1... | collective-permute-start | bytes 221192 | tf_op jit(solution)/shard_map/ppermute | solution.py:260
  228.2 8.1 %collective-permute-start.19 = (bf16[32,1152]{1,0:T(8,128)(2,1)S(1)}, bf16[32,1152]{1,0:T(8,128)(2,1)S(1)}, u32[]{:S(2)}, u32[]{:S(2)}) collective-permute-start(bf16[32,1152]{1,0:T(8,128)(2,1)S(1)} %get-tuple-element.70), channel_id=1, source_target_pairs={{0,128},{32,160},{64,192},{96,224},{128,0},{160,32},{192,64},{224,... | collective-permute-start | bytes 221192 | tf_op jit(solution)/shard_map/ppermute | solution.py:260
  232.2 5.7 %collective-permute-start.20 = (bf16[32,1152]{1,0:T(8,128)(2,1)S(1)}, bf16[32,1152]{1,0:T(8,128)(2,1)S(1)}, u32[]{:S(2)}, u32[]{:S(2)}) collective-permute-start(bf16[32,1152]{1,0:T(8,128)(2,1)S(1)} %get-tuple-element.71), channel_id=1, source_target_pairs={{0,192},{32,224},{64,128},{96,160},{128,64},{160,96},{192,0},{224,... | collective-permute-start | bytes 221192 | tf_op jit(solution)/shard_map/ppermute | solution.py:260
  (1 other events, 1.0 us)

commit v5 on v4

v5 whole, which is shorter than its diff:
```python
import functools
import jax
import jax.numpy as jnp
from jax import lax
from jax.experimental import pallas as pl
from jax.experimental.pallas import tpu as pltpu
from jax.sharding import PartitionSpec as P

damping = 1.0
BAND = "band"
SPACE = "space"
f32, bf16 = jnp.float32, jnp.bfloat16
EXTRA = 8
TAIL = 128
STEP = 256

VMEM = pl.BlockSpec(memory_space=pltpu.VMEM)
ANY = pl.BlockSpec(memory_space=pl.ANY)
SMEM = pl.BlockSpec(memory_space=pltpu.SMEM)


def order_of(blocks):
    if blocks != 32:
        return list(range(blocks))
    return [(x if z % 2 == 0 else 3 - x) * 8 + z for z in range(8) for x in range(4)]


def dot(a, b, dims=((1,), (0,))):
    return lax.dot_general(a, b, (dims, ((), ())), preferred_element_type=f32)


def call(body, outs, scratch, flops, args, specs=None):
    moved = sum(a.size * a.dtype.itemsize for a in args) + sum(o.size * o.dtype.itemsize for o in outs)
    return pl.pallas_call(
        body,
        out_shape=outs,
        in_specs=specs or [VMEM] * len(args),
        out_specs=[VMEM] * len(outs),
        scratch_shapes=scratch,
        cost_estimate=pl.CostEstimate(flops=flops, bytes_accessed=moved, transcendentals=0),
        compiler_params=pltpu.CompilerParams(vmem_limit_bytes=24 * 1024 * 1024),
    )(*args)


def shape(dims, kind):
    return jax.ShapeDtypeStruct(dims, kind)


def bring_body(a, out, sem):
    copy = pltpu.make_async_copy(a, out, sem)
    copy.start()
    copy.wait()


def put_blocks(out, rows, first, place, rank):
    half = rows.shape[1] // 2
    for i in range(rows.shape[0] // rank):
        block = rows[i * rank:(i + 1) * rank]
        out[place[first + i], :rank, :] = block[:, :half]
        out[place[first + i], rank:2 * rank, :] = block[:, half:]


def take_blocks(got, natural, order, rank):
    half = got.shape[2]
    for q, s in enumerate(order):
        natural[s * rank:(s + 1) * rank, :half] = got[q, :rank, :]
        natural[s * rank:(s + 1) * rank, half:] = got[q, rank:2 * rank, :]


def put_band(out, rows, first, place, rank, band):
    for i in range(rows.shape[0] // rank):
        out[place[first + i], band * rank:(band + 1) * rank, :] = rows[i * rank:(i + 1) * rank]


def take_band(got, natural, order, rank, band):
    width = len(order) * rank
    for q, s in enumerate(order):
        natural[band * width + s * rank:band * width + (s + 1) * rank, :] = got[q, band * rank:(band + 1) * rank, :]


def first_body(place, rank, share, perm, d, r, out, dp):
    for k in range(d.shape[0] // share):
        dp[k * share:(k + 1) * share, :] = d[pl.ds(pl.multiple_of(perm[k] * share, share), share), :]
    step = min(STEP, r.shape[0])
    for j in range(0, r.shape[0], step):
        put_blocks(out, dot(r[j:j + step, :], dp[...], ((1,), (1,))).astype(bf16), j // rank, place, rank)


def adjoint_body(order, rank, got, l, own, oth, natural):
    take_blocks(got, natural, order, rank)
    adjoint_rows(natural, l, 0, l.shape[0] // 2, own, oth)


def adjoint_rows(natural, l, begin, end, own, oth):
    half = own.shape[0]
    step = min(STEP, end - begin)
    for j in range(begin, end, step):
        t = dot(l[j:j + step, :], natural[...]).T
        columns = slice(j - begin, j - begin + step)
        own[:, columns] = t[:half]
        oth[:, columns] = t[half:].astype(bf16)


def adjoint_second_body(natural, l, own, oth):
    adjoint_rows(natural, l, l.shape[0] // 2, l.shape[0], own, oth)


def both_rows(natural, l, other, begin, end, out):
    width = l.shape[1]
    step = min(STEP, end - begin)
    for j in range(begin, end, step):
        t = dot(l[j:j + step, :], natural[:width, :]) + dot(other[j:j + step, :], natural[width:, :])
        out[:, j - begin:j - begin + step] = t.T.astype(out.dtype)


def both_body(order, rank, got, l, other, out, natural):
    for band in range(2):
        take_band(got, natural, order, rank, band)
    mid = l.shape[0] // 2
    both_rows(natural, l, other, 0, mid, out)
    rows = got[0, 2 * rank:, :].astype(f32)
    for q in range(1, len(order)):
        rows = rows + got[q, 2 * rank:, :].astype(f32)
    rows = rows[:4] + rows[4:]
    high = rows.astype(bf16).astype(f32)
    t = jnp.concatenate([high, rows - high, jnp.zeros((TAIL - 8, rows.shape[1]), f32)], axis=0).T
    out[:, mid:] = t.astype(out.dtype)


def both_second_body(natural, l, other, out):
    both_rows(natural, l, other, l.shape[0] // 2, l.shape[0], out)


def resplit(part):
    lane = lax.broadcasted_iota(jnp.int32, part.shape, 1)
    both = part + pltpu.roll(part, TAIL - 4, 1)
    high = both.astype(bf16).astype(f32)
    return jnp.where(lane < 4, high, jnp.where(lane < 8, pltpu.roll(both - high, 4, 1), 0.0))


def pair_body(mid, own, got, out):
    out[:, :mid] = (own[:, :mid] + got[:, :mid].astype(f32)).astype(bf16)
    if own.shape[1] > mid:
        out[:, mid:] = resplit(own[:, mid:] + got[:, mid:].astype(f32)).astype(bf16)


def summed(v, got, k, b, share, columns):
    rows, far = slice(b * share, (b + 1) * share), slice((b ^ k) * share, ((b ^ k) + 1) * share)
    return v[rows, columns].astype(f32) + got[far, columns].astype(f32)


def step_body(k, pairs, cells, v, got, out):
    share = v.shape[0] // pairs
    for b in range(pairs):
        rows = slice(b * share, (b + 1) * share)
        out[rows, :cells] = summed(v, got, k, b, share, slice(0, cells)).astype(bf16)
        if v.shape[1] > cells:
            out[rows, cells:] = resplit(summed(v, got, k, b, share, slice(cells, None))).astype(bf16)


def spread_body(low, high, mine, *rest):
    share, mid = mine.shape[0], high.shape[1]
    cells = 2 * mid
    for k, out in enumerate((mine, *rest)):
        rows = slice(k * share, (k + 1) * share)
        out[:, :mid] = low[rows, :mid].astype(out.dtype)
        out[:, mid:cells] = high[rows, :].astype(out.dtype)
        out[:, cells:] = low[rows, mid:].astype(out.dtype)


def start_body(k, pairs, v, got, r, p):
    share = r.shape[0] // pairs
    for b in range(pairs):
        rows = slice(b * share, (b + 1) * share)
        total = summed(v, got, k, b, share, slice(None))
        r[rows, :] = total
        p[rows, :] = total.astype(bf16)


def update_body(k, pairs, first, v, got, old, *rest):
    if first:
        q, r, p, scalars = rest
    else:
        scalars, q, r, p = rest
    share, mid = r.shape[0] // pairs, r.shape[1]
    for b in range(pairs):
        rows = slice(b * share, (b + 1) * share)
        if first:
            tail = summed(v, got, k, b, share, slice(mid, None))
            scalars[rows, :] = tail + pltpu.roll(tail, TAIL - 4, 1)
        tail = scalars[rows, :]
        alpha = tail[:, 0:1] / tail[:, 1:2]
        was = old[rows, :]
        image = summed(v, got, k, b, share, slice(0, mid)) + damping * was
        new = was - alpha * image
        q[rows, :] = image
        r[rows, :] = new
        p[rows, :] = new.astype(bf16)


def coeff_body(place, rank, copies, cross, *refs):
    now, old, (l, other, out, norms, p) = refs[:2], refs[2:-5], refs[-5:]
    half, mid = now[0].shape
    lane = lax.broadcasted_iota(jnp.int32, (half, TAIL), 1)
    square = product = 0.0
    for c in range(2):
        v = now[c][...]
        p[:, c * mid:(c + 1) * mid] = v
        v = v.astype(f32)
        square = square + jnp.sum(v * v, axis=1, keepdims=True)
        if cross:
            product = product + jnp.sum(v * old[c][...].astype(f32), axis=1, keepdims=True)
    col = jnp.where(lane == 0, square * (1.0 / copies), 0.0)
    if cross:
        col = jnp.where(lane == 1, product * (1.0 / copies), col)
    norms[...] = col
    width = l.shape[1]
    step = min(STEP, width)
    for band, factor in enumerate((l, other)):
        for j in range(0, width, step):
            put_band(out, dot(p[...], factor[:, j:j + step]).astype(bf16).T, j // rank, place, rank, band)


def middle_body(order, place, rank, cross, got, norms, r, other, *rest):
    if cross:
        old, out, seen, natural, turned = rest
    else:
        out, seen, natural, turned = rest
    width, cells = r.shape
    half = got.shape[2]
    square = product = 0.0
    for band, factor in enumerate((r, other)):
        take_band(got, natural, order, rank, band)
        images = slice(band * half, (band + 1) * half)
        step = min(STEP, width)
        for j in range(0, width, step):
            turned[images, j:j + step] = natural[band * width + j:band * width + j + step, :].T
        step = min(STEP, cells)
        for j in range(0, cells, step):
            s = dot(turned[images, :], factor[:, j:j + step])
            seen[images, j:j + step] = s.astype(bf16)
            square = square + jnp.sum(s * s, axis=1, keepdims=True)
            if cross:
                product = product + jnp.sum(s * old[images, j:j + step].astype(f32), axis=1, keepdims=True)
        step = min(STEP, width)
        for j in range(0, width, step):
            back = dot(factor[j:j + step, :], seen[images, :], ((1,), (1,))).astype(bf16)
            put_band(out, back, j // rank, place, rank, band)
    tile = norms[...]
    lane = lax.broadcasted_iota(jnp.int32, tile.shape, 1)
    pp, px = tile[:, 0:1], tile[:, 1:2]
    cols = jnp.where(lane == 0, pp, jnp.where(lane == 1, square + damping * pp, 0.0))
    if cross:
        cols = jnp.where(lane == 2, product + damping * px, cols)
    rows = cols.T[:4]
    high = rows.astype(bf16).astype(f32)
    rows = jnp.concatenate([high, rows - high], axis=0).astype(bf16)
    for q in range(len(order)):
        out[q, 2 * rank:, :] = rows


def per_device(left_factor, right_factor, data):
    left, right, d = left_factor[0], right_factor[0], data[0]
    m, cells = d.shape
    width = left.shape[1]
    bands, blocks = lax.axis_size(BAND), lax.axis_size(SPACE)
    rank = width // blocks
    share, half, pairs = m // bands, m // 2, bands // 2
    mid = cells // 2
    order = order_of(blocks)
    place = [order.index(s) for s in range(blocks)]
    me = lax.axis_index(BAND)
    work = 2 * m * cells * width

    def exchange(v):
        return lax.all_to_all(v, SPACE, 0, 0, tiled=True, axis_index_groups=[order])

    def swap(v, flip):
        return lax.ppermute(v, BAND, [(i, i ^ flip) for i in range(bands)])

    left_other, right_other = swap(left, 1), swap(right, 1)

    def adjoint(got):
        own, oth, natural = call(
            functools.partial(adjoint_body, order, rank),
            [shape((half, mid), f32), shape((half, mid), bf16), shape((width, m), bf16)], [], work // 2, (got, left),
        )
        low = own, swap(oth, 1)
        own, oth = call(
            adjoint_second_body, [shape((half, mid), f32), shape((half, mid), bf16)], [], work // 2, (natural, left)
        )
        return [
            call(functools.partial(pair_body, mid), [shape((half, mid), bf16)], [], half * mid, piece)[0]
            for piece in (low, (own, swap(oth, 1)))
        ]

    def adjoint_both(got, kind):
        low, natural = call(
            functools.partial(both_body, order, rank),
            [shape((half, mid + TAIL), kind), shape((2 * width, half), bf16)], [], work // 2, (got, left, left_other),
        )
        high = call(both_second_body, [shape((half, mid), kind)], [], work // 2, (natural, left, left_other))[0]
        return low, high

    def along_y(k, v):
        got = swap(v, 2 * k)
        v = call(functools.partial(step_body, k, pairs, mid), [shape(v.shape, bf16)], [], v.size, (v, got))[0]
        return v, swap(v, 2 * (4 - k))

    def forward(now, old=()):
        coeff, norms = call(
            functools.partial(coeff_body, place, rank, pairs, bool(old)),
            [shape((blocks, 2 * rank, half), bf16), shape((half, TAIL), f32)],
            [pltpu.VMEM((half, cells), bf16)], work, (*now, *old, left, left_other),
        )
        return exchange(coeff), norms

    def middle(got, norms, old=()):
        out, seen = call(
            functools.partial(middle_body, order, place, rank, bool(old)),
            [shape((blocks, 2 * rank + EXTRA, half), bf16), shape((m, cells), bf16)],
            [pltpu.VMEM((2 * width, half), bf16), pltpu.VMEM((m, width), bf16)], 2 * work,
            (got, norms, right, right_other, *old),
        )
        return exchange(out), seen

    perm = jnp.stack([me ^ (2 * y + c) for c in range(2) for y in range(pairs)]).astype(jnp.int32)
    back = call(
        functools.partial(first_body, place, rank, share),
        [shape((blocks, 2 * rank, half), bf16)], [pltpu.VMEM((m, cells), bf16)], work, (perm, d, right),
        [SMEM, VMEM, VMEM],
    )[0]
    state, sent = shape((half, mid), f32), shape((half, mid), bf16)
    ways = (1, 3)
    r0, p0 = [], []
    got, left_other, right_other = lax.optimization_barrier((exchange(back), left_other, right_other))
    left_other, right_other = (
        call(bring_body, [shape(v.shape, bf16)], [pltpu.SemaphoreType.DMA], 0, (v,), [ANY])[0]
        for v in (left_other, right_other)
    )
    for k, piece in zip(ways, adjoint(got)):
        r, p = call(functools.partial(start_body, 4 - k, pairs), [state, sent], [], state.size, along_y(k, piece))
        r0.append(r)
        p0.append(p)
    p0, left_other, right_other = lax.optimization_barrier((p0, left_other, right_other))
    got, norms = forward(p0)
    got, s0 = middle(got, norms)
    low, high = adjoint_both(got, bf16)
    q, r, p, sums0 = call(
        functools.partial(update_body, 3, pairs, True),
        [state, state, sent, shape((half, TAIL), f32)], [], state.size, (*along_y(1, low), r0[0]),
    )
    q0, r1, p1 = [q], [r], [p]
    q, r, p = call(
        functools.partial(update_body, 1, pairs, False),
        [state, state, sent], [], state.size, (*along_y(3, high), r0[1], sums0),
    )
    q0, r1, p1 = q0 + [q], r1 + [r], p1 + [p]
    got, norms = forward(p1, p0)
    got, _ = middle(got, norms, (s0,))
    low, high = adjoint_both(got, f32)
    columns = cells + TAIL
    mine, *rest = call(
        spread_body,
        [shape((share, columns), f32)] + [shape((share, columns), bf16)] * (pairs - 1),
        [], half * columns, (low, high),
    )
    total = mine
    for k in range(1, pairs):
        total = total + swap(rest[k - 1], 2 * k).astype(f32)
    sums1 = total[:, cells:cells + 4] + total[:, cells + 4:cells + 8]
    r0, q0, r1 = (jnp.concatenate([v[:share] for v in pair], axis=1) for pair in (r0, q0, r1))
    sums0 = sums0[:share]
    q1 = total[:, :cells] + damping * r1
    rr0, c0 = sums0[:, 0:1], sums0[:, 1:2]
    rr1, n11, n01 = sums1[:, 0:1], sums1[:, 1:2], sums1[:, 2:3]
    a0, b0 = rr0 / c0, rr1 / rr0
    a1 = rr1 / (n11 + 2 * b0 * n01 + b0 * b0 * c0)
    return a0 * r0 + a1 * (r1 + b0 * r0), r1 - a1 * (q1 + b0 * q0)


def solution(mesh):
    return jax.shard_map(
        per_device,
        mesh=mesh,
        in_specs=(P("band", "space", None), P("band", None, "space"), P("band", None, "space")),
        out_specs=(P("band", "space"), P("band", "space")),
        check_vma=False,
    )
```

time: 241 us -> 231 us (0.959)
  Pallas kernels: 15.5 us -> 24.4 us
  blocking collectives: 175 us -> 168 us
  waiting for transfers between devices: 22.9 us -> 16.8 us
  starting transfers between devices: 20 us -> 15 us
    pallas_call x24, Pallas kernels: 15.5 us -> 24.4 us  [call(): pl.pallas_call(body, out_shape=outs, in_specs=specs or [VMEM] * len(args)...]
    all_to_all x5, blocking collectives: 175 us -> 168 us  [exchange(): return lax.all_to_all(v, SPACE, 0, 0, tiled=True, axis_index_groups=[order])]
    ppermute x21 -> x15, waiting for transfers between devices: 22.9 us -> 16.8 us  [swap(): return lax.ppermute(v, BAND, [(i, i ^ flip) for i in range(bands)])]
    ppermute x21 -> x15, starting transfers between devices: 20 us -> 15 us  [swap(): return lax.ppermute(v, BAND, [(i, i ^ flip) for i in range(bands)])]
  transfers between devices with their start and end apart: 21 -> 15, of which waited for: 13 -> 10; matrix products, arithmetic and copies ran while one was open for 0% -> 0% of each run, Pallas kernels for 1% -> 4%
where the time goes in v5:
time: 231 us; the launch traced here: 230 us
  blocking collectives  168 us (73%)
  Pallas kernels  24.4 us (11%)
  waiting for transfers between devices  16.8 us (7%)
  starting transfers between devices  15 us (6%)
  local copies, waits for them, and re-layouts  3.69 us (2%)
    all_to_all x5, blocking collectives, exchange(): return lax.all_to_all(v, SPACE, 0, 0, tiled=True, axis_index_groups=[order])  168 us
    pallas_call x24, Pallas kernels, call(): pl.pallas_call(body, out_shape=outs, in_specs=specs or [VMEM] * len(args)...  24.4 us
    ppermute x15, waiting for transfers between devices, swap(): return lax.ppermute(v, BAND, [(i, i ^ flip) for i in range(bands)])  16.8 us
    ppermute x15, starting transfers between devices, swap(): return lax.ppermute(v, BAND, [(i, i ^ flip) for i in range(bands)])  15 us
  transfers between devices with their start and end apart: 15, of which 10 were waited for; matrix products, arithmetic and copies ran while one was open for 0% of the time, Pallas kernels for 4%

profile of v5, /device:TPU:32, one launch (start us, length us, event | category | flops | bytes accessed | tf_op | source)
XLA Modules:
  0.0 229.8 jit_solution(1156898945027976480)
XLA Ops:
  1.3 2.3 %copy-done.1 = bf16[1,2048,1024]{2,1,0:T(8,128)(2,1)S(1)} copy-done((bf16[1,2048,1024]{2,1,0:T(8,128)(2,1)S(1)}, bf16[1,2048,1024]{2,1,0:T(8,128)(2,1)}, u32[]{:S(2)}) %copy-start.1) | copy-done | bytes 4194328
  4.9 1.8 shard_map.50
  6.7 39.9 %all_to_all.25.got = bf16[32,128,128]{2,1,0:T(8,128)(2,1)S(1)} all-to-all(bf16[32,128,128]{2,1,0:T(8,128)(2,1)S(1)} %shard_map.50), channel_id=1, replica_groups={{0,8,16,24,25,17,9,1,2,10,18,26,27,19,11,3,4,12,20,28,29,21,13,5,6,14,2..., dimensions={0} | all-to-all | bytes 2097152 | tf_op jit(solution)/shard_map/all_to_all | solution.py:276
  49.7 3.1 %collective-permute-start.6 = (bf16[128,512]{1,0:T(8,128)(2,1)S(1)}, bf16[128,512]{1,0:T(8,128)(2,1)S(1)}, u32[]{:S(2)}, u32[]{:S(2)}) collective-permute-start(bf16[128,512]{1,0:T(8,128)(2,1)S(1)} %shard_map.56.v), channel_id=1, source_target_pairs={{0,192},{32,224},{64,128},{96,160},{128,64},{160,96},{192,0},{224,... | collective-permute-start | bytes 393224 | tf_op jit(solution)/shard_map/ppermute | solution.py:279
  53.0 3.6 %collective-permute-done.6.got = bf16[128,512]{1,0:T(8,128)(2,1)S(1)} collective-permute-done((bf16[128,512]{1,0:T(8,128)(2,1)S(1)}, bf16[128,512]{1,0:T(8,128)(2,1)S(1)}, u32[]{:S(2)}, u32[]{:S(2)}) %collective-permute-start.6) | collective-permute-done | bytes 131104 | tf_op jit(solution)/shard_map/ppermute | solution.py:279
  58.2 1.6 collective-permute-start.4
  59.8 2.2 shard_map.59.refs_3_.other.refs_5_
  62.0 2.2 shard_map.60.other
  64.5 1.3 shard_map.61
  65.9 31.5 %all_to_all.26.got = bf16[32,128,128]{2,1,0:T(8,128)(2,1)S(1)} all-to-all(bf16[32,128,128]{2,1,0:T(8,128)(2,1)S(1)} %get-tuple-element.53), channel_id=1, replica_groups={{0,8,16,24,25,17,9,1,2,10,18,26,27,19,11,3,4,12,20,28,29,21,13,5,6,14,2..., dimensions={0} | all-to-all | bytes 2097152 | tf_op jit(solution)/shard_map/all_to_all | solution.py:276
  97.4 3.5 %shard_map.62 = (bf16[32,136,128]{2,1,0:T(8,128)(2,1)S(1)}, bf16[256,1024]{1,0:T(8,128)(2,1)S(1)}) custom-call(bf16[32,128,128]{2,1,0:T(8,128)(2,1)S(1)} %all_to_all.26.got, f32[128,128]{1,0:T(8,128)S(1)} %get-tuple-element.54.norms, bf16[2048,1024]{1,0:T(8,128)(2,1)S(1)} %bitcast.22, bf16[2048,1024]{1,0:T(8,128)(2,1)S(1)} %shard_map.60.other), custom_call_target="tpu_custom_call" | custom-call | flops 2147483648 | bytes 11141120 | tf_op jit(solution)/shard_map/pallas_call | solution.py:34
  100.9 34.9 %all_to_all.27.got = bf16[32,136,128]{2,1,0:T(8,128)(2,1)S(1)} all-to-all(bf16[32,136,128]{2,1,0:T(8,128)(2,1)S(1)} %get-tuple-element.56), channel_id=1, replica_groups={{0,8,16,24,25,17,9,1,2,10,18,26,27,19,11,3,4,12,20,28,29,21,13,5,6,14,2..., dimensions={0} | all-to-all | bytes 2228224 | tf_op jit(solution)/shard_map/all_to_all | solution.py:276
  135.8 1.3 shard_map.63
  140.6 1.9 collective-permute-done.8.got
  142.7 1.5 collective-permute-start.9
  144.2 1.9 collective-permute-done.10.got
  146.2 3.1 %collective-permute-done.9.got = bf16[128,640]{1,0:T(8,128)(2,1)S(1)} collective-permute-done((bf16[128,640]{1,0:T(8,128)(2,1)S(1)}, bf16[128,640]{1,0:T(8,128)(2,1)S(1)}, u32[]{:S(2)}, u32[]{:S(2)}) %collective-permute-start.9) | collective-permute-done | bytes 163872 | tf_op jit(solution)/shard_map/ppermute | solution.py:279
  149.6 1.6 collective-permute-done.11.got
  151.3 1.4 shard_map.69
  152.7 29.7 %all_to_all.28.got = bf16[32,128,128]{2,1,0:T(8,128)(2,1)S(1)} all-to-all(bf16[32,128,128]{2,1,0:T(8,128)(2,1)S(1)} %get-tuple-element.64), channel_id=1, replica_groups={{0,8,16,24,25,17,9,1,2,10,18,26,27,19,11,3,4,12,20,28,29,21,13,5,6,14,2..., dimensions={0} | all-to-all | bytes 2097152 | tf_op jit(solution)/shard_map/all_to_all | solution.py:276
  182.4 4.2 %shard_map.70 = (bf16[32,136,128]{2,1,0:T(8,128)(2,1)S(1)}, bf16[256,1024]{1,0:T(8,128)(2,1)}) custom-call(bf16[32,128,128]{2,1,0:T(8,128)(2,1)S(1)} %all_to_all.28.got, f32[128,128]{1,0:T(8,128)S(1)} %get-tuple-element.65.norms, bf16[2048,1024]{1,0:T(8,128)(2,1)S(1)} %bitcast.23, bf16[2048,1024]{1,0:T(8,128)(2,1)S(1)} %shard_map.60.other, ...), custom_call_target="tpu_custom_call" | custom-call | flops 2147483648 | bytes 11665408 | tf_op jit(solution)/shard_map/pallas_call | solution.py:34
  186.6 31.9 %all_to_all.29.got = bf16[32,136,128]{2,1,0:T(8,128)(2,1)S(1)} all-to-all(bf16[32,136,128]{2,1,0:T(8,128)(2,1)S(1)} %get-tuple-element.67), channel_id=1, replica_groups={{0,8,16,24,25,17,9,1,2,10,18,26,27,19,11,3,4,12,20,28,29,21,13,5,6,14,2..., dimensions={0} | all-to-all | bytes 2228224 | tf_op jit(solution)/shard_map/all_to_all | solution.py:276
  222.9 3.1 %collective-permute-start.14 = (bf16[32,1152]{1,0:T(8,128)(2,1)S(1)}, bf16[32,1152]{1,0:T(8,128)(2,1)S(1)}, u32[]{:S(2)}, u32[]{:S(2)}) collective-permute-start(bf16[32,1152]{1,0:T(8,128)(2,1)S(1)} %get-tuple-element.73), channel_id=1, source_target_pairs={{0,192},{32,224},{64,128},{96,160},{128,64},{160,96},{192,0},{224,... | collective-permute-start | bytes 221192 | tf_op jit(solution)/shard_map/ppermute | solution.py:279
  226.1 1.8 collective-permute-done.13
  (54 shorter events, 17.7 us)
Async XLA Ops:
  0.6 46.0 %collective-permute-start = (bf16[1024,2048]{1,0:T(8,128)(2,1)}, bf16[1024,2048]{1,0:T(8,128)(2,1)}, u32[]{:S(2)}, u32[]{:S(2)}) collective-permute-start(bf16[1024,2048]{1,0:T(8,128)(2,1)} %bitcast.11), channel_id=1, source_target_pairs={{0,32},{32,0},{64,96},{96,64},{128,160},{160,128},{192,224},{224,1... | collective-permute-start | bytes 12582920 | tf_op jit(solution)/shard_map/ppermute | solution.py:279
  0.7 45.9 %collective-permute-start.1 = (bf16[2048,1024]{1,0:T(8,128)(2,1)}, bf16[2048,1024]{1,0:T(8,128)(2,1)}, u32[]{:S(2)}, u32[]{:S(2)}) collective-permute-start(bf16[2048,1024]{1,0:T(8,128)(2,1)} %bitcast.20), channel_id=1, source_target_pairs={{0,32},{32,0},{64,96},{96,64},{128,160},{160,128},{192,224},{224,1... | collective-permute-start | bytes 12582920 | tf_op jit(solution)/shard_map/ppermute | solution.py:279
  1.3 45.3 %copy-start = (bf16[1,1024,2048]{2,1,0:T(8,128)(2,1)S(1)}, bf16[1,1024,2048]{2,1,0:T(8,128)(2,1)}, u32[]{:S(2)}) copy-start(bf16[1,1024,2048]{2,1,0:T(8,128)(2,1)} %param.3) | copy-start | bytes 12582916
  1.3 2.3 %copy-start.1 = (bf16[1,2048,1024]{2,1,0:T(8,128)(2,1)S(1)}, bf16[1,2048,1024]{2,1,0:T(8,128)(2,1)}, u32[]{:S(2)}) copy-start(bf16[1,2048,1024]{2,1,0:T(8,128)(2,1)} %param.4) | copy-start | bytes 12582916
  3.7 1.2 copy-start.3
  48.2 1.4 collective-permute-start.5
  48.4 4.4 %collective-permute-start.2 = (bf16[128,512]{1,0:T(8,128)(2,1)S(1)}, bf16[128,512]{1,0:T(8,128)(2,1)S(1)}, u32[]{:S(2)}, u32[]{:S(2)}) collective-permute-start(bf16[128,512]{1,0:T(8,128)(2,1)S(1)} %get-tuple-element.42), channel_id=1, source_target_pairs={{0,32},{32,0},{64,96},{96,64},{128,160},{160,128},{192,224},{224,1... | collective-permute-start | bytes 393224 | tf_op jit(solution)/shard_map/ppermute | solution.py:279
  49.7 6.9 %collective-permute-start.6 = (bf16[128,512]{1,0:T(8,128)(2,1)S(1)}, bf16[128,512]{1,0:T(8,128)(2,1)S(1)}, u32[]{:S(2)}, u32[]{:S(2)}) collective-permute-start(bf16[128,512]{1,0:T(8,128)(2,1)S(1)} %shard_map.56.v), channel_id=1, source_target_pairs={{0,192},{32,224},{64,128},{96,160},{128,64},{160,96},{192,0},{224,... | collective-permute-start | bytes 393224 | tf_op jit(solution)/shard_map/ppermute | solution.py:279
  52.8 5.4 %collective-permute-start.3 = (bf16[128,512]{1,0:T(8,128)(2,1)S(1)}, bf16[128,512]{1,0:T(8,128)(2,1)S(1)}, u32[]{:S(2)}, u32[]{:S(2)}) collective-permute-start(bf16[128,512]{1,0:T(8,128)(2,1)S(1)} %shard_map.52.v), channel_id=1, source_target_pairs={{0,64},{32,96},{64,0},{96,32},{128,192},{160,224},{192,128},{224,1... | collective-permute-start | bytes 393224 | tf_op jit(solution)/shard_map/ppermute | solution.py:279
  56.6 7.6 %collective-permute-start.7 = (bf16[128,512]{1,0:T(8,128)(2,1)S(1)}, bf16[128,512]{1,0:T(8,128)(2,1)S(1)}, u32[]{:S(2)}, u32[]{:S(2)}) collective-permute-start(bf16[128,512]{1,0:T(8,128)(2,1)S(1)} %shard_map.57.v), channel_id=1, source_target_pairs={{0,64},{32,96},{64,0},{96,32},{128,192},{160,224},{192,128},{224,1... | collective-permute-start | bytes 393224 | tf_op jit(solution)/shard_map/ppermute | solution.py:279
  58.2 6.3 %collective-permute-start.4 = (bf16[128,512]{1,0:T(8,128)(2,1)S(1)}, bf16[128,512]{1,0:T(8,128)(2,1)S(1)}, u32[]{:S(2)}, u32[]{:S(2)}) collective-permute-start(bf16[128,512]{1,0:T(8,128)(2,1)S(1)} %shard_map.53.v), channel_id=1, source_target_pairs={{0,192},{32,224},{64,128},{96,160},{128,64},{160,96},{192,0},{224,... | collective-permute-start | bytes 393224 | tf_op jit(solution)/shard_map/ppermute | solution.py:279
  64.5 32.9 %copy-start.2 = (bf16[1,2048,1024]{2,1,0:T(8,128)(2,1)S(1)}, bf16[1,2048,1024]{2,1,0:T(8,128)(2,1)}, u32[]{:S(2)}) copy-start(bf16[1,2048,1024]{2,1,0:T(8,128)(2,1)} %param.4) | copy-start | bytes 12582916
  137.1 5.4 %collective-permute-start.8 = (bf16[128,640]{1,0:T(8,128)(2,1)S(1)}, bf16[128,640]{1,0:T(8,128)(2,1)S(1)}, u32[]{:S(2)}, u32[]{:S(2)}) collective-permute-start(bf16[128,640]{1,0:T(8,128)(2,1)S(1)} %get-tuple-element.57.v), channel_id=1, source_target_pairs={{0,64},{32,96},{64,0},{96,32},{128,192},{160,224},{192,128},{224,1... | collective-permute-start | bytes 491528 | tf_op jit(solution)/shard_map/ppermute | solution.py:279
  139.6 6.4 %collective-permute-start.10 = (bf16[128,512]{1,0:T(8,128)(2,1)S(1)}, bf16[128,512]{1,0:T(8,128)(2,1)S(1)}, u32[]{:S(2)}, u32[]{:S(2)}) collective-permute-start(bf16[128,512]{1,0:T(8,128)(2,1)S(1)} %shard_map.66.v), channel_id=1, source_target_pairs={{0,192},{32,224},{64,128},{96,160},{128,64},{160,96},{192,0},{224,... | collective-permute-start | bytes 393224 | tf_op jit(solution)/shard_map/ppermute | solution.py:279
  142.7 6.6 %collective-permute-start.9 = (bf16[128,640]{1,0:T(8,128)(2,1)S(1)}, bf16[128,640]{1,0:T(8,128)(2,1)S(1)}, u32[]{:S(2)}, u32[]{:S(2)}) collective-permute-start(bf16[128,640]{1,0:T(8,128)(2,1)S(1)} %shard_map.64.v), channel_id=1, source_target_pairs={{0,192},{32,224},{64,128},{96,160},{128,64},{160,96},{192,0},{224,... | collective-permute-start | bytes 491528 | tf_op jit(solution)/shard_map/ppermute | solution.py:279
  146.1 5.1 %collective-permute-start.11 = (bf16[128,512]{1,0:T(8,128)(2,1)S(1)}, bf16[128,512]{1,0:T(8,128)(2,1)S(1)}, u32[]{:S(2)}, u32[]{:S(2)}) collective-permute-start(bf16[128,512]{1,0:T(8,128)(2,1)S(1)} %shard_map.67.v), channel_id=1, source_target_pairs={{0,64},{32,96},{64,0},{96,32},{128,192},{160,224},{192,128},{224,1... | collective-permute-start | bytes 393224 | tf_op jit(solution)/shard_map/ppermute | solution.py:279
  221.2 4.9 %collective-permute-start.12 = (bf16[32,1152]{1,0:T(8,128)(2,1)S(1)}, bf16[32,1152]{1,0:T(8,128)(2,1)S(1)}, u32[]{:S(2)}, u32[]{:S(2)}) collective-permute-start(bf16[32,1152]{1,0:T(8,128)(2,1)S(1)} %get-tuple-element.71), channel_id=1, source_target_pairs={{0,64},{32,96},{64,0},{96,32},{128,192},{160,224},{192,128},{224,1... | collective-permute-start | bytes 221192 | tf_op jit(solution)/shard_map/ppermute | solution.py:279
  222.0 5.9 %collective-permute-start.13 = (bf16[32,1152]{1,0:T(8,128)(2,1)S(1)}, bf16[32,1152]{1,0:T(8,128)(2,1)S(1)}, u32[]{:S(2)}, u32[]{:S(2)}) collective-permute-start(bf16[32,1152]{1,0:T(8,128)(2,1)S(1)} %get-tuple-element.72), channel_id=1, source_target_pairs={{0,128},{32,160},{64,192},{96,224},{128,0},{160,32},{192,64},{224,... | collective-permute-start | bytes 221192 | tf_op jit(solution)/shard_map/ppermute | solution.py:279
  222.9 5.7 %collective-permute-start.14 = (bf16[32,1152]{1,0:T(8,128)(2,1)S(1)}, bf16[32,1152]{1,0:T(8,128)(2,1)S(1)}, u32[]{:S(2)}, u32[]{:S(2)}) collective-permute-start(bf16[32,1152]{1,0:T(8,128)(2,1)S(1)} %get-tuple-element.73), channel_id=1, source_target_pairs={{0,192},{32,224},{64,128},{96,160},{128,64},{160,96},{192,0},{224,... | collective-permute-start | bytes 221192 | tf_op jit(solution)/shard_map/ppermute | solution.py:279

commit v6 on v5

--- a/solution.py
+++ b/solution.py
@@ -22,7 +22,7 @@
 def order_of(blocks):
     if blocks != 32:
         return list(range(blocks))
-    return [(x if z % 2 == 0 else 3 - x) * 8 + z for z in range(8) for x in range(4)]
+    return [x * 8 + z for z in range(8) for x in range(4)]
 
 
 def dot(a, b, dims=((1,), (0,))):
@@ -222,15 +222,21 @@
 
 
 def middle_body(order, place, rank, cross, got, norms, r, other, *rest):
+    fetch = None
     if cross:
         old, out, seen, natural, turned = rest
     else:
-        out, seen, natural, turned = rest
+        out, seen, kept, natural, turned, sem = rest
+        fetch = pltpu.make_async_copy(other, kept, sem)
+        fetch.start()
+        other = kept
     width, cells = r.shape
     half = got.shape[2]
     square = product = 0.0
     for band, factor in enumerate((r, other)):
         take_band(got, natural, order, rank, band)
+        if band and fetch is not None:
+            fetch.wait()
         images = slice(band * half, (band + 1) * half)
         step = min(STEP, width)
         for j in range(0, width, step):
@@ -315,14 +321,19 @@
         )
         return exchange(coeff), norms
 
-    def middle(got, norms, old=()):
-        out, seen = call(
+    def middle(got, norms, other, old=()):
+        outs = [shape((blocks, 2 * rank + EXTRA, half), bf16), shape((m, cells), bf16)]
+        scratch = [pltpu.VMEM((2 * width, half), bf16), pltpu.VMEM((m, width), bf16)]
+        specs = [VMEM] * (4 + len(old))
+        if not old:
+            outs.append(shape(other.shape, bf16))
+            scratch.append(pltpu.SemaphoreType.DMA)
+            specs[3] = ANY
+        out, seen, *kept = call(
             functools.partial(middle_body, order, place, rank, bool(old)),
-            [shape((blocks, 2 * rank + EXTRA, half), bf16), shape((m, cells), bf16)],
-            [pltpu.VMEM((2 * width, half), bf16), pltpu.VMEM((m, width), bf16)], 2 * work,
-            (got, norms, right, right_other, *old),
-        )
-        return exchange(out), seen
+            outs, scratch, 2 * work, (got, norms, right, other, *old), specs,
+        )
+        return exchange(out), seen, kept
 
     perm = jnp.stack([me ^ (2 * y + c) for c in range(2) for y in range(pairs)]).astype(jnp.int32)
     back = call(
@@ -334,17 +345,16 @@
     ways = (1, 3)
     r0, p0 = [], []
     got, left_other, right_other = lax.optimization_barrier((exchange(back), left_other, right_other))
-    left_other, right_other = (
-        call(bring_body, [shape(v.shape, bf16)], [pltpu.SemaphoreType.DMA], 0, (v,), [ANY])[0]
-        for v in (left_other, right_other)
-    )
+    left_other = call(
+        bring_body, [shape(left.shape, bf16)], [pltpu.SemaphoreType.DMA], 0, (left_other,), [ANY]
+    )[0]
     for k, piece in zip(ways, adjoint(got)):
         r, p = call(functools.partial(start_body, 4 - k, pairs), [state, sent], [], state.size, along_y(k, piece))
         r0.append(r)
         p0.append(p)
-    p0, left_other, right_other = lax.optimization_barrier((p0, left_other, right_other))
+    p0, left_other = lax.optimization_barrier((p0, left_other))
     got, norms = forward(p0)
-    got, s0 = middle(got, norms)
+    got, s0, (right_other,) = middle(got, norms, right_other)
     low, high = adjoint_both(got, bf16)
     q, r, p, sums0 = call(
         functools.partial(update_body, 3, pairs, True),
@@ -357,7 +367,7 @@
     )
     q0, r1, p1 = q0 + [q], r1 + [r], p1 + [p]
     got, norms = forward(p1, p0)
-    got, _ = middle(got, norms, (s0,))
+    got, _, _ = middle(got, norms, right_other, (s0,))
     low, high = adjoint_both(got, f32)
     columns = cells + TAIL
     mine, *rest = call(

time: 231 us -> 228 us (0.987)
  blocking collectives: 168 us -> 163 us
  waiting for transfers between devices: 16.8 us -> 19.8 us
    all_to_all x5, blocking collectives: 168 us -> 163 us  [exchange(): return lax.all_to_all(v, SPACE, 0, 0, tiled=True, axis_index_groups=[order])]
    ppermute x15, waiting for transfers between devices: 16.8 us -> 19.8 us  [swap(): return lax.ppermute(v, BAND, [(i, i ^ flip) for i in range(bands)])]
    pallas_call x24 -> x23, Pallas kernels: 24.4 us -> 22.7 us  [call(): pl.pallas_call(body, out_shape=outs, in_specs=specs or [VMEM] * len(args)...]
  transfers between devices with their start and end apart: 15 -> 15, of which waited for: 10 -> 9; matrix products, arithmetic and copies ran while one was open for 0% -> 0% of each run, Pallas kernels for 4% -> 3%
where the time goes in v6:
time: 228 us
  blocking collectives  163 us (71%)
  Pallas kernels  22.7 us (10%)
  waiting for transfers between devices  19.8 us (9%)
  starting transfers between devices  16.7 us (7%)
  local copies, waits for them, and re-layouts  3.69 us (2%)
    all_to_all x5, blocking collectives, exchange(): return lax.all_to_all(v, SPACE, 0, 0, tiled=True, axis_index_groups=[order])  163 us
    pallas_call x23, Pallas kernels, call(): pl.pallas_call(body, out_shape=outs, in_specs=specs or [VMEM] * len(args)...  22.7 us
    ppermute x15, waiting for transfers between devices, swap(): return lax.ppermute(v, BAND, [(i, i ^ flip) for i in range(bands)])  19.8 us
    ppermute x15, starting transfers between devices, swap(): return lax.ppermute(v, BAND, [(i, i ^ flip) for i in range(bands)])  16.7 us
  transfers between devices with their start and end apart: 15, of which 9 were waited for; matrix products, arithmetic and copies ran while one was open for 0% of the time, Pallas kernels for 3%

profile of v6, /device:TPU:32, one launch (start us, length us, event | category | flops | bytes accessed | tf_op | source)
XLA Modules:
  0.0 227.5 jit_solution(9476041690126989090)
XLA Ops:
  1.3 2.3 %copy-done.1 = bf16[1,2048,1024]{2,1,0:T(8,128)(2,1)S(1)} copy-done((bf16[1,2048,1024]{2,1,0:T(8,128)(2,1)S(1)}, bf16[1,2048,1024]{2,1,0:T(8,128)(2,1)}, u32[]{:S(2)}) %copy-start.1) | copy-done | bytes 4194328
  4.9 1.8 shard_map.50
  6.7 38.4 %all_to_all.25.got = bf16[32,128,128]{2,1,0:T(8,128)(2,1)S(1)} all-to-all(bf16[32,128,128]{2,1,0:T(8,128)(2,1)S(1)} %shard_map.50), channel_id=1, replica_groups={{0,8,16,24,1,9,17,25,2,10,18,26,3,11,19,27,4,12,20,28,5,13,21,29,6,14,2..., dimensions={0} | all-to-all | bytes 2097152 | tf_op jit(solution)/shard_map/all_to_all | solution.py:282
  48.3 3.1 %collective-permute-start.6 = (bf16[128,512]{1,0:T(8,128)(2,1)S(1)}, bf16[128,512]{1,0:T(8,128)(2,1)S(1)}, u32[]{:S(2)}, u32[]{:S(2)}) collective-permute-start(bf16[128,512]{1,0:T(8,128)(2,1)S(1)} %shard_map.56.v), channel_id=1, source_target_pairs={{0,192},{32,224},{64,128},{96,160},{128,64},{160,96},{192,0},{224,... | collective-permute-start | bytes 393224 | tf_op jit(solution)/shard_map/ppermute | solution.py:285
  51.6 3.6 %collective-permute-done.6.got = bf16[128,512]{1,0:T(8,128)(2,1)S(1)} collective-permute-done((bf16[128,512]{1,0:T(8,128)(2,1)S(1)}, bf16[128,512]{1,0:T(8,128)(2,1)S(1)}, u32[]{:S(2)}, u32[]{:S(2)}) %collective-permute-start.6) | collective-permute-done | bytes 131104 | tf_op jit(solution)/shard_map/ppermute | solution.py:285
  56.8 1.6 collective-permute-start.4
  58.4 2.2 shard_map.59.refs_3_.other.refs_5_
  60.7 2.4 %collective-permute-done.4.got = bf16[128,512]{1,0:T(8,128)(2,1)S(1)} collective-permute-done((bf16[128,512]{1,0:T(8,128)(2,1)S(1)}, bf16[128,512]{1,0:T(8,128)(2,1)S(1)}, u32[]{:S(2)}, u32[]{:S(2)}) %collective-permute-start.4) | collective-permute-done | bytes 131104 | tf_op jit(solution)/shard_map/ppermute | solution.py:285
  63.1 1.3 shard_map.60
  64.5 31.8 %all_to_all.26.got = bf16[32,128,128]{2,1,0:T(8,128)(2,1)S(1)} all-to-all(bf16[32,128,128]{2,1,0:T(8,128)(2,1)S(1)} %get-tuple-element.52), channel_id=1, replica_groups={{0,8,16,24,1,9,17,25,2,10,18,26,3,11,19,27,4,12,20,28,5,13,21,29,6,14,2..., dimensions={0} | all-to-all | bytes 2097152 | tf_op jit(solution)/shard_map/all_to_all | solution.py:282
  96.3 4.0 %shard_map.61 = (bf16[32,136,128]{2,1,0:T(8,128)(2,1)S(1)}, bf16[256,1024]{1,0:T(8,128)(2,1)S(1)}, bf16[2048,1024]{1,0:T(8,128)(2,1)S(1)}) custom-call(bf16[32,128,128]{2,1,0:T(8,128)(2,1)S(1)} %all_to_all.26.got, f32[128,128]{1,0:T(8,128)S(1)} %get-tuple-element.53.norms, bf16[2048,1024]{1,0:T(8,128)(2,1)S(1)} %bitcast.22, ...), custom_call_target="tpu_custom_call" | custom-call | flops 2147483648 | bytes 15335424 | tf_op jit(solution)/shard_map/pallas_call | solution.py:34
  100.4 34.2 %all_to_all.27.got = bf16[32,136,128]{2,1,0:T(8,128)(2,1)S(1)} all-to-all(bf16[32,136,128]{2,1,0:T(8,128)(2,1)S(1)} %get-tuple-element.55), channel_id=1, replica_groups={{0,8,16,24,1,9,17,25,2,10,18,26,3,11,19,27,4,12,20,28,5,13,21,29,6,14,2..., dimensions={0} | all-to-all | bytes 2228224 | tf_op jit(solution)/shard_map/all_to_all | solution.py:282
  134.5 1.3 shard_map.62
  137.7 2.3 collective-permute-start.10
  139.9 1.7 collective-permute-done.8.got
  141.8 2.5 %collective-permute-start.9 = (bf16[128,640]{1,0:T(8,128)(2,1)S(1)}, bf16[128,640]{1,0:T(8,128)(2,1)S(1)}, u32[]{:S(2)}, u32[]{:S(2)}) collective-permute-start(bf16[128,640]{1,0:T(8,128)(2,1)S(1)} %shard_map.63.v), channel_id=1, source_target_pairs={{0,192},{32,224},{64,128},{96,160},{128,64},{160,96},{192,0},{224,... | collective-permute-start | bytes 491528 | tf_op jit(solution)/shard_map/ppermute | solution.py:285
  144.5 4.0 %collective-permute-done.9.got = bf16[128,640]{1,0:T(8,128)(2,1)S(1)} collective-permute-done((bf16[128,640]{1,0:T(8,128)(2,1)S(1)}, bf16[128,640]{1,0:T(8,128)(2,1)S(1)}, u32[]{:S(2)}, u32[]{:S(2)}) %collective-permute-start.9) | collective-permute-done | bytes 163872 | tf_op jit(solution)/shard_map/ppermute | solution.py:285
  149.6 1.4 shard_map.68
  151.0 26.7 %all_to_all.28.got = bf16[32,128,128]{2,1,0:T(8,128)(2,1)S(1)} all-to-all(bf16[32,128,128]{2,1,0:T(8,128)(2,1)S(1)} %get-tuple-element.63), channel_id=1, replica_groups={{0,8,16,24,1,9,17,25,2,10,18,26,3,11,19,27,4,12,20,28,5,13,21,29,6,14,2..., dimensions={0} | all-to-all | bytes 2097152 | tf_op jit(solution)/shard_map/all_to_all | solution.py:282
  177.6 4.1 %shard_map.69 = (bf16[32,136,128]{2,1,0:T(8,128)(2,1)S(1)}, bf16[256,1024]{1,0:T(8,128)(2,1)}) custom-call(bf16[32,128,128]{2,1,0:T(8,128)(2,1)S(1)} %all_to_all.28.got, f32[128,128]{1,0:T(8,128)S(1)} %get-tuple-element.64.norms, bf16[2048,1024]{1,0:T(8,128)(2,1)S(1)} %bitcast.23, bf16[2048,1024]{1,0:T(8,128)(2,1)S(1)} %get-tuple-element.65.other, ...), custom_call_target="tpu_custom_call" | custom-call | flops 2147483648 | bytes 11665408 | tf_op jit(solution)/shard_map/pallas_call | solution.py:34
  181.8 31.5 %all_to_all.29.got = bf16[32,136,128]{2,1,0:T(8,128)(2,1)S(1)} all-to-all(bf16[32,136,128]{2,1,0:T(8,128)(2,1)S(1)} %get-tuple-element.67), channel_id=1, replica_groups={{0,8,16,24,1,9,17,25,2,10,18,26,3,11,19,27,4,12,20,28,5,13,21,29,6,14,2..., dimensions={0} | all-to-all | bytes 2228224 | tf_op jit(solution)/shard_map/all_to_all | solution.py:282
  216.7 4.1 %collective-permute-start.13 = (bf16[32,1152]{1,0:T(8,128)(2,1)S(1)}, bf16[32,1152]{1,0:T(8,128)(2,1)S(1)}, u32[]{:S(2)}, u32[]{:S(2)}) collective-permute-start(bf16[32,1152]{1,0:T(8,128)(2,1)S(1)} %get-tuple-element.72), channel_id=1, source_target_pairs={{0,128},{32,160},{64,192},{96,224},{128,0},{160,32},{192,64},{224,... | collective-permute-start | bytes 221192 | tf_op jit(solution)/shard_map/ppermute | solution.py:285
  220.9 3.0 %collective-permute-done.13 = bf16[32,1152]{1,0:T(8,128)(2,1)S(1)} collective-permute-done((bf16[32,1152]{1,0:T(8,128)(2,1)S(1)}, bf16[32,1152]{1,0:T(8,128)(2,1)S(1)}, u32[]{:S(2)}, u32[]{:S(2)}) %collective-permute-start.13) | collective-permute-done | bytes 73760 | tf_op jit(solution)/shard_map/ppermute | solution.py:285
  223.9 2.4 %collective-permute-done.14 = bf16[32,1152]{1,0:T(8,128)(2,1)S(1)} collective-permute-done((bf16[32,1152]{1,0:T(8,128)(2,1)S(1)}, bf16[32,1152]{1,0:T(8,128)(2,1)S(1)}, u32[]{:S(2)}, u32[]{:S(2)}) %collective-permute-start.14) | collective-permute-done | bytes 73760 | tf_op jit(solution)/shard_map/ppermute | solution.py:285
  (53 shorter events, 14.8 us)
Async XLA Ops:
  0.6 44.5 %collective-permute-start = (bf16[1024,2048]{1,0:T(8,128)(2,1)}, bf16[1024,2048]{1,0:T(8,128)(2,1)}, u32[]{:S(2)}, u32[]{:S(2)}) collective-permute-start(bf16[1024,2048]{1,0:T(8,128)(2,1)} %bitcast.11), channel_id=1, source_target_pairs={{0,32},{32,0},{64,96},{96,64},{128,160},{160,128},{192,224},{224,1... | collective-permute-start | bytes 12582920 | tf_op jit(solution)/shard_map/ppermute | solution.py:285
  0.7 44.4 %collective-permute-start.1 = (bf16[2048,1024]{1,0:T(8,128)(2,1)}, bf16[2048,1024]{1,0:T(8,128)(2,1)}, u32[]{:S(2)}, u32[]{:S(2)}) collective-permute-start(bf16[2048,1024]{1,0:T(8,128)(2,1)} %bitcast.20), channel_id=1, source_target_pairs={{0,32},{32,0},{64,96},{96,64},{128,160},{160,128},{192,224},{224,1... | collective-permute-start | bytes 12582920 | tf_op jit(solution)/shard_map/ppermute | solution.py:285
  1.3 43.9 %copy-start = (bf16[1,1024,2048]{2,1,0:T(8,128)(2,1)S(1)}, bf16[1,1024,2048]{2,1,0:T(8,128)(2,1)}, u32[]{:S(2)}) copy-start(bf16[1,1024,2048]{2,1,0:T(8,128)(2,1)} %param.3) | copy-start | bytes 12582916
  1.3 2.3 %copy-start.1 = (bf16[1,2048,1024]{2,1,0:T(8,128)(2,1)S(1)}, bf16[1,2048,1024]{2,1,0:T(8,128)(2,1)}, u32[]{:S(2)}) copy-start(bf16[1,2048,1024]{2,1,0:T(8,128)(2,1)} %param.4) | copy-start | bytes 12582916
  3.7 1.2 copy-start.3
  46.8 1.4 collective-permute-start.5
  46.9 4.5 %collective-permute-start.2 = (bf16[128,512]{1,0:T(8,128)(2,1)S(1)}, bf16[128,512]{1,0:T(8,128)(2,1)S(1)}, u32[]{:S(2)}, u32[]{:S(2)}) collective-permute-start(bf16[128,512]{1,0:T(8,128)(2,1)S(1)} %get-tuple-element.42), channel_id=1, source_target_pairs={{0,32},{32,0},{64,96},{96,64},{128,160},{160,128},{192,224},{224,1... | collective-permute-start | bytes 393224 | tf_op jit(solution)/shard_map/ppermute | solution.py:285
  48.3 6.9 %collective-permute-start.6 = (bf16[128,512]{1,0:T(8,128)(2,1)S(1)}, bf16[128,512]{1,0:T(8,128)(2,1)S(1)}, u32[]{:S(2)}, u32[]{:S(2)}) collective-permute-start(bf16[128,512]{1,0:T(8,128)(2,1)S(1)} %shard_map.56.v), channel_id=1, source_target_pairs={{0,192},{32,224},{64,128},{96,160},{128,64},{160,96},{192,0},{224,... | collective-permute-start | bytes 393224 | tf_op jit(solution)/shard_map/ppermute | solution.py:285
  51.4 5.4 %collective-permute-start.3 = (bf16[128,512]{1,0:T(8,128)(2,1)S(1)}, bf16[128,512]{1,0:T(8,128)(2,1)S(1)}, u32[]{:S(2)}, u32[]{:S(2)}) collective-permute-start(bf16[128,512]{1,0:T(8,128)(2,1)S(1)} %shard_map.52.v), channel_id=1, source_target_pairs={{0,64},{32,96},{64,0},{96,32},{128,192},{160,224},{192,128},{224,1... | collective-permute-start | bytes 393224 | tf_op jit(solution)/shard_map/ppermute | solution.py:285
  55.2 5.4 %collective-permute-start.7 = (bf16[128,512]{1,0:T(8,128)(2,1)S(1)}, bf16[128,512]{1,0:T(8,128)(2,1)S(1)}, u32[]{:S(2)}, u32[]{:S(2)}) collective-permute-start(bf16[128,512]{1,0:T(8,128)(2,1)S(1)} %shard_map.57.v), channel_id=1, source_target_pairs={{0,64},{32,96},{64,0},{96,32},{128,192},{160,224},{192,128},{224,1... | collective-permute-start | bytes 393224 | tf_op jit(solution)/shard_map/ppermute | solution.py:285
  56.8 6.3 %collective-permute-start.4 = (bf16[128,512]{1,0:T(8,128)(2,1)S(1)}, bf16[128,512]{1,0:T(8,128)(2,1)S(1)}, u32[]{:S(2)}, u32[]{:S(2)}) collective-permute-start(bf16[128,512]{1,0:T(8,128)(2,1)S(1)} %shard_map.53.v), channel_id=1, source_target_pairs={{0,192},{32,224},{64,128},{96,160},{128,64},{160,96},{192,0},{224,... | collective-permute-start | bytes 393224 | tf_op jit(solution)/shard_map/ppermute | solution.py:285
  63.1 33.2 %copy-start.2 = (bf16[1,2048,1024]{2,1,0:T(8,128)(2,1)S(1)}, bf16[1,2048,1024]{2,1,0:T(8,128)(2,1)}, u32[]{:S(2)}) copy-start(bf16[1,2048,1024]{2,1,0:T(8,128)(2,1)} %param.4) | copy-start | bytes 12582916
  135.9 5.8 %collective-permute-start.8 = (bf16[128,640]{1,0:T(8,128)(2,1)S(1)}, bf16[128,640]{1,0:T(8,128)(2,1)S(1)}, u32[]{:S(2)}, u32[]{:S(2)}) collective-permute-start(bf16[128,640]{1,0:T(8,128)(2,1)S(1)} %get-tuple-element.56.v), channel_id=1, source_target_pairs={{0,64},{32,96},{64,0},{96,32},{128,192},{160,224},{192,128},{224,1... | collective-permute-start | bytes 491528 | tf_op jit(solution)/shard_map/ppermute | solution.py:285
  137.7 6.6 %collective-permute-start.10 = (bf16[128,512]{1,0:T(8,128)(2,1)S(1)}, bf16[128,512]{1,0:T(8,128)(2,1)S(1)}, u32[]{:S(2)}, u32[]{:S(2)}) collective-permute-start(bf16[128,512]{1,0:T(8,128)(2,1)S(1)} %shard_map.65.v), channel_id=1, source_target_pairs={{0,192},{32,224},{64,128},{96,160},{128,64},{160,96},{192,0},{224,... | collective-permute-start | bytes 393224 | tf_op jit(solution)/shard_map/ppermute | solution.py:285
  141.8 6.6 %collective-permute-start.9 = (bf16[128,640]{1,0:T(8,128)(2,1)S(1)}, bf16[128,640]{1,0:T(8,128)(2,1)S(1)}, u32[]{:S(2)}, u32[]{:S(2)}) collective-permute-start(bf16[128,640]{1,0:T(8,128)(2,1)S(1)} %shard_map.63.v), channel_id=1, source_target_pairs={{0,192},{32,224},{64,128},{96,160},{128,64},{160,96},{192,0},{224,... | collective-permute-start | bytes 491528 | tf_op jit(solution)/shard_map/ppermute | solution.py:285
  144.3 5.1 %collective-permute-start.11 = (bf16[128,512]{1,0:T(8,128)(2,1)S(1)}, bf16[128,512]{1,0:T(8,128)(2,1)S(1)}, u32[]{:S(2)}, u32[]{:S(2)}) collective-permute-start(bf16[128,512]{1,0:T(8,128)(2,1)S(1)} %shard_map.66.v), channel_id=1, source_target_pairs={{0,64},{32,96},{64,0},{96,32},{128,192},{160,224},{192,128},{224,1... | collective-permute-start | bytes 393224 | tf_op jit(solution)/shard_map/ppermute | solution.py:285
  216.0 4.9 %collective-permute-start.12 = (bf16[32,1152]{1,0:T(8,128)(2,1)S(1)}, bf16[32,1152]{1,0:T(8,128)(2,1)S(1)}, u32[]{:S(2)}, u32[]{:S(2)}) collective-permute-start(bf16[32,1152]{1,0:T(8,128)(2,1)S(1)} %get-tuple-element.71), channel_id=1, source_target_pairs={{0,64},{32,96},{64,0},{96,32},{128,192},{160,224},{192,128},{224,1... | collective-permute-start | bytes 221192 | tf_op jit(solution)/shard_map/ppermute | solution.py:285
  216.7 7.2 %collective-permute-start.13 = (bf16[32,1152]{1,0:T(8,128)(2,1)S(1)}, bf16[32,1152]{1,0:T(8,128)(2,1)S(1)}, u32[]{:S(2)}, u32[]{:S(2)}) collective-permute-start(bf16[32,1152]{1,0:T(8,128)(2,1)S(1)} %get-tuple-element.72), channel_id=1, source_target_pairs={{0,128},{32,160},{64,192},{96,224},{128,0},{160,32},{192,64},{224,... | collective-permute-start | bytes 221192 | tf_op jit(solution)/shard_map/ppermute | solution.py:285
  220.8 5.6 %collective-permute-start.14 = (bf16[32,1152]{1,0:T(8,128)(2,1)S(1)}, bf16[32,1152]{1,0:T(8,128)(2,1)S(1)}, u32[]{:S(2)}, u32[]{:S(2)}) collective-permute-start(bf16[32,1152]{1,0:T(8,128)(2,1)S(1)} %get-tuple-element.73), channel_id=1, source_target_pairs={{0,192},{32,224},{64,128},{96,160},{128,64},{160,96},{192,0},{224,... | collective-permute-start | bytes 221192 | tf_op jit(solution)/shard_map/ppermute | solution.py:285

commit v7 on v6

--- a/solution.py
+++ b/solution.py
@@ -12,7 +12,7 @@
 f32, bf16 = jnp.float32, jnp.bfloat16
 EXTRA = 8
 TAIL = 128
-STEP = 256
+STEP = 512
 
 VMEM = pl.BlockSpec(memory_space=pltpu.VMEM)
 ANY = pl.BlockSpec(memory_space=pl.ANY)
@@ -22,7 +22,7 @@
 def order_of(blocks):
     if blocks != 32:
         return list(range(blocks))
-    return [x * 8 + z for z in range(8) for x in range(4)]
+    return [x * 8 + (z + x) % 8 for z in range(8) for x in range(4)]
 
 
 def dot(a, b, dims=((1,), (0,))):

time: 228 us -> 227 us (level)
  transfers between devices with their start and end apart: 15 -> 15, of which waited for: 9 -> 10; matrix products, arithmetic and copies ran while one was open for 0% -> 0% of each run, Pallas kernels for 3% -> 3%
where the time goes in v7:
time: 227 us
  blocking collectives  163 us (72%)
  Pallas kernels  22.2 us (10%)
  waiting for transfers between devices  19.1 us (8%)
  starting transfers between devices  16.7 us (7%)
  local copies, waits for them, and re-layouts  3.69 us (2%)
    all_to_all x5, blocking collectives, exchange(): return lax.all_to_all(v, SPACE, 0, 0, tiled=True, axis_index_groups=[order])  163 us
    pallas_call x23, Pallas kernels, call(): pl.pallas_call(body, out_shape=outs, in_specs=specs or [VMEM] * len(args)...  22.2 us
    ppermute x15, waiting for transfers between devices, swap(): return lax.ppermute(v, BAND, [(i, i ^ flip) for i in range(bands)])  19.1 us
    ppermute x15, starting transfers between devices, swap(): return lax.ppermute(v, BAND, [(i, i ^ flip) for i in range(bands)])  16.7 us
  transfers between devices with their start and end apart: 15, of which 10 were waited for; matrix products, arithmetic and copies ran while one was open for 0% of the time, Pallas kernels for 3%

profile of v7, /device:TPU:32, one launch (start us, length us, event | category | flops | bytes accessed | tf_op | source)
XLA Modules:
  0.0 226.8 jit_solution(3836383455272944138)
XLA Ops:
  1.3 2.3 %copy-done.1 = bf16[1,2048,1024]{2,1,0:T(8,128)(2,1)S(1)} copy-done((bf16[1,2048,1024]{2,1,0:T(8,128)(2,1)S(1)}, bf16[1,2048,1024]{2,1,0:T(8,128)(2,1)}, u32[]{:S(2)}) %copy-start.1) | copy-done | bytes 4194328
  4.9 1.8 shard_map.50
  6.7 38.4 %all_to_all.25.got = bf16[32,128,128]{2,1,0:T(8,128)(2,1)S(1)} all-to-all(bf16[32,128,128]{2,1,0:T(8,128)(2,1)S(1)} %shard_map.50), channel_id=1, replica_groups={{0,9,18,27,1,10,19,28,2,11,20,29,3,12,21,30,4,13,22,31,5,14,23,24,6,15,..., dimensions={0} | all-to-all | bytes 2097152 | tf_op jit(solution)/shard_map/all_to_all | solution.py:282
  48.3 3.1 %collective-permute-start.6 = (bf16[128,512]{1,0:T(8,128)(2,1)S(1)}, bf16[128,512]{1,0:T(8,128)(2,1)S(1)}, u32[]{:S(2)}, u32[]{:S(2)}) collective-permute-start(bf16[128,512]{1,0:T(8,128)(2,1)S(1)} %shard_map.56.v), channel_id=1, source_target_pairs={{0,192},{32,224},{64,128},{96,160},{128,64},{160,96},{192,0},{224,... | collective-permute-start | bytes 393224 | tf_op jit(solution)/shard_map/ppermute | solution.py:285
  51.6 3.6 %collective-permute-done.6.got = bf16[128,512]{1,0:T(8,128)(2,1)S(1)} collective-permute-done((bf16[128,512]{1,0:T(8,128)(2,1)S(1)}, bf16[128,512]{1,0:T(8,128)(2,1)S(1)}, u32[]{:S(2)}, u32[]{:S(2)}) %collective-permute-start.6) | collective-permute-done | bytes 131104 | tf_op jit(solution)/shard_map/ppermute | solution.py:285
  56.8 1.6 collective-permute-start.4
  58.4 2.2 shard_map.59.refs_3_.other.refs_5_
  60.7 2.4 %collective-permute-done.4.got = bf16[128,512]{1,0:T(8,128)(2,1)S(1)} collective-permute-done((bf16[128,512]{1,0:T(8,128)(2,1)S(1)}, bf16[128,512]{1,0:T(8,128)(2,1)S(1)}, u32[]{:S(2)}, u32[]{:S(2)}) %collective-permute-start.4) | collective-permute-done | bytes 131104 | tf_op jit(solution)/shard_map/ppermute | solution.py:285
  63.1 1.3 shard_map.60
  64.5 31.6 %all_to_all.26.got = bf16[32,128,128]{2,1,0:T(8,128)(2,1)S(1)} all-to-all(bf16[32,128,128]{2,1,0:T(8,128)(2,1)S(1)} %get-tuple-element.52), channel_id=1, replica_groups={{0,9,18,27,1,10,19,28,2,11,20,29,3,12,21,30,4,13,22,31,5,14,23,24,6,15,..., dimensions={0} | all-to-all | bytes 2097152 | tf_op jit(solution)/shard_map/all_to_all | solution.py:282
  96.0 4.0 %shard_map.61 = (bf16[32,136,128]{2,1,0:T(8,128)(2,1)S(1)}, bf16[256,1024]{1,0:T(8,128)(2,1)S(1)}, bf16[2048,1024]{1,0:T(8,128)(2,1)S(1)}) custom-call(bf16[32,128,128]{2,1,0:T(8,128)(2,1)S(1)} %all_to_all.26.got, f32[128,128]{1,0:T(8,128)S(1)} %get-tuple-element.53.norms, bf16[2048,1024]{1,0:T(8,128)(2,1)S(1)} %bitcast.22, ...), custom_call_target="tpu_custom_call" | custom-call | flops 2147483648 | bytes 15335424 | tf_op jit(solution)/shard_map/pallas_call | solution.py:34
  100.1 33.6 %all_to_all.27.got = bf16[32,136,128]{2,1,0:T(8,128)(2,1)S(1)} all-to-all(bf16[32,136,128]{2,1,0:T(8,128)(2,1)S(1)} %get-tuple-element.55), channel_id=1, replica_groups={{0,9,18,27,1,10,19,28,2,11,20,29,3,12,21,30,4,13,22,31,5,14,23,24,6,15,..., dimensions={0} | all-to-all | bytes 2228224 | tf_op jit(solution)/shard_map/all_to_all | solution.py:282
  133.7 1.4 shard_map.62
  136.7 2.5 %collective-permute-start.10 = (bf16[128,512]{1,0:T(8,128)(2,1)S(1)}, bf16[128,512]{1,0:T(8,128)(2,1)S(1)}, u32[]{:S(2)}, u32[]{:S(2)}) collective-permute-start(bf16[128,512]{1,0:T(8,128)(2,1)S(1)} %shard_map.65.v), channel_id=1, source_target_pairs={{0,192},{32,224},{64,128},{96,160},{128,64},{160,96},{192,0},{224,... | collective-permute-start | bytes 393224 | tf_op jit(solution)/shard_map/ppermute | solution.py:285
  140.6 2.1 collective-permute-start.9
  143.7 3.6 %collective-permute-done.9.got = bf16[128,640]{1,0:T(8,128)(2,1)S(1)} collective-permute-done((bf16[128,640]{1,0:T(8,128)(2,1)S(1)}, bf16[128,640]{1,0:T(8,128)(2,1)S(1)}, u32[]{:S(2)}, u32[]{:S(2)}) %collective-permute-start.9) | collective-permute-done | bytes 163872 | tf_op jit(solution)/shard_map/ppermute | solution.py:285
  148.4 1.4 shard_map.68
  149.8 27.8 %all_to_all.28.got = bf16[32,128,128]{2,1,0:T(8,128)(2,1)S(1)} all-to-all(bf16[32,128,128]{2,1,0:T(8,128)(2,1)S(1)} %get-tuple-element.63), channel_id=1, replica_groups={{0,9,18,27,1,10,19,28,2,11,20,29,3,12,21,30,4,13,22,31,5,14,23,24,6,15,..., dimensions={0} | all-to-all | bytes 2097152 | tf_op jit(solution)/shard_map/all_to_all | solution.py:282
  177.6 3.5 %shard_map.69 = (bf16[32,136,128]{2,1,0:T(8,128)(2,1)S(1)}, bf16[256,1024]{1,0:T(8,128)(2,1)}) custom-call(bf16[32,128,128]{2,1,0:T(8,128)(2,1)S(1)} %all_to_all.28.got, f32[128,128]{1,0:T(8,128)S(1)} %get-tuple-element.64.norms, bf16[2048,1024]{1,0:T(8,128)(2,1)S(1)} %bitcast.23, bf16[2048,1024]{1,0:T(8,128)(2,1)S(1)} %get-tuple-element.65.other, ...), custom_call_target="tpu_custom_call" | custom-call | flops 2147483648 | bytes 11665408 | tf_op jit(solution)/shard_map/pallas_call | solution.py:34
  181.1 31.8 %all_to_all.29.got = bf16[32,136,128]{2,1,0:T(8,128)(2,1)S(1)} all-to-all(bf16[32,136,128]{2,1,0:T(8,128)(2,1)S(1)} %get-tuple-element.67), channel_id=1, replica_groups={{0,9,18,27,1,10,19,28,2,11,20,29,3,12,21,30,4,13,22,31,5,14,23,24,6,15,..., dimensions={0} | all-to-all | bytes 2228224 | tf_op jit(solution)/shard_map/all_to_all | solution.py:282
  212.9 1.4 shard_map.70
  215.8 4.3 %collective-permute-start.13 = (bf16[32,1152]{1,0:T(8,128)(2,1)S(1)}, bf16[32,1152]{1,0:T(8,128)(2,1)S(1)}, u32[]{:S(2)}, u32[]{:S(2)}) collective-permute-start(bf16[32,1152]{1,0:T(8,128)(2,1)S(1)} %get-tuple-element.72), channel_id=1, source_target_pairs={{0,128},{32,160},{64,192},{96,224},{128,0},{160,32},{192,64},{224,... | collective-permute-start | bytes 221192 | tf_op jit(solution)/shard_map/ppermute | solution.py:285
  220.5 2.7 %collective-permute-done.13 = bf16[32,1152]{1,0:T(8,128)(2,1)S(1)} collective-permute-done((bf16[32,1152]{1,0:T(8,128)(2,1)S(1)}, bf16[32,1152]{1,0:T(8,128)(2,1)S(1)}, u32[]{:S(2)}, u32[]{:S(2)}) %collective-permute-start.13) | collective-permute-done | bytes 73760 | tf_op jit(solution)/shard_map/ppermute | solution.py:285
  223.2 2.4 %collective-permute-done.14 = bf16[32,1152]{1,0:T(8,128)(2,1)S(1)} collective-permute-done((bf16[32,1152]{1,0:T(8,128)(2,1)S(1)}, bf16[32,1152]{1,0:T(8,128)(2,1)S(1)}, u32[]{:S(2)}, u32[]{:S(2)}) %collective-permute-start.14) | collective-permute-done | bytes 73760 | tf_op jit(solution)/shard_map/ppermute | solution.py:285
  (53 shorter events, 15.1 us)
Async XLA Ops:
  0.6 44.5 %collective-permute-start = (bf16[1024,2048]{1,0:T(8,128)(2,1)}, bf16[1024,2048]{1,0:T(8,128)(2,1)}, u32[]{:S(2)}, u32[]{:S(2)}) collective-permute-start(bf16[1024,2048]{1,0:T(8,128)(2,1)} %bitcast.11), channel_id=1, source_target_pairs={{0,32},{32,0},{64,96},{96,64},{128,160},{160,128},{192,224},{224,1... | collective-permute-start | bytes 12582920 | tf_op jit(solution)/shard_map/ppermute | solution.py:285
  0.7 44.4 %collective-permute-start.1 = (bf16[2048,1024]{1,0:T(8,128)(2,1)}, bf16[2048,1024]{1,0:T(8,128)(2,1)}, u32[]{:S(2)}, u32[]{:S(2)}) collective-permute-start(bf16[2048,1024]{1,0:T(8,128)(2,1)} %bitcast.20), channel_id=1, source_target_pairs={{0,32},{32,0},{64,96},{96,64},{128,160},{160,128},{192,224},{224,1... | collective-permute-start | bytes 12582920 | tf_op jit(solution)/shard_map/ppermute | solution.py:285
  1.3 43.8 %copy-start = (bf16[1,1024,2048]{2,1,0:T(8,128)(2,1)S(1)}, bf16[1,1024,2048]{2,1,0:T(8,128)(2,1)}, u32[]{:S(2)}) copy-start(bf16[1,1024,2048]{2,1,0:T(8,128)(2,1)} %param.3) | copy-start | bytes 12582916
  1.3 2.3 %copy-start.1 = (bf16[1,2048,1024]{2,1,0:T(8,128)(2,1)S(1)}, bf16[1,2048,1024]{2,1,0:T(8,128)(2,1)}, u32[]{:S(2)}) copy-start(bf16[1,2048,1024]{2,1,0:T(8,128)(2,1)} %param.4) | copy-start | bytes 12582916
  3.7 1.2 copy-start.3
  46.8 1.4 collective-permute-start.5
  46.9 4.5 %collective-permute-start.2 = (bf16[128,512]{1,0:T(8,128)(2,1)S(1)}, bf16[128,512]{1,0:T(8,128)(2,1)S(1)}, u32[]{:S(2)}, u32[]{:S(2)}) collective-permute-start(bf16[128,512]{1,0:T(8,128)(2,1)S(1)} %get-tuple-element.42), channel_id=1, source_target_pairs={{0,32},{32,0},{64,96},{96,64},{128,160},{160,128},{192,224},{224,1... | collective-permute-start | bytes 393224 | tf_op jit(solution)/shard_map/ppermute | solution.py:285
  48.3 6.9 %collective-permute-start.6 = (bf16[128,512]{1,0:T(8,128)(2,1)S(1)}, bf16[128,512]{1,0:T(8,128)(2,1)S(1)}, u32[]{:S(2)}, u32[]{:S(2)}) collective-permute-start(bf16[128,512]{1,0:T(8,128)(2,1)S(1)} %shard_map.56.v), channel_id=1, source_target_pairs={{0,192},{32,224},{64,128},{96,160},{128,64},{160,96},{192,0},{224,... | collective-permute-start | bytes 393224 | tf_op jit(solution)/shard_map/ppermute | solution.py:285
  51.4 5.4 %collective-permute-start.3 = (bf16[128,512]{1,0:T(8,128)(2,1)S(1)}, bf16[128,512]{1,0:T(8,128)(2,1)S(1)}, u32[]{:S(2)}, u32[]{:S(2)}) collective-permute-start(bf16[128,512]{1,0:T(8,128)(2,1)S(1)} %shard_map.52.v), channel_id=1, source_target_pairs={{0,64},{32,96},{64,0},{96,32},{128,192},{160,224},{192,128},{224,1... | collective-permute-start | bytes 393224 | tf_op jit(solution)/shard_map/ppermute | solution.py:285
  55.2 5.4 %collective-permute-start.7 = (bf16[128,512]{1,0:T(8,128)(2,1)S(1)}, bf16[128,512]{1,0:T(8,128)(2,1)S(1)}, u32[]{:S(2)}, u32[]{:S(2)}) collective-permute-start(bf16[128,512]{1,0:T(8,128)(2,1)S(1)} %shard_map.57.v), channel_id=1, source_target_pairs={{0,64},{32,96},{64,0},{96,32},{128,192},{160,224},{192,128},{224,1... | collective-permute-start | bytes 393224 | tf_op jit(solution)/shard_map/ppermute | solution.py:285
  56.8 6.3 %collective-permute-start.4 = (bf16[128,512]{1,0:T(8,128)(2,1)S(1)}, bf16[128,512]{1,0:T(8,128)(2,1)S(1)}, u32[]{:S(2)}, u32[]{:S(2)}) collective-permute-start(bf16[128,512]{1,0:T(8,128)(2,1)S(1)} %shard_map.53.v), channel_id=1, source_target_pairs={{0,192},{32,224},{64,128},{96,160},{128,64},{160,96},{192,0},{224,... | collective-permute-start | bytes 393224 | tf_op jit(solution)/shard_map/ppermute | solution.py:285
  63.1 32.9 %copy-start.2 = (bf16[1,2048,1024]{2,1,0:T(8,128)(2,1)S(1)}, bf16[1,2048,1024]{2,1,0:T(8,128)(2,1)}, u32[]{:S(2)}) copy-start(bf16[1,2048,1024]{2,1,0:T(8,128)(2,1)} %param.4) | copy-start | bytes 12582916
  135.0 5.4 %collective-permute-start.8 = (bf16[128,640]{1,0:T(8,128)(2,1)S(1)}, bf16[128,640]{1,0:T(8,128)(2,1)S(1)}, u32[]{:S(2)}, u32[]{:S(2)}) collective-permute-start(bf16[128,640]{1,0:T(8,128)(2,1)S(1)} %get-tuple-element.56.v), channel_id=1, source_target_pairs={{0,64},{32,96},{64,0},{96,32},{128,192},{160,224},{192,128},{224,1... | collective-permute-start | bytes 491528 | tf_op jit(solution)/shard_map/ppermute | solution.py:285
  136.7 6.5 %collective-permute-start.10 = (bf16[128,512]{1,0:T(8,128)(2,1)S(1)}, bf16[128,512]{1,0:T(8,128)(2,1)S(1)}, u32[]{:S(2)}, u32[]{:S(2)}) collective-permute-start(bf16[128,512]{1,0:T(8,128)(2,1)S(1)} %shard_map.65.v), channel_id=1, source_target_pairs={{0,192},{32,224},{64,128},{96,160},{128,64},{160,96},{192,0},{224,... | collective-permute-start | bytes 393224 | tf_op jit(solution)/shard_map/ppermute | solution.py:285
  140.6 6.6 %collective-permute-start.9 = (bf16[128,640]{1,0:T(8,128)(2,1)S(1)}, bf16[128,640]{1,0:T(8,128)(2,1)S(1)}, u32[]{:S(2)}, u32[]{:S(2)}) collective-permute-start(bf16[128,640]{1,0:T(8,128)(2,1)S(1)} %shard_map.63.v), channel_id=1, source_target_pairs={{0,192},{32,224},{64,128},{96,160},{128,64},{160,96},{192,0},{224,... | collective-permute-start | bytes 491528 | tf_op jit(solution)/shard_map/ppermute | solution.py:285
  143.2 5.1 %collective-permute-start.11 = (bf16[128,512]{1,0:T(8,128)(2,1)S(1)}, bf16[128,512]{1,0:T(8,128)(2,1)S(1)}, u32[]{:S(2)}, u32[]{:S(2)}) collective-permute-start(bf16[128,512]{1,0:T(8,128)(2,1)S(1)} %shard_map.66.v), channel_id=1, source_target_pairs={{0,64},{32,96},{64,0},{96,32},{128,192},{160,224},{192,128},{224,1... | collective-permute-start | bytes 393224 | tf_op jit(solution)/shard_map/ppermute | solution.py:285
  215.7 4.9 %collective-permute-start.12 = (bf16[32,1152]{1,0:T(8,128)(2,1)S(1)}, bf16[32,1152]{1,0:T(8,128)(2,1)S(1)}, u32[]{:S(2)}, u32[]{:S(2)}) collective-permute-start(bf16[32,1152]{1,0:T(8,128)(2,1)S(1)} %get-tuple-element.71), channel_id=1, source_target_pairs={{0,64},{32,96},{64,0},{96,32},{128,192},{160,224},{192,128},{224,1... | collective-permute-start | bytes 221192 | tf_op jit(solution)/shard_map/ppermute | solution.py:285
  215.8 7.4 %collective-permute-start.13 = (bf16[32,1152]{1,0:T(8,128)(2,1)S(1)}, bf16[32,1152]{1,0:T(8,128)(2,1)S(1)}, u32[]{:S(2)}, u32[]{:S(2)}) collective-permute-start(bf16[32,1152]{1,0:T(8,128)(2,1)S(1)} %get-tuple-element.72), channel_id=1, source_target_pairs={{0,128},{32,160},{64,192},{96,224},{128,0},{160,32},{192,64},{224,... | collective-permute-start | bytes 221192 | tf_op jit(solution)/shard_map/ppermute | solution.py:285
  220.1 5.6 %collective-permute-start.14 = (bf16[32,1152]{1,0:T(8,128)(2,1)S(1)}, bf16[32,1152]{1,0:T(8,128)(2,1)S(1)}, u32[]{:S(2)}, u32[]{:S(2)}) collective-permute-start(bf16[32,1152]{1,0:T(8,128)(2,1)S(1)} %get-tuple-element.73), channel_id=1, source_target_pairs={{0,192},{32,224},{64,128},{96,160},{128,64},{160,96},{192,0},{224,... | collective-permute-start | bytes 221192 | tf_op jit(solution)/shard_map/ppermute | solution.py:285

commit v8 on v7

--- a/solution.py
+++ b/solution.py
@@ -284,8 +284,6 @@
     def swap(v, flip):
         return lax.ppermute(v, BAND, [(i, i ^ flip) for i in range(bands)])
 
-    left_other, right_other = swap(left, 1), swap(right, 1)
-
     def adjoint(got):
         own, oth, natural = call(
             functools.partial(adjoint_body, order, rank),
@@ -341,6 +339,8 @@
         [shape((blocks, 2 * rank, half), bf16)], [pltpu.VMEM((m, cells), bf16)], work, (perm, d, right),
         [SMEM, VMEM, VMEM],
     )[0]
+    back, mine = lax.optimization_barrier((back, (left, right)))
+    left_other, right_other = swap(mine[0], 1), swap(mine[1], 1)
     state, sent = shape((half, mid), f32), shape((half, mid), bf16)
     ways = (1, 3)
     r0, p0 = [], []

time: 227 us -> 227 us (level)
  transfers between devices with their start and end apart: 15 -> 15, of which waited for: 10 -> 11; matrix products, arithmetic and copies ran while one was open for 0% -> 0% of each run, Pallas kernels for 3% -> 1%
where the time goes in v8:
time: 227 us
  blocking collectives  163 us (72%)
  waiting for transfers between devices  21 us (9%)
  Pallas kernels  20.2 us (9%)
  starting transfers between devices  16.7 us (7%)
  local copies, waits for them, and re-layouts  3.69 us (2%)
    all_to_all x5, blocking collectives, exchange(): return lax.all_to_all(v, SPACE, 0, 0, tiled=True, axis_index_groups=[order])  163 us
    ppermute x15, waiting for transfers between devices, swap(): return lax.ppermute(v, BAND, [(i, i ^ flip) for i in range(bands)])  21 us
    pallas_call x23, Pallas kernels, call(): pl.pallas_call(body, out_shape=outs, in_specs=specs or [VMEM] * len(args)...  20.2 us
    ppermute x15, starting transfers between devices, swap(): return lax.ppermute(v, BAND, [(i, i ^ flip) for i in range(bands)])  16.7 us
  transfers between devices with their start and end apart: 15, of which 11 were waited for; matrix products, arithmetic and copies ran while one was open for 0% of the time, Pallas kernels for 1%

profile of v8, /device:TPU:32, one launch (start us, length us, event | category | flops | bytes accessed | tf_op | source)
XLA Modules:
  0.0 226.7 jit_solution(18115774459027917501)
XLA Ops:
  0.7 2.3 %copy-done.1 = bf16[1,2048,1024]{2,1,0:T(8,128)(2,1)S(1)} copy-done((bf16[1,2048,1024]{2,1,0:T(8,128)(2,1)S(1)}, bf16[1,2048,1024]{2,1,0:T(8,128)(2,1)}, u32[]{:S(2)}) %copy-start.1) | copy-done | bytes 4194328
  4.3 1.8 shard_map.50
  6.7 38.4 %all_to_all.25.got = bf16[32,128,128]{2,1,0:T(8,128)(2,1)S(1)} all-to-all(bf16[32,128,128]{2,1,0:T(8,128)(2,1)S(1)} %shard_map.50), channel_id=1, replica_groups={{0,9,18,27,1,10,19,28,2,11,20,29,3,12,21,30,4,13,22,31,5,14,23,24,6,15,..., dimensions={0} | all-to-all | bytes 2097152 | tf_op jit(solution)/shard_map/all_to_all | solution.py:282
  48.3 3.1 %collective-permute-start.6 = (bf16[128,512]{1,0:T(8,128)(2,1)S(1)}, bf16[128,512]{1,0:T(8,128)(2,1)S(1)}, u32[]{:S(2)}, u32[]{:S(2)}) collective-permute-start(bf16[128,512]{1,0:T(8,128)(2,1)S(1)} %shard_map.56.v), channel_id=1, source_target_pairs={{0,192},{32,224},{64,128},{96,160},{128,64},{160,96},{192,0},{224,... | collective-permute-start | bytes 393224 | tf_op jit(solution)/shard_map/ppermute | solution.py:285
  51.6 3.6 %collective-permute-done.6.got = bf16[128,512]{1,0:T(8,128)(2,1)S(1)} collective-permute-done((bf16[128,512]{1,0:T(8,128)(2,1)S(1)}, bf16[128,512]{1,0:T(8,128)(2,1)S(1)}, u32[]{:S(2)}, u32[]{:S(2)}) %collective-permute-start.6) | collective-permute-done | bytes 131104 | tf_op jit(solution)/shard_map/ppermute | solution.py:285
  56.8 1.6 collective-permute-start.4
  58.7 1.6 collective-permute-done.7.got
  60.3 2.8 %collective-permute-done.4.got = bf16[128,512]{1,0:T(8,128)(2,1)S(1)} collective-permute-done((bf16[128,512]{1,0:T(8,128)(2,1)S(1)}, bf16[128,512]{1,0:T(8,128)(2,1)S(1)}, u32[]{:S(2)}, u32[]{:S(2)}) %collective-permute-start.4) | collective-permute-done | bytes 131104 | tf_op jit(solution)/shard_map/ppermute | solution.py:285
  63.1 1.3 shard_map.60
  64.5 31.5 %all_to_all.26.got = bf16[32,128,128]{2,1,0:T(8,128)(2,1)S(1)} all-to-all(bf16[32,128,128]{2,1,0:T(8,128)(2,1)S(1)} %get-tuple-element.58), channel_id=1, replica_groups={{0,9,18,27,1,10,19,28,2,11,20,29,3,12,21,30,4,13,22,31,5,14,23,24,6,15,..., dimensions={0} | all-to-all | bytes 2097152 | tf_op jit(solution)/shard_map/all_to_all | solution.py:282
  96.0 4.0 %shard_map.61 = (bf16[32,136,128]{2,1,0:T(8,128)(2,1)S(1)}, bf16[256,1024]{1,0:T(8,128)(2,1)S(1)}, bf16[2048,1024]{1,0:T(8,128)(2,1)S(1)}) custom-call(bf16[32,128,128]{2,1,0:T(8,128)(2,1)S(1)} %all_to_all.26.got, f32[128,128]{1,0:T(8,128)S(1)} %get-tuple-element.59.norms, bf16[2048,1024]{1,0:T(8,128)(2,1)S(1)} %bitcast.22, ...), custom_call_target="tpu_custom_call" | custom-call | flops 2147483648 | bytes 15335424 | tf_op jit(solution)/shard_map/pallas_call | solution.py:34
  100.0 33.6 %all_to_all.27.got = bf16[32,136,128]{2,1,0:T(8,128)(2,1)S(1)} all-to-all(bf16[32,136,128]{2,1,0:T(8,128)(2,1)S(1)} %get-tuple-element.61), channel_id=1, replica_groups={{0,9,18,27,1,10,19,28,2,11,20,29,3,12,21,30,4,13,22,31,5,14,23,24,6,15,..., dimensions={0} | all-to-all | bytes 2228224 | tf_op jit(solution)/shard_map/all_to_all | solution.py:282
  133.6 1.4 shard_map.62
  136.6 2.5 %collective-permute-start.10 = (bf16[128,512]{1,0:T(8,128)(2,1)S(1)}, bf16[128,512]{1,0:T(8,128)(2,1)S(1)}, u32[]{:S(2)}, u32[]{:S(2)}) collective-permute-start(bf16[128,512]{1,0:T(8,128)(2,1)S(1)} %shard_map.65.v), channel_id=1, source_target_pairs={{0,192},{32,224},{64,128},{96,160},{128,64},{160,96},{192,0},{224,... | collective-permute-start | bytes 393224 | tf_op jit(solution)/shard_map/ppermute | solution.py:285
  140.6 2.1 collective-permute-start.9
  143.6 3.6 %collective-permute-done.9.got = bf16[128,640]{1,0:T(8,128)(2,1)S(1)} collective-permute-done((bf16[128,640]{1,0:T(8,128)(2,1)S(1)}, bf16[128,640]{1,0:T(8,128)(2,1)S(1)}, u32[]{:S(2)}, u32[]{:S(2)}) %collective-permute-start.9) | collective-permute-done | bytes 163872 | tf_op jit(solution)/shard_map/ppermute | solution.py:285
  148.3 1.4 shard_map.68
  149.7 27.8 %all_to_all.28.got = bf16[32,128,128]{2,1,0:T(8,128)(2,1)S(1)} all-to-all(bf16[32,128,128]{2,1,0:T(8,128)(2,1)S(1)} %get-tuple-element.69), channel_id=1, replica_groups={{0,9,18,27,1,10,19,28,2,11,20,29,3,12,21,30,4,13,22,31,5,14,23,24,6,15,..., dimensions={0} | all-to-all | bytes 2097152 | tf_op jit(solution)/shard_map/all_to_all | solution.py:282
  177.5 3.5 %shard_map.69 = (bf16[32,136,128]{2,1,0:T(8,128)(2,1)S(1)}, bf16[256,1024]{1,0:T(8,128)(2,1)}) custom-call(bf16[32,128,128]{2,1,0:T(8,128)(2,1)S(1)} %all_to_all.28.got, f32[128,128]{1,0:T(8,128)S(1)} %get-tuple-element.70.norms, bf16[2048,1024]{1,0:T(8,128)(2,1)S(1)} %bitcast.23, bf16[2048,1024]{1,0:T(8,128)(2,1)S(1)} %get-tuple-element.71.other, ...), custom_call_target="tpu_custom_call" | custom-call | flops 2147483648 | bytes 11665408 | tf_op jit(solution)/shard_map/pallas_call | solution.py:34
  181.0 31.8 %all_to_all.29.got = bf16[32,136,128]{2,1,0:T(8,128)(2,1)S(1)} all-to-all(bf16[32,136,128]{2,1,0:T(8,128)(2,1)S(1)} %get-tuple-element.73), channel_id=1, replica_groups={{0,9,18,27,1,10,19,28,2,11,20,29,3,12,21,30,4,13,22,31,5,14,23,24,6,15,..., dimensions={0} | all-to-all | bytes 2228224 | tf_op jit(solution)/shard_map/all_to_all | solution.py:282
  212.9 1.4 shard_map.70
  215.7 4.3 %collective-permute-start.13 = (bf16[32,1152]{1,0:T(8,128)(2,1)S(1)}, bf16[32,1152]{1,0:T(8,128)(2,1)S(1)}, u32[]{:S(2)}, u32[]{:S(2)}) collective-permute-start(bf16[32,1152]{1,0:T(8,128)(2,1)S(1)} %get-tuple-element.78), channel_id=1, source_target_pairs={{0,128},{32,160},{64,192},{96,224},{128,0},{160,32},{192,64},{224,... | collective-permute-start | bytes 221192 | tf_op jit(solution)/shard_map/ppermute | solution.py:285
  220.5 2.7 %collective-permute-done.13 = bf16[32,1152]{1,0:T(8,128)(2,1)S(1)} collective-permute-done((bf16[32,1152]{1,0:T(8,128)(2,1)S(1)}, bf16[32,1152]{1,0:T(8,128)(2,1)S(1)}, u32[]{:S(2)}, u32[]{:S(2)}) %collective-permute-start.13) | collective-permute-done | bytes 73760 | tf_op jit(solution)/shard_map/ppermute | solution.py:285
  223.1 2.4 %collective-permute-done.14 = bf16[32,1152]{1,0:T(8,128)(2,1)S(1)} collective-permute-done((bf16[32,1152]{1,0:T(8,128)(2,1)S(1)}, bf16[32,1152]{1,0:T(8,128)(2,1)S(1)}, u32[]{:S(2)}, u32[]{:S(2)}) %collective-permute-start.14) | collective-permute-done | bytes 73760 | tf_op jit(solution)/shard_map/ppermute | solution.py:285
  (53 shorter events, 15.3 us)
Async XLA Ops:
  0.7 5.4 %copy-start = (bf16[1,1024,2048]{2,1,0:T(8,128)(2,1)S(1)}, bf16[1,1024,2048]{2,1,0:T(8,128)(2,1)}, u32[]{:S(2)}) copy-start(bf16[1,1024,2048]{2,1,0:T(8,128)(2,1)} %param.3) | copy-start | bytes 12582916
  0.7 2.3 %copy-start.1 = (bf16[1,2048,1024]{2,1,0:T(8,128)(2,1)S(1)}, bf16[1,2048,1024]{2,1,0:T(8,128)(2,1)}, u32[]{:S(2)}) copy-start(bf16[1,2048,1024]{2,1,0:T(8,128)(2,1)} %param.4) | copy-start | bytes 12582916
  3.1 1.2 copy-start.3
  6.1 39.0 %collective-permute-start = (bf16[1024,2048]{1,0:T(8,128)(2,1)S(1)}, bf16[1024,2048]{1,0:T(8,128)(2,1)S(1)}, u32[]{:S(2)}, u32[]{:S(2)}) collective-permute-start(bf16[1024,2048]{1,0:T(8,128)(2,1)S(1)} %bitcast.11), channel_id=1, source_target_pairs={{0,32},{32,0},{64,96},{96,64},{128,160},{160,128},{192,224},{224,1... | collective-permute-start | bytes 12582920 | tf_op jit(solution)/shard_map/ppermute | solution.py:285
  6.2 38.9 %collective-permute-start.1 = (bf16[2048,1024]{1,0:T(8,128)(2,1)S(1)}, bf16[2048,1024]{1,0:T(8,128)(2,1)S(1)}, u32[]{:S(2)}, u32[]{:S(2)}) collective-permute-start(bf16[2048,1024]{1,0:T(8,128)(2,1)S(1)} %bitcast.21), channel_id=1, source_target_pairs={{0,32},{32,0},{64,96},{96,64},{128,160},{160,128},{192,224},{224,1... | collective-permute-start | bytes 12582920 | tf_op jit(solution)/shard_map/ppermute | solution.py:285
  46.8 1.4 collective-permute-start.5
  46.9 4.5 %collective-permute-start.2 = (bf16[128,512]{1,0:T(8,128)(2,1)S(1)}, bf16[128,512]{1,0:T(8,128)(2,1)S(1)}, u32[]{:S(2)}, u32[]{:S(2)}) collective-permute-start(bf16[128,512]{1,0:T(8,128)(2,1)S(1)} %get-tuple-element.48), channel_id=1, source_target_pairs={{0,32},{32,0},{64,96},{96,64},{128,160},{160,128},{192,224},{224,1... | collective-permute-start | bytes 393224 | tf_op jit(solution)/shard_map/ppermute | solution.py:285
  48.3 6.9 %collective-permute-start.6 = (bf16[128,512]{1,0:T(8,128)(2,1)S(1)}, bf16[128,512]{1,0:T(8,128)(2,1)S(1)}, u32[]{:S(2)}, u32[]{:S(2)}) collective-permute-start(bf16[128,512]{1,0:T(8,128)(2,1)S(1)} %shard_map.56.v), channel_id=1, source_target_pairs={{0,192},{32,224},{64,128},{96,160},{128,64},{160,96},{192,0},{224,... | collective-permute-start | bytes 393224 | tf_op jit(solution)/shard_map/ppermute | solution.py:285
  51.4 5.4 %collective-permute-start.3 = (bf16[128,512]{1,0:T(8,128)(2,1)S(1)}, bf16[128,512]{1,0:T(8,128)(2,1)S(1)}, u32[]{:S(2)}, u32[]{:S(2)}) collective-permute-start(bf16[128,512]{1,0:T(8,128)(2,1)S(1)} %shard_map.52.v), channel_id=1, source_target_pairs={{0,64},{32,96},{64,0},{96,32},{128,192},{160,224},{192,128},{224,1... | collective-permute-start | bytes 393224 | tf_op jit(solution)/shard_map/ppermute | solution.py:285
  55.2 5.1 %collective-permute-start.7 = (bf16[128,512]{1,0:T(8,128)(2,1)S(1)}, bf16[128,512]{1,0:T(8,128)(2,1)S(1)}, u32[]{:S(2)}, u32[]{:S(2)}) collective-permute-start(bf16[128,512]{1,0:T(8,128)(2,1)S(1)} %shard_map.57.v), channel_id=1, source_target_pairs={{0,64},{32,96},{64,0},{96,32},{128,192},{160,224},{192,128},{224,1... | collective-permute-start | bytes 393224 | tf_op jit(solution)/shard_map/ppermute | solution.py:285
  56.8 6.3 %collective-permute-start.4 = (bf16[128,512]{1,0:T(8,128)(2,1)S(1)}, bf16[128,512]{1,0:T(8,128)(2,1)S(1)}, u32[]{:S(2)}, u32[]{:S(2)}) collective-permute-start(bf16[128,512]{1,0:T(8,128)(2,1)S(1)} %shard_map.53.v), channel_id=1, source_target_pairs={{0,192},{32,224},{64,128},{96,160},{128,64},{160,96},{192,0},{224,... | collective-permute-start | bytes 393224 | tf_op jit(solution)/shard_map/ppermute | solution.py:285
  63.1 32.9 %copy-start.2 = (bf16[1,2048,1024]{2,1,0:T(8,128)(2,1)S(1)}, bf16[1,2048,1024]{2,1,0:T(8,128)(2,1)}, u32[]{:S(2)}) copy-start(bf16[1,2048,1024]{2,1,0:T(8,128)(2,1)} %param.4) | copy-start | bytes 12582916
  135.0 5.4 %collective-permute-start.8 = (bf16[128,640]{1,0:T(8,128)(2,1)S(1)}, bf16[128,640]{1,0:T(8,128)(2,1)S(1)}, u32[]{:S(2)}, u32[]{:S(2)}) collective-permute-start(bf16[128,640]{1,0:T(8,128)(2,1)S(1)} %get-tuple-element.62.v), channel_id=1, source_target_pairs={{0,64},{32,96},{64,0},{96,32},{128,192},{160,224},{192,128},{224,1... | collective-permute-start | bytes 491528 | tf_op jit(solution)/shard_map/ppermute | solution.py:285
  136.6 6.5 %collective-permute-start.10 = (bf16[128,512]{1,0:T(8,128)(2,1)S(1)}, bf16[128,512]{1,0:T(8,128)(2,1)S(1)}, u32[]{:S(2)}, u32[]{:S(2)}) collective-permute-start(bf16[128,512]{1,0:T(8,128)(2,1)S(1)} %shard_map.65.v), channel_id=1, source_target_pairs={{0,192},{32,224},{64,128},{96,160},{128,64},{160,96},{192,0},{224,... | collective-permute-start | bytes 393224 | tf_op jit(solution)/shard_map/ppermute | solution.py:285
  140.6 6.6 %collective-permute-start.9 = (bf16[128,640]{1,0:T(8,128)(2,1)S(1)}, bf16[128,640]{1,0:T(8,128)(2,1)S(1)}, u32[]{:S(2)}, u32[]{:S(2)}) collective-permute-start(bf16[128,640]{1,0:T(8,128)(2,1)S(1)} %shard_map.63.v), channel_id=1, source_target_pairs={{0,192},{32,224},{64,128},{96,160},{128,64},{160,96},{192,0},{224,... | collective-permute-start | bytes 491528 | tf_op jit(solution)/shard_map/ppermute | solution.py:285
  143.1 5.1 %collective-permute-start.11 = (bf16[128,512]{1,0:T(8,128)(2,1)S(1)}, bf16[128,512]{1,0:T(8,128)(2,1)S(1)}, u32[]{:S(2)}, u32[]{:S(2)}) collective-permute-start(bf16[128,512]{1,0:T(8,128)(2,1)S(1)} %shard_map.66.v), channel_id=1, source_target_pairs={{0,64},{32,96},{64,0},{96,32},{128,192},{160,224},{192,128},{224,1... | collective-permute-start | bytes 393224 | tf_op jit(solution)/shard_map/ppermute | solution.py:285
  215.6 4.9 %collective-permute-start.12 = (bf16[32,1152]{1,0:T(8,128)(2,1)S(1)}, bf16[32,1152]{1,0:T(8,128)(2,1)S(1)}, u32[]{:S(2)}, u32[]{:S(2)}) collective-permute-start(bf16[32,1152]{1,0:T(8,128)(2,1)S(1)} %get-tuple-element.77), channel_id=1, source_target_pairs={{0,64},{32,96},{64,0},{96,32},{128,192},{160,224},{192,128},{224,1... | collective-permute-start | bytes 221192 | tf_op jit(solution)/shard_map/ppermute | solution.py:285
  215.7 7.4 %collective-permute-start.13 = (bf16[32,1152]{1,0:T(8,128)(2,1)S(1)}, bf16[32,1152]{1,0:T(8,128)(2,1)S(1)}, u32[]{:S(2)}, u32[]{:S(2)}) collective-permute-start(bf16[32,1152]{1,0:T(8,128)(2,1)S(1)} %get-tuple-element.78), channel_id=1, source_target_pairs={{0,128},{32,160},{64,192},{96,224},{128,0},{160,32},{192,64},{224,... | collective-permute-start | bytes 221192 | tf_op jit(solution)/shard_map/ppermute | solution.py:285
  220.0 5.6 %collective-permute-start.14 = (bf16[32,1152]{1,0:T(8,128)(2,1)S(1)}, bf16[32,1152]{1,0:T(8,128)(2,1)S(1)}, u32[]{:S(2)}, u32[]{:S(2)}) collective-permute-start(bf16[32,1152]{1,0:T(8,128)(2,1)S(1)} %get-tuple-element.79), channel_id=1, source_target_pairs={{0,192},{32,224},{64,128},{96,160},{128,64},{160,96},{192,0},{224,... | collective-permute-start | bytes 221192 | tf_op jit(solution)/shard_map/ppermute | solution.py:285
